TPU v7x, 32 devices: a whole 2x2x4 slice. The times are simulated.
32 devices in a mesh: section: 4 (over z), dp: 8 (over y, x, core).
Axes of the slice: x: 2, y: 2, z: 4, core: 2. Of those that a mesh axis runs over, the one named last changes fastest.
Arguments:
- tokens_in: bfloat16 [8, 2048, 640], P('dp'), may hold values from -6 to 6
- doc_starts: int32 [8, 2048], P('dp'), may hold values from 0 to 1
- cotangent: bfloat16 [8, 2048, 640], P('dp'), may hold values from -6 to 6
- tap_weight: bfloat16 [4, 640, 1920], P('section', 'dp'), may hold values from -0.15625 to 0.15625
- gate_bias: bfloat16 [2, 1920], replicated, may hold values from -8.5 to 8.5
Outputs:
- hidden_out: bfloat16 [8, 2048, 640], P('dp', 'section')
- input_grad: float32 [8, 2048, 640], P('dp', 'section')
- weight_grad: float32 [4, 640, 1920], P('section', 'dp')
- bias_grad: float32 [2, 1920], replicated
- last_states: float32 [2, 8, 640], P(None, 'dp')
All inputs are finite; a program needn't handle non-finite values.
Results may differ from a plain program's by a relative error of at most 0.012.
Values may be sent and summed in bfloat16 or wider, within the bound.
No kernel may reach another device: no remote copies, remote signals or barrier semaphores. Data moves between devices by JAX's collectives and lax.ppermute only.
A program may use at most 256 MiB of HBM per device.

v0:
```python
import functools

import jax
import jax.numpy as jnp
from jax import lax
from jax.experimental import pallas as pl
from jax.experimental.pallas import tpu as pltpu
from jax.sharding import PartitionSpec as P

F32 = jnp.float32
BF16 = jnp.bfloat16
LANES = 128
SUBS = 8
BIAS_ROWS = 16
UNROLL = 16
LIMITS = (30, 22, 28, 18, 28, 16)
ANY = pl.BlockSpec(memory_space=pl.ANY)
HBM = pl.BlockSpec(memory_space=pltpu.HBM)
VMEM = pl.BlockSpec(memory_space=pltpu.VMEM)
SMEM = pl.BlockSpec(memory_space=pltpu.SMEM)


def tiles_of(ref):
    return range(ref.shape[0])


def columns_of(tile):
    return slice(tile * LANES, (tile + 1) * LANES)


def joined(tiles):
    return jnp.concatenate(tiles, axis=1)


def first_row(ref):
    return joined([ref[tile, 0:1, :] for tile in tiles_of(ref)])


def ones_and_zeros(tiles):
    return [jnp.ones((SUBS, LANES), F32)] * tiles, [jnp.zeros((SUBS, LANES), F32)] * tiles


def over_steps(steps, body, state):
    def turn(index, state):
        for part in range(UNROLL):
            state = body(index * UNROLL + part, state)
        return state

    return lax.fori_loop(0, steps // UNROLL, turn, state)


def group(step):
    row = step * SUBS
    return pl.ds(row if isinstance(row, int) else pl.multiple_of(row, SUBS), SUBS)


def forward_steps(candid, forget, keep, first, steps, gains, cells):
    def body(step, state):
        gains, cells = state
        spot = group(first + step)
        kept = keep[spot, :]
        new_gains, new_cells = [], []
        for tile, (gain, cell) in enumerate(zip(gains, cells, strict=True)):
            share = forget[tile, spot, :]
            now = share * kept
            new_cells.append(now * cell + (1.0 - share) * candid[tile, spot, :])
            new_gains.append(gain * now)
        return new_gains, new_cells

    return over_steps(steps, body, (list(gains), list(cells)))


def forward_entries(gains, cells, carry):
    gain, cell = joined(gains), joined(cells)
    entries = []
    for sub in range(SUBS):
        entries.append(carry)
        carry = cell[sub : sub + 1] + gain[sub : sub + 1] * carry
    return jnp.concatenate(entries, axis=0), carry


def forward_fill(candid, forget, keep, steps, entries, out):
    cells = [entries[:, columns_of(tile)] for tile in tiles_of(out)]
    for tile in tiles_of(out):
        out[tile, group(0), :] = cells[tile]

    def body(step, cells):
        spot = group(step)
        kept = keep[spot, :]
        new_cells = []
        for tile, cell in enumerate(cells):
            share = forget[tile, spot, :]
            cell = share * kept * cell + (1.0 - share) * candid[tile, spot, :]
            out[tile, group(step + 1), :] = cell
            new_cells.append(cell)
        return new_cells

    over_steps(steps, body, cells)


def backward_steps(forget, keep, emit, steps):
    tiles = emit.shape[0]

    def body(step, state):
        gains, backs = state
        spot = group(steps - 1 - step)
        kept = keep[spot, :]
        new_gains, new_backs = [], []
        for tile, (gain, back) in enumerate(zip(gains, backs, strict=True)):
            now = forget[tile, spot, :] * kept
            new_backs.append(now * (emit[tile, spot, :] + back))
            new_gains.append(gain * now)
        return new_gains, new_backs

    state = ones_and_zeros(tiles)
    whole = (steps - 1) // UNROLL * UNROLL
    state = over_steps(whole, body, state)
    for step in range(whole, steps - 1):
        state = body(step, state)
    first_gains, backs = state
    firsts = [emit[tile, group(0), :] + backs[tile] for tile in range(tiles)]
    gains, backs = body(steps - 1, state)
    return joined(gains), joined(backs), joined(first_gains), joined(firsts)


def backward_entries(gain, back, carry):
    entries = []
    for sub in reversed(range(SUBS)):
        entries.append(carry)
        carry = back[sub : sub + 1] + gain[sub : sub + 1] * carry
    return jnp.concatenate(entries[::-1], axis=0)


def backward_fill(forget, keep, emit, steps, entries):
    def body(step, backs):
        spot = group(steps - 1 - step)
        kept = keep[spot, :]
        new_backs = []
        for tile, back in enumerate(backs):
            now = emit[tile, spot, :] + back
            emit[tile, spot, :] = now
            new_backs.append(forget[tile, spot, :] * kept * now)
        return new_backs

    over_steps(steps, body, [entries[:, columns_of(tile)] for tile in tiles_of(emit)])


def chunk_backward_summary(forget, keep, emit, steps):
    gain, back, first_gain, first = backward_steps(forget, keep, emit, steps)
    gain_all = jnp.ones_like(gain[0:1])
    back_all = jnp.zeros_like(gain[0:1])
    for sub in reversed(range(SUBS)):
        entry_gain, entry_back = gain_all, back_all
        gain_all = gain[sub : sub + 1] * entry_gain
        back_all = back[sub : sub + 1] + gain[sub : sub + 1] * entry_back
    row_gain = first_gain[0:1] * entry_gain
    row_value = first[0:1] + first_gain[0:1] * entry_back
    return gain_all, back_all, row_gain, row_value


def store_gates(pre, here, candid_out, forget_out, gate_out):
    tiles = candid_out.shape[0]
    for tile in range(tiles):
        candid_out[tile, here, :] = jnp.tanh(pre[:, columns_of(tile)])
        forget_out[tile, here, :] = jax.nn.sigmoid(pre[:, columns_of(tiles + tile)])
        if gate_out is not None:
            gate_out[tile, here, :] = jax.nn.sigmoid(pre[:, columns_of(2 * tiles + tile)])


class Weights:
    def __init__(self, place, layer, near, far, target, sems):
        self.place, self.layer, self.target, self.sems = place, layer, target, sems
        self.near, self.far = near, far

    def each(self, pieces, act):
        section, stream = self.place[0], self.place[1]
        width = self.target.shape[0] // 2
        for tap, masks in enumerate(pieces):
            for mask, piece in enumerate(masks):
                height = piece.shape[0]
                slot = (section % 2) ^ tap
                row = slot * width + (stream ^ mask) * height
                row = pl.multiple_of(row, 16)
                act(
                    pltpu.make_async_copy(
                        piece, self.target.at[pl.ds(row, height), :], self.sems.at[tap * len(masks) + mask]
                    )
                )

    def both(self, act):
        if self.far is None:
            width = self.target.shape[0] // 2
            for tap in range(2):
                act(
                    pltpu.make_async_copy(
                        self.near.at[2 * self.layer + tap],
                        self.target.at[pl.ds(tap * width, width), :],
                        self.sems.at[tap],
                    )
                )
            return
        is_near = self.place[0] // 2 == self.layer

        @pl.when(is_near)
        def _():
            self.each(self.near, act)

        @pl.when(jnp.logical_not(is_near))
        def _():
            self.each(self.far, act)

    def start(self):
        self.both(lambda copy: copy.start())

    def wait(self):
        self.both(lambda copy: copy.wait())


def weight_refs(refs, plan):
    if plan is None:
        return refs[0], None
    near = [refs[tap * plan : (tap + 1) * plan] for tap in range(2)]
    far = [refs[(2 + tap) * plan : (3 + tap) * plan] for tap in range(2)]
    return near, far


def weight_operands(weights):
    if isinstance(weights, jax.Array):
        return [weights], None
    return [piece for tap in weights for piece in tap], len(weights[0])


def first_forward_kernel(plan, rows, block, *refs):
    place, x, prev, keep, bias = refs[:5]
    count = 1 if plan is None else 4 * plan
    near, far = weight_refs(refs[5 : 5 + count], plan)
    (
        candid_out,
        forget_out,
        gate_out,
        cell_out,
        hidden_out,
        delayed_out,
        last_out,
        matrix,
        delayed,
        weight_sems,
    ) = refs[-10:]
    section = place[0]
    width = x.shape[1]
    tiles = delayed.shape[0]
    block_steps = block // SUBS
    steps = rows // SUBS
    weights = Weights(place, 0, near, far, matrix, weight_sems)
    weights.start()
    weights.wait()

    def pre_of(row, height, first, last):
        here = pl.ds(row, height)
        return (
            jnp.dot(x[here, :], matrix[:width, first:last], preferred_element_type=F32)
            + jnp.dot(prev[here, :], matrix[width:, first:last], preferred_element_type=F32)
            + bias[:, first:last]
        )

    def earlier(index, carry):
        chunk = pl.multiple_of(index * rows, rows)
        keep_chunk = keep.at[pl.ds(chunk, rows), :]

        def part(index, state):
            base = pl.multiple_of(index * block, block)
            pre = pre_of(pl.multiple_of(chunk + base, block), block, 0, 2 * width)
            store_gates(pre, pl.ds(base, block), candid_out, forget_out, None)
            return forward_steps(candid_out, forget_out, keep_chunk, index * block_steps, block_steps, *state)

        gains, cells = lax.fori_loop(0, rows // block, part, ones_and_zeros(tiles))
        return forward_entries(gains, cells, carry)[1]

    start = pl.multiple_of(section * rows, rows)
    keep_own = keep.at[pl.ds(start, rows), :]
    carry = lax.fori_loop(0, section, earlier, jnp.zeros((1, width), F32))
    tail = pl.multiple_of(jnp.maximum(start - 16, 0), 16)
    tail_gate = jax.nn.sigmoid(pre_of(tail, 16, 2 * width, 3 * width))
    tail_hidden = jnp.where(section > 0, tail_gate[15:16] * carry, 0.0)

    def part(index, state):
        base = pl.multiple_of(index * block, block)
        pre = pre_of(pl.multiple_of(start + base, block), block, 0, 3 * width)
        store_gates(pre, pl.ds(base, block), candid_out, forget_out, gate_out)
        return forward_steps(candid_out, forget_out, keep_own, index * block_steps, block_steps, *state)

    gains, cells = lax.fori_loop(0, rows // block, part, ones_and_zeros(tiles))
    entries, carry = forward_entries(gains, cells, carry)
    forward_fill(candid_out, forget_out, keep_own, steps, entries, cell_out)
    for tile in range(tiles):
        delayed[tile, pl.ds(SUBS, rows), :] = gate_out[tile, :, :] * cell_out[tile, pl.ds(SUBS, rows), :]
        delayed[tile, group(0), :] = jnp.concatenate(
            [tail_hidden[:, columns_of(tile)], delayed[tile, rows : rows + SUBS - 1, :]], axis=0
        )
        hidden_out[:, columns_of(tile)] = delayed[tile, pl.ds(SUBS, rows), :].astype(BF16)
        delayed_out[:, columns_of(tile)] = (
            delayed[tile, pl.ds(0, rows), :].astype(BF16).astype(F32) * keep_own[...]
        ).astype(BF16)
    last_out[...] = jnp.broadcast_to(carry, last_out.shape)


def second_forward_kernel(plan, rows, block, *refs):
    place, hidden, delayed, keep, cot, bias, last = refs[:7]
    count = 1 if plan is None else 4 * plan
    near, far = weight_refs(refs[7 : 7 + count], plan)
    candid_out, forget_out, gate_out, summary_out, matrix, emit, weight_sems = refs[7 + count :]
    width = hidden.shape[1]
    tiles = emit.shape[0]
    block_steps = block // SUBS
    weights = Weights(place, 1, near, far, matrix, weight_sems)
    weights.start()
    weights.wait()

    def part(index, state):
        here = pl.ds(pl.multiple_of(index * block, block), block)
        pre = (
            jnp.dot(hidden[here, :], matrix[:width, :], preferred_element_type=F32)
            + jnp.dot(delayed[here, :], matrix[width:, :], preferred_element_type=F32)
            + bias[...]
        )
        store_gates(pre, here, candid_out, forget_out, gate_out)
        for tile in range(tiles):
            emit[tile, here, :] = cot[here, columns_of(tile)].astype(F32) * gate_out[tile, here, :]
        return forward_steps(candid_out, forget_out, keep, index * block_steps, block_steps, *state)

    gains, cells = lax.fori_loop(0, rows // block, part, ones_and_zeros(tiles))
    cell_all = forward_entries(gains, cells, jnp.zeros((1, width), F32))[1]
    gain_all, back_all, row_gain, row_value = chunk_backward_summary(forget_out, keep, emit, rows // SUBS)
    parts = [
        gain_all,
        cell_all,
        back_all,
        row_gain,
        row_value,
        first_row(candid_out),
        first_row(forget_out),
        first_row(gate_out),
        last[0:1, :],
    ]
    parts += [jnp.zeros((1, width), F32)] * (16 - len(parts))
    summary_out[...] = jnp.concatenate(parts, axis=0)


def gate_grads(dcell, before, cell, candid, forget, gate, arriving):
    return (
        dcell * (1.0 - forget) * (1.0 - candid * candid),
        dcell * (before - candid) * forget * (1.0 - forget),
        arriving * cell * gate * (1.0 - gate),
    )


def pick(values, section):
    out = values[0]
    for index in range(1, len(values)):
        out = jnp.where(section == index, values[index], out)
    return out


def store_weight_grads(place, lefts, right, kept, sent):
    for tap, left in enumerate(lefts):
        grads = lax.dot_general(left, right, (((0,), (0,)), ((), ())), preferred_element_type=F32).astype(BF16)
        if sent is None:
            kept[tap] = grads
            continue
        chips, height = kept.shape[1], kept.shape[2]
        stream = place[1]
        odd = stream % 2 == 1
        for chip in range(chips):
            even_rows = grads[2 * chip * height : (2 * chip + 1) * height]
            odd_rows = grads[(2 * chip + 1) * height : (2 * chip + 2) * height]
            kept[tap, chip ^ (stream // 2)] = jnp.where(odd, odd_rows, even_rows)
            sent[tap, chip ^ (stream // 2)] = jnp.where(odd, even_rows, odd_rows)


def heads_of(order, summaries, section):
    for index, summary in enumerate(summaries):
        order[section ^ index] = summary[...]
    return [order[index] for index in range(len(summaries))]


def back_entries(heads):
    back = jnp.zeros_like(heads[0][0:1])
    backs = []
    for head in reversed(heads):
        backs.append(back)
        back = head[2:3] + head[0:1] * back
    return backs[::-1]


def following_row(heads, backs, section, keep_firsts, cell, arriving):
    nexts = [min(index + 1, len(heads) - 1) for index in range(len(heads))]
    head = pick([heads[index] for index in nexts], section)
    back = pick([backs[index] for index in nexts], section)
    valid = jnp.where(section < len(heads) - 1, 1.0, 0.0)
    keep = pick([keep_firsts[index : index + 1, :] for index in nexts], section)
    keep = joined([keep] * (cell.shape[1] // LANES))
    candid, forget, gate = head[5:6], head[6:7], head[7:8]
    if arriving is None:
        arriving = head[1:2]
    before = keep * cell
    after = forget * before + (1.0 - forget) * candid
    dcell = (head[4:5] + head[3:4] * back) * valid
    return gate_grads(dcell, before, after, candid, forget, gate, arriving * valid), keep


def store_grads(rows, dcells, cells, candid, forget, gate, arriving, keep, next_first, extra, shifted, outs):
    dpre_out, shifted_out, bias_out, after = outs
    tiles = dcells.shape[0]
    width = tiles * LANES
    part_rows = 64
    for index in range(3):
        rounded = extra[index].astype(BF16).astype(F32) * joined([next_first[:, :LANES]] * tiles)
        after[:, index * width : (index + 1) * width] = jnp.broadcast_to(rounded, (SUBS, width))

    def of_tile(tile, carry):
        def of_rows(part, sums):
            base = pl.multiple_of(part * part_rows, part_rows)
            here = pl.ds(base, part_rows)
            kept = keep[here, :]
            parts = gate_grads(
                dcells[tile, here, :],
                cells[tile, here, :] * kept,
                cells[tile, pl.ds(pl.multiple_of(base + SUBS, SUBS), part_rows), :],
                candid[tile, here, :],
                forget[tile, here, :],
                gate[tile, here, :],
                arriving[here, pl.ds(pl.multiple_of(tile * LANES, LANES), LANES)].astype(F32),
            )
            new_sums = []
            for index, part in enumerate(parts):
                rounded = part.astype(BF16)
                columns = pl.ds(pl.multiple_of((index * tiles + tile) * LANES, LANES), LANES)
                dpre_out[here, columns] = rounded
                rounded = rounded.astype(F32)
                shifted[index, here, :] = rounded * kept
                new_sums.append(
                    sums[index] + jnp.sum(rounded.reshape(part_rows // SUBS, SUBS, LANES), axis=0)
                )
            return new_sums

        sums = lax.fori_loop(0, rows // part_rows, of_rows, [jnp.zeros((SUBS, LANES), F32)] * 3)
        for index in range(3):
            columns = pl.ds(pl.multiple_of((index * tiles + tile) * LANES, LANES), LANES)
            shifted[index, pl.ds(rows, SUBS), :] = jnp.concatenate(
                [shifted[index, 1:SUBS, :], after[0:1, columns]], axis=0
            )
            shifted_out[:, columns] = shifted[index, pl.ds(SUBS, rows), :].astype(BF16)
            bias_out[:, columns] = jnp.broadcast_to(
                jnp.sum(sums[index], axis=0, keepdims=True), (bias_out.shape[0], LANES)
            )
        return carry

    lax.fori_loop(0, tiles, of_tile, 0)


def second_backward_kernel(rows, has_sent, *refs):
    (place, candid, forget, gate, hidden, delayed, keep, cot, cot_next, keep_firsts) = refs[:10]
    summaries = refs[10:14]
    outs = refs[14:]
    hidden_out, dpre_out, shifted_out, bias_out, last_out, kept = outs[:6]
    sent = outs[6] if has_sent else None
    order, cells, dcells, shifted, after = outs[7 if has_sent else 6 :]
    section = place[0]
    width = hidden.shape[1]
    tiles = dcells.shape[0]
    steps = rows // SUBS
    heads = heads_of(order, summaries, section)
    carry = jnp.zeros((1, width), F32)
    carries = []
    for head in heads:
        carries.append(carry)
        carry = head[1:2] + head[0:1] * carry
    last_out[0] = heads[-1][8:9]
    last_out[1] = carry
    backs = back_entries(heads)
    carry = pick(carries, section)
    back = pick(backs, section)
    for tile in range(tiles):
        dcells[tile, :, :] = cot[:, columns_of(tile)].astype(F32) * gate[tile, :, :]
    gains, ends = forward_steps(candid, forget, keep, 0, steps, *ones_and_zeros(tiles))
    entries, carry = forward_entries(gains, ends, carry)
    forward_fill(candid, forget, keep, steps, entries, cells)
    for tile in range(tiles):
        hidden_out[:, columns_of(tile)] = (gate[tile, :, :] * cells[tile, pl.ds(SUBS, rows), :]).astype(BF16)
    gain, leaving, _, _ = backward_steps(forget, keep, dcells, steps)
    backward_fill(forget, keep, dcells, steps, backward_entries(gain, leaving, back))
    extra, next_first = following_row(heads, backs, section, keep_firsts, carry, cot_next[...].astype(F32)[0:1])
    store_grads(
        rows, dcells, cells, candid, forget, gate, cot, keep, next_first, extra, shifted,
        (dpre_out, shifted_out, bias_out, after),
    )
    store_weight_grads(place, (hidden[...], delayed[...]), dpre_out[...], kept, sent)


def input_grad_tile(dpre, shifted, matrix, here):
    width = matrix.shape[0] // 2
    contract = (((1,), (1,)), ((), ()))
    return lax.dot_general(
        dpre[here, :], matrix[:width, :], contract, preferred_element_type=F32
    ) + lax.dot_general(shifted[here, :], matrix[width:, :], contract, preferred_element_type=F32)


def middle_kernel(rows, block, *refs):
    place, dpre, shifted, candid, forget, gate, keep, matrix = refs[:8]
    arriving_out, summary_out, emit = refs[8:]

    def part(index, carry):
        here = pl.ds(pl.multiple_of(index * block, block), block)
        arriving = input_grad_tile(dpre, shifted, matrix, here).astype(BF16)
        arriving_out[here, :] = arriving
        for tile in tiles_of(emit):
            emit[tile, here, :] = arriving[:, columns_of(tile)].astype(F32) * gate[tile, here, :]
        return carry

    lax.fori_loop(0, rows // block, part, 0)
    row_arriving = arriving_out[0:16, :].astype(F32)[0:1]
    gain_all, back_all, row_gain, row_value = chunk_backward_summary(forget, keep, emit, rows // SUBS)
    parts = [
        gain_all,
        row_arriving,
        back_all,
        row_gain,
        row_value,
        first_row(candid),
        first_row(forget),
        first_row(gate),
    ]
    summary_out[...] = jnp.concatenate(parts, axis=0)


def first_backward_kernel(rows, has_sent, *refs):
    (place, candid, forget, gate, cells, last, x, prev, keep, arriving, keep_firsts, other_bias) = refs[:12]
    summaries = refs[12:16]
    order, dcells, shifted, after = refs[-4:]
    outs = refs[-9:-4] if has_sent else refs[-8:-4]
    dpre_out, shifted_out, bias_out, kept = outs[:4]
    sent = outs[4] if has_sent else None
    section = place[0]
    steps = rows // SUBS
    heads = heads_of(order, summaries, section)
    backs = back_entries(heads)
    back = pick(backs, section)
    for tile in tiles_of(dcells):
        dcells[tile, :, :] = arriving[:, columns_of(tile)].astype(F32) * gate[tile, :, :]
    gain, leaving, _, _ = backward_steps(forget, keep, dcells, steps)
    backward_fill(forget, keep, dcells, steps, backward_entries(gain, leaving, back))
    extra, next_first = following_row(heads, backs, section, keep_firsts, last[0:1, :], None)
    store_grads(
        rows, dcells, cells, candid, forget, gate, arriving, keep, next_first, extra, shifted,
        (dpre_out, shifted_out, bias_out.at[pl.ds(0, SUBS), :], after),
    )
    bias_out[SUBS:, :] = other_bias[...]
    store_weight_grads(place, (x[...], prev[...]), dpre_out[...], kept, sent)


def last_kernel(rows, block, *refs):
    dpre, shifted, matrix, out = refs

    def part(index, carry):
        here = pl.ds(pl.multiple_of(index * block, block), block)
        out[here, :] = input_grad_tile(dpre, shifted, matrix, here)
        return carry

    lax.fori_loop(0, rows // block, part, 0)


def added(*parts):
    return functools.reduce(jnp.add, [part.astype(F32) for part in parts])


def bias_rows(bias):
    rows = []
    for row in (bias[0:1], bias[SUBS : SUBS + 1]):
        high = row.astype(BF16).astype(F32)
        rows += [high, row - high]
    rows.append(jnp.zeros((BIAS_ROWS - len(rows), bias.shape[1]), F32))
    return jnp.concatenate(rows, axis=0).astype(BF16)


def bias_of(rows):
    rows = rows.astype(F32)
    return jnp.concatenate([rows[0:1] + rows[1:2], rows[2:3] + rows[3:4]], axis=0)


def sum_in_order(order, values, position):
    for index, value in enumerate(values):
        order[position ^ index] = value
    out = order[0]
    for index in range(1, len(values)):
        out = out + order[index]
    return out


def corner_kernel(has_bias, *refs):
    if has_bias:
        kept, got, bias, got_bias = refs[:4]
        rows = bias_rows(bias[...] + got_bias[...])
    else:
        kept, got = refs[:2]
    by_x, by_y = refs[-2:]
    height = kept.shape[2]
    for tap, out in enumerate((by_x, by_y)):
        out[0:height, :] = added(kept[tap, 3], got[tap, 3]).astype(BF16)
        if has_bias:
            out[height:, :] = rows


def sides_kernel(has_bias, *refs):
    kept, got, from_x, from_y = refs[:4]
    by_x, by_y = refs[-2:]
    height = kept.shape[2]
    for tap in range(2):
        here = pl.ds(tap * height, height)
        parts = [kept[tap, 1], got[tap, 1]] + ([from_y[0:height, :]] if tap == 1 else [])
        by_x[here, :] = added(*parts).astype(BF16)
        parts = [kept[tap, 2], got[tap, 2]] + ([from_x[0:height, :]] if tap == 0 else [])
        by_y[here, :] = added(*parts).astype(BF16)
    if has_bias:
        by_x[2 * height :, :] = from_y[height:, :]


def plane_kernel(has_bias, *refs):
    if has_bias:
        place, kept, got, from_x, from_y, bias, got_bias, corner_x, corner_y = refs[:9]
        out, order = refs[-2:]
    else:
        kept, got, from_x, from_y = refs[:4]
        out = refs[-1]
    height = kept.shape[2]
    for tap in range(2):
        here = pl.ds(tap * height, height)
        out[here, :] = added(kept[tap, 0], got[tap, 0], from_x[here, :], from_y[here, :]).astype(BF16)
    if has_bias:
        parts = [bias_rows(bias[...] + got_bias[...]), corner_x[height:, :], corner_y[height:, :], from_x[2 * height :, :]]
        whole = sum_in_order(order, [bias_of(part) for part in parts], place[1] // 2)
        whole = jnp.concatenate([whole[0:1]] * SUBS + [whole[1:2]] * SUBS, axis=0)
        out[2 * height :, :] = bias_rows(whole)


def messages_kernel(*refs):
    place, first, second = refs[:3]
    outs = refs[-3:]
    height = (first.shape[0] - BIAS_ROWS) // 2
    for index, out in enumerate(outs):
        to = place[0] ^ (index + 1)
        row = pl.ds(pl.multiple_of((to % 2) * height, 16), height)

        @pl.when(to < 2)
        def _(out=out, row=row):
            out[0:height, :] = first[row, :]

        @pl.when(to >= 2)
        def _(out=out, row=row):
            out[0:height, :] = second[row, :]

        out[height:, :] = first[2 * height :, :]


def whole_kernel(*refs):
    place, first, second = refs[:3]
    got = refs[3:6]
    out, bias_out, order = refs[-3:]
    section = place[0]
    height = out.shape[0]
    row = pl.ds(pl.multiple_of((section % 2) * height, 16), height)
    rest = added(*[part[0:height, :] for part in got])

    @pl.when(section < 2)
    def _():
        out[...] = first[row, :].astype(F32) + rest

    @pl.when(section >= 2)
    def _():
        out[...] = second[row, :].astype(F32) + rest

    parts = [first[2 * height :, :]] + [part[height:, :] for part in got]
    bias_out[...] = sum_in_order(order, [bias_of(part) for part in parts], section)


def call(kernel, outs, in_specs, out_specs, scratch, flops, moved, megabytes, name):
    return pl.pallas_call(
        kernel,
        out_shape=outs,
        in_specs=in_specs,
        out_specs=out_specs,
        scratch_shapes=scratch,
        compiler_params=pltpu.CompilerParams(vmem_limit_bytes=megabytes * 2**20),
        cost_estimate=pl.CostEstimate(flops=flops, bytes_accessed=moved, transcendentals=0),
        name=name,
    )


def small_call(kernel, outs, operands, name, ties=(), scratch=()):
    has_place = operands[0].dtype == jnp.int32
    specs = [SMEM if has_place and index == 0 else VMEM for index in range(len(operands))]
    return call(
        kernel,
        outs,
        specs + [ANY] * len(ties),
        [VMEM] * len(outs),
        list(scratch),
        1000000,
        1000000,
        12,
        name,
    )(*operands, *ties)


def swap(value, axis, mask):
    pairs = [(index, index ^ mask) for index in range(lax.axis_size(axis))]
    return lax.ppermute(value, axis, pairs)


def gathered_pieces(shard):
    one = swap(shard, "section", 1)
    two = swap(shard, "section", 2)
    three = swap(two, "section", 1)
    taps = []
    for index, own in enumerate((shard, one, two, three)):
        by_x = swap(own, "dp", 2)
        by_y = swap(own, "dp", 4)
        across_chip = swap(by_y, "dp", 2) if index % 2 == 0 else swap(by_x, "dp", 4)
        mine = [own, by_x, by_y, across_chip]
        taps.append([piece for one_piece in mine for piece in (one_piece, swap(one_piece, "dp", 1))])
    return taps


class LayerSum:
    def __init__(self, kept, sent, bias=None, place=None):
        self.kept, self.got = kept, swap(sent, "dp", 1)
        self.bias, self.place = bias, place
        self.got_bias = None if bias is None else swap(bias, "dp", 1)
        self.height, self.gates = kept.shape[2], kept.shape[3]
        self.extra = 0 if bias is None else BIAS_ROWS

    def rows(self, taps, extra):
        return jax.ShapeDtypeStruct((taps * self.height + extra, self.gates), BF16)

    def has_bias(self):
        return self.bias is not None

    def corners(self, ties=()):
        operands = [self.kept, self.got] + ([self.bias, self.got_bias] if self.has_bias() else [])
        by_x, by_y = small_call(
            functools.partial(corner_kernel, self.has_bias()), [self.rows(1, self.extra)] * 2, operands, "corners", ties
        )
        self.corner_x, self.corner_y = swap(by_x, "dp", 2), swap(by_y, "dp", 4)

    def sides(self, ties=()):
        by_x, by_y = small_call(
            functools.partial(sides_kernel, self.has_bias()),
            [self.rows(2, self.extra), self.rows(2, 0)],
            [self.kept, self.got, self.corner_x, self.corner_y],
            "sides",
            ties,
        )
        self.by = (by_x, by_y)
        self.side_x, self.side_y = swap(by_x, "dp", 2), swap(by_y, "dp", 4)

    def plane(self, ties=()):
        operands = [self.kept, self.got, self.side_x, self.side_y]
        scratch = []
        if self.has_bias():
            operands = [self.place, *operands, self.bias, self.got_bias, self.corner_x, self.corner_y]
            scratch = [pltpu.VMEM((4, 2, self.gates), F32)]
        (out,) = small_call(
            functools.partial(plane_kernel, self.has_bias()), [self.rows(2, self.extra)], operands, "plane", ties, scratch
        )
        return out


def whole_sums(place, first, second, ties=()):
    height = (first.shape[0] - BIAS_ROWS) // 2
    gates = first.shape[1]
    message = jax.ShapeDtypeStruct((height + BIAS_ROWS, gates), BF16)
    sent = small_call(messages_kernel, [message] * 3, [place, first, second], "messages", ties)
    got = [swap(part, "section", index + 1) for index, part in enumerate(sent)]
    return small_call(
        whole_kernel,
        [jax.ShapeDtypeStruct((height, gates), F32), jax.ShapeDtypeStruct((2, gates), F32)],
        [place, first, second, *got],
        "whole",
        scratch=[pltpu.VMEM((4, 2, gates), F32)],
    )


def all_sums(value):
    for axis in ("dp", "section"):
        mask = 1
        while mask < lax.axis_size(axis):
            value = value + swap(value, axis, mask)
            mask *= 2
    return value


def grouped(value, rows):
    length, width = value.shape
    return value.reshape(length // rows, SUBS, rows // SUBS, width).swapaxes(1, 2).reshape(length, width)


def ungrouped(value):
    rows, width = value.shape
    return value.reshape(rows // SUBS, SUBS, width).swapaxes(0, 1).reshape(rows, width)


def per_device(tokens_in, doc_starts, cotangent, tap_weight, gate_bias):
    sections = lax.axis_size("section")
    streams = lax.axis_size("dp")
    section = lax.axis_index("section")
    stream = lax.axis_index("dp")
    _, length, width = tokens_in.shape
    gates = 3 * width
    tiles = width // LANES
    rows = length // sections
    block = 256
    start = section * rows
    height = tap_weight.shape[1]
    quick = sections == 4 and streams == 8 and height % 16 == 0

    if quick:
        near_far = gathered_pieces(tap_weight[0])
    else:
        near_far = lax.all_gather(
            lax.all_gather(tap_weight, "dp", axis=1, tiled=True), "section", axis=0, tiled=True
        )
    weights, plan = weight_operands(near_far)
    weight_count = 1 if plan is None else 2 * plan

    def own(value):
        return lax.dynamic_slice_in_dim(value, start, rows, 0)

    keep = (1 - doc_starts[0]).astype(F32)[:, None]
    x_before = jnp.concatenate([jnp.zeros_like(tokens_in[0, :1]), tokens_in[0, :-1]], axis=0)
    x = grouped(tokens_in[0], rows)
    prev = grouped(x_before * keep.astype(BF16), rows)
    keep_all = grouped(jnp.broadcast_to(keep, (length, LANES)), rows)
    keep_firsts = jnp.concatenate([keep_all[::rows], jnp.zeros((8 - sections, LANES), F32)], axis=0)
    keep_own, x_own, prev_own = own(keep_all), own(x), own(prev)
    place = jnp.stack([section, stream]).astype(jnp.int32)
    bias = gate_bias.astype(F32)
    cot = grouped(own(cotangent[0]), rows)
    cot_next = lax.dynamic_slice_in_dim(cotangent[0], jnp.minimum(start + rows, length - 16), 16, 0)

    def shape(*dims, dtype=F32):
        return jax.ShapeDtypeStruct(dims, dtype)

    def buffer(*dims, dtype=F32):
        return pltpu.VMEM(dims, dtype)

    dma = pltpu.SemaphoreType.DMA
    layer_flops = 2 * rows * width * gates * 2
    weight_bytes = 4 * width * gates
    half = shape(rows, width, dtype=BF16)
    full = shape(tiles, rows, LANES)
    scan = buffer(tiles, rows, LANES)
    matrix = shape(2 * width, gates, dtype=BF16)

    early = [keep_firsts, keep_own, x_own, prev_own, cot, cot_next]
    candid0, forget0, gate0, cells0, hidden0, delayed0, last0, matrix0 = call(
        functools.partial(first_forward_kernel, plan, rows, block),
        [full] * 3 + [shape(tiles, rows + SUBS, LANES)] + [half] * 2 + [shape(8, width), matrix],
        [SMEM] + [VMEM] * 4 + [HBM] * len(weights) + [ANY] * len(early),
        [VMEM] * 8,
        [buffer(tiles, rows + SUBS, LANES), dma((weight_count + 1,))],
        2 * layer_flops,
        weight_bytes + 30 * rows * width,
        LIMITS[0],
        "first_forward",
    )(place, x, prev, keep_all, bias[0:1], *weights, *early)

    candid1, forget1, gate1, summary1, matrix1 = call(
        functools.partial(second_forward_kernel, plan, rows, block),
        [full] * 3 + [shape(16, width), matrix],
        [SMEM] + [VMEM] * 6 + [HBM] * len(weights),
        [VMEM] * 5,
        [scan, dma((weight_count + 1,))],
        layer_flops,
        weight_bytes + 20 * rows * width,
        LIMITS[1],
        "second_forward",
    )(place, hidden0, delayed0, keep_own, cot, bias[1:2], last0, *weights)

    def exchanged(summary):
        return [summary] + [swap(summary, "section", index) for index in range(1, sections)]

    if quick:
        kept_shape = [shape(2, 4, height, gates, dtype=BF16)] * 2
    else:
        kept_shape = [shape(2, width, gates, dtype=BF16)]
    wide = shape(rows, gates, dtype=BF16)

    hidden1, dpre1, shifted1, bias1, lasts, *kept1 = call(
        functools.partial(second_backward_kernel, rows, quick),
        [half, wide, wide, shape(8, gates), shape(2, 1, width)] + kept_shape,
        [SMEM] + [VMEM] * 13,
        [VMEM] * (5 + len(kept_shape)),
        [buffer(sections, 16, width), buffer(tiles, rows + SUBS, LANES), scan, buffer(3, rows + SUBS, LANES), buffer(SUBS, gates)],
        layer_flops,
        weight_bytes + 30 * rows * width,
        LIMITS[2],
        "second_backward",
    )(
        place, candid1, forget1, gate1, hidden0, delayed0, keep_own, cot, cot_next, keep_firsts,
        *exchanged(summary1),
    )

    if quick:
        second = LayerSum(*kept1)
        second.corners()

    arriving, summary0 = call(
        functools.partial(middle_kernel, rows, block),
        [half, shape(8, width)],
        [SMEM] + [VMEM] * 7,
        [VMEM] * 2,
        [scan],
        layer_flops,
        weight_bytes + 20 * rows * width,
        LIMITS[3],
        "middle",
    )(place, dpre1, shifted1, candid0, forget0, gate0, keep_own, matrix1)

    ties = []
    if quick:
        second.sides()
        ties = second.by
    dpre0, shifted0, bias_both, *kept0 = call(
        functools.partial(first_backward_kernel, rows, quick),
        [wide, wide, shape(2 * SUBS, gates)] + kept_shape,
        [SMEM] + [VMEM] * 15 + [ANY] * len(ties),
        [VMEM] * (3 + len(kept_shape)),
        [buffer(sections, 8, width), scan, buffer(3, rows + SUBS, LANES), buffer(SUBS, gates)],
        layer_flops,
        weight_bytes + 30 * rows * width,
        LIMITS[4],
        "first_backward",
    )(
        place, candid0, forget0, gate0, cells0, last0, x_own, prev_own, keep_own, arriving, keep_firsts, bias1,
        *exchanged(summary0), *ties,
    )
    if quick:
        plane1 = second.plane()

    input_grad = call(
        functools.partial(last_kernel, rows, block),
        shape(rows, width),
        [VMEM] * 3,
        VMEM,
        [],
        layer_flops,
        weight_bytes + 20 * rows * width,
        LIMITS[5],
        "last",
    )(dpre0, shifted0, matrix0)

    if quick:
        first = LayerSum(*kept0, bias_both, place)
        first.corners(ties=[plane1, input_grad])
        first.sides()
        weight_grad, bias_grad = whole_sums(place, first.plane(), plane1)
        weight_grad = weight_grad[None]
    else:
        bias_grad = all_sums(bias_both[::8])
        stacked = jnp.concatenate([kept0[0], kept1[0]], axis=0)
        by_rows = lax.psum_scatter(stacked, "dp", scatter_dimension=1, tiled=True)
        weight_grad = lax.psum_scatter(by_rows, "section", scatter_dimension=0, tiled=True).astype(F32)
    return (ungrouped(hidden1)[None], ungrouped(input_grad)[None], weight_grad, bias_grad, lasts)


def solution(mesh):
    in_specs = (
        P("dp", None, None),
        P("dp", None),
        P("dp", None, None),
        P("section", "dp", None),
        P(),
    )
    out_specs = (
        P("dp", "section", None),
        P("dp", "section", None),
        P("section", "dp", None),
        P(),
        P(None, "dp", None),
    )
    return jax.shard_map(
        per_device, mesh=mesh, in_specs=in_specs, out_specs=out_specs, check_vma=False
    )
```

profile of v0, /device:TPU:0, one launch (start us, length us, event | category | flops | bytes accessed | tf_op | source)
XLA Modules:
  0.0 216.8 jit_solution(5913179606052775921)
XLA Ops:
  0.7 4.1 %collective-permute-start.15 = (bf16[80,1920]{1,0:T(8,128)(2,1)}, bf16[80,1920]{1,0:T(8,128)(2,1)S(1)}, u32[]{:S(2)}, u32[]{:S(2)}) collective-permute-start(bf16[80,1920]{1,0:T(8,128)(2,1)} %bitcast.47), channel_id=1, source_target_pairs={{0,16},{8,24},{16,0},{24,8},{1,17},{9,25},{17,1},{25,9},{2,18},{10... | collective-permute-start | bytes 921608 | tf_op jit(solution)/shard_map/ppermute | solution.py:716
  4.8 1.6 collective-permute-start.7
  6.3 1.5 collective-permute-start.3
  7.9 1.5 collective-permute-start.1
  9.4 9.6 %collective-permute-done.15.refs_21_.refs_23_ = bf16[80,1920]{1,0:T(8,128)(2,1)S(1)} collective-permute-done((bf16[80,1920]{1,0:T(8,128)(2,1)}, bf16[80,1920]{1,0:T(8,128)(2,1)S(1)}, u32[]{:S(2)}, u32[]{:S(2)}) %collective-permute-start.15) | collective-permute-done | bytes 307232 | tf_op jit(solution)/shard_map/ppermute | solution.py:716
  19.7 1.5 collective-permute-start.19
  21.2 1.5 collective-permute-start.17
  23.9 3.5 %collective-permute-done.23.refs_29_.refs_31_ = bf16[80,1920]{1,0:T(8,128)(2,1)} collective-permute-done((bf16[80,1920]{1,0:T(8,128)(2,1)S(1)}, bf16[80,1920]{1,0:T(8,128)(2,1)}, u32[]{:S(2)}, u32[]{:S(2)}) %collective-permute-start.23) | collective-permute-done | bytes 307232 | tf_op jit(solution)/shard_map/ppermute | solution.py:716
  27.4 1.3 collective-permute-start.9
  28.7 3.4 %slice_bitcast_fusion = bf16[2047,640]{1,0:T(8,128)(2,1)} fusion(bf16[1,2048,640]{2,1,0:T(8,128)(2,1)} %param.5), kind=kLoop, calls=%fused_computation.1 | loop fusion | bytes 5240320 | tf_op jit(solution)/shard_map/squeeze | solution.py:838
  33.3 2.0 collective-permute-done.11.refs_17_.refs_19_
  35.3 2.0 collective-permute-done.9.refs_15_.refs_17_
  37.3 4.1 %pad_multiply_fusion = bf16[2048,640]{1,0:T(8,128)(2,1)} fusion(bf16[2047,640]{1,0:T(8,128)(2,1)} %slice_bitcast_fusion, bf16[2048]{0:T(1024)(128)(2,1)S(1)} %convert_reduce_fusion), kind=kLoop, calls=%fused_computation | loop fusion | flops 5242880 | bytes 5245696 | tf_op jit(solution)/shard_map/mul | solution.py:840
  42.1 2.2 %collective-permute-start.25 = (bf16[80,1920]{1,0:T(8,128)(2,1)}, bf16[80,1920]{1,0:T(8,128)(2,1)}, u32[]{:S(2)}, u32[]{:S(2)}) collective-permute-start(bf16[80,1920]{1,0:T(8,128)(2,1)} %collective-permute-done.23.refs_29_.refs_31_), channel_id=1, source_target_pairs={{0,2},{1,3},{2,0},{3,1},{4,6},{5,7},{6,4},{7,5},{8,10},{9,11},{10,... | collective-permute-start | bytes 921608 | tf_op jit(solution)/shard_map/ppermute | solution.py:716
  47.5 5.3 %collective-permute-done.25.refs_31_.refs_33_ = bf16[80,1920]{1,0:T(8,128)(2,1)} collective-permute-done((bf16[80,1920]{1,0:T(8,128)(2,1)}, bf16[80,1920]{1,0:T(8,128)(2,1)}, u32[]{:S(2)}, u32[]{:S(2)}) %collective-permute-start.25) | collective-permute-done | bytes 307232 | tf_op jit(solution)/shard_map/ppermute | solution.py:716
  53.8 4.1 %collective-permute-done.21.refs_27_.refs_29_ = bf16[80,1920]{1,0:T(8,128)(2,1)} collective-permute-done((bf16[80,1920]{1,0:T(8,128)(2,1)}, bf16[80,1920]{1,0:T(8,128)(2,1)}, u32[]{:S(2)}, u32[]{:S(2)}) %collective-permute-start.21) | collective-permute-done | bytes 307232 | tf_op jit(solution)/shard_map/ppermute | solution.py:716
  60.6 1.5 copy.22
  62.5 3.4 %copy.15 = bf16[4,8,64,640]{3,1,2,0:T(8,128)(2,1)S(1)} copy(bf16[4,8,64,640]{3,2,1,0:T(8,128)(2,1)} %bitcast.54) | data formatting | bytes 5242880 | tf_op jit(solution)/shard_map/reshape;squeeze | solution.py:803
  65.9 1.5 copy.16
  71.5 9.5 %first_forward.1 = (f32[5,512,128]{2,1,0:T(8,128)S(1)}, f32[5,512,128]{2,1,0:T(8,128)S(1)}, f32[5,512,128]{2,1,0:T(8,128)S(1)}, f32[5,520,128]{2,1,0:T(8,128)S(1...) custom-call(s32[2]{0:T(128)S(1)} %pad_add_fusion.refs_0_, ...), custom_call_target="tpu_custom_call" | custom-call | flops 5033164800 | bytes 14745600 | tf_op jit(solution)/shard_map/first_forward/pallas_call | solution.py:864
  81.0 6.9 %second_forward.1 = (f32[5,512,128]{2,1,0:T(8,128)S(1)}, f32[5,512,128]{2,1,0:T(8,128)S(1)}, f32[5,512,128]{2,1,0:T(8,128)S(1)}, f32[16,640]{1,0:T(8,128)S(1)}, bf16[1280,1920]{1,0:T(8,128)(2,1)S(1)}) custom-call(s32[2]{0:T(128)S(1)} %pad_add_fusion.refs_0_, bf16[512,640]{1,0:T(8,128)(2,1)S(1)} %get-tuple-element.45.refs_1_.refs_4_, ...), custom_call_target="tpu_custom_call" | custom-call | flops 2516582400 | bytes 11468800 | tf_op jit(solution)/shard_map/second_forward/pallas_call | solution.py:876
  88.0 1.0 copy-done.19
  89.0 11.4 %collective-permute-start.33 = (f32[16,640]{1,0:T(8,128)S(1)}, f32[16,640]{1,0:T(8,128)S(1)}, u32[]{:S(2)}, u32[]{:S(2)}) collective-permute-start(f32[16,640]{1,0:T(8,128)S(1)} %get-tuple-element.51.refs_10_), channel_id=1, source_target_pairs={{0,24},{8,16},{16,8},{24,0},{1,25},{9,17},{17,9},{25,1},{2,26},{10... | collective-permute-start | bytes 122888 | tf_op jit(solution)/shard_map/ppermute | solution.py:716
  101.0 1.7 collective-permute-done.33.refs_13_
  102.7 2.6 %collective-permute-done.32.refs_12_ = f32[16,640]{1,0:T(8,128)S(1)} collective-permute-done((f32[16,640]{1,0:T(8,128)S(1)}, f32[16,640]{1,0:T(8,128)S(1)}, u32[]{:S(2)}, u32[]{:S(2)}) %collective-permute-start.32) | collective-permute-done | bytes 40992 | tf_op jit(solution)/shard_map/ppermute | solution.py:716
  105.4 1.3 copy-done.20
  106.7 7.2 %second_backward.1 = (bf16[512,640]{1,0:T(8,128)(2,1)S(1)}, bf16[512,1920]{1,0:T(8,128)(2,1)S(1)}, bf16[512,1920]{1,0:T(8,128)(2,1)S(1)}, f32[8,1920]{1,0:T(8,12...) custom-call(s32[2]{0:T(128)S(1)} %pad_add_fusion.refs_0_, ...), custom_call_target="tpu_custom_call" | custom-call | flops 2516582400 | bytes 14745600 | tf_op jit(solution)/shard_map/second_backward/pallas_call | solution.py:897
  114.0 4.7 %collective-permute-done.37.refs_1_ = bf16[2,4,80,1920]{3,2,1,0:T(8,128)(2,1)S(1)} collective-permute-done((bf16[2,4,80,1920]{3,2,1,0:T(8,128)(2,1)S(1)}, bf16[2,4,80,1920]{3,2,1,0:T(8,128)(2,1)S(1)}, u32[]{:S(2)}, u32[]{:S(2)}) %collective-permute-start.37) | collective-permute-done | bytes 2457632 | tf_op jit(solution)/shard_map/ppermute | solution.py:716
  118.8 1.7 collective-permute-start.38
  120.5 1.5 collective-permute-start.39
  122.0 4.7 %middle.1 = (bf16[512,640]{1,0:T(8,128)(2,1)S(1)}, f32[8,640]{1,0:T(8,128)S(1)}) custom-call(s32[2]{0:T(128)S(1)} %pad_add_fusion.refs_0_, bf16[512,1920]{1,0:T(8,128)(2,1)S(1)} %get-tuple-element.57.refs_1_, bf16[512,1920]{1,0:T(8,128)(2,1)S(1)} %get-tuple-element.58.refs_2_, f32[5,512,128]{2,1,0:T(8,128)S(1)} %get-tuple-element.53.refs_3_.refs_1_, ...), custom_call_target="tpu_custom_call" | custom-call | flops 2516582400 | bytes 11468800 | tf_op jit(solution)/shard_map/middle/pallas_call | solution.py:916
  126.7 1.8 collective-permute-start.36
  128.8 2.3 %collective-permute-start.34 = (f32[8,640]{1,0:T(8,128)S(1)}, f32[8,640]{1,0:T(8,128)S(1)}, u32[]{:S(2)}, u32[]{:S(2)}) collective-permute-start(f32[8,640]{1,0:T(8,128)S(1)} %get-tuple-element.62.refs_12_), channel_id=1, source_target_pairs={{0,8},{8,0},{16,24},{24,16},{1,9},{9,1},{17,25},{25,17},{2,10},{10... | collective-permute-start | bytes 61448 | tf_op jit(solution)/shard_map/ppermute | solution.py:716
  133.2 6.6 %first_backward.1 = (bf16[512,1920]{1,0:T(8,128)(2,1)S(1)}, bf16[512,1920]{1,0:T(8,128)(2,1)S(1)}, f32[16,1920]{1,0:T(8,128)S(1)}, bf16[2,4,80,1920]{3,2,1,0:T(8,128)(2,1)S(1)}, bf16[2,4,80,1920]{3,2,1,0:T(8,128)(2,1)S(1)}) custom-call(s32[2]{0:T(128)S(1)} %pad_add_fusion.refs_0_, f32[5,512,128]{2,1,0:T(8,128)S(1)} %get-tuple-element.53.refs_3_.refs_1_, ...), custom_call_target="tpu_custom_call" | custom-call | flops 2516582400 | bytes 14745600 | tf_op jit(solution)/shard_map/first_backward/pallas_call | solution.py:932
  140.9 3.9 %last.1.refs_5_ = f32[512,640]{1,0:T(8,128)S(1)} custom-call(bf16[512,1920]{1,0:T(8,128)(2,1)S(1)} %get-tuple-element.69.refs_0_, bf16[512,1920]{1,0:T(8,128)(2,1)S(1)} %get-tuple-element.70.refs_1_, bf16[1280,1920]{1,0:T(8,128)(2,1)S(1)} %bitcast.35), custom_call_target="tpu_custom_call" | custom-call | flops 2516582400 | bytes 11468800 | tf_op jit(solution)/shard_map/last/pallas_call | solution.py:949
  144.8 11.3 %collective-permute-done.42.refs_2_ = bf16[160,1920]{1,0:T(8,128)(2,1)S(1)} collective-permute-done((bf16[160,1920]{1,0:T(8,128)(2,1)S(1)}, bf16[160,1920]{1,0:T(8,128)(2,1)S(1)}, u32[]{:S(2)}, u32[]{:S(2)}) %collective-permute-start.42) | collective-permute-done | bytes 614432 | tf_op jit(solution)/shard_map/ppermute | solution.py:716
  156.8 1.7 collective-permute-start.44
  159.0 7.9 %collective-permute-done.44.refs_2_.refs_7_ = bf16[96,1920]{1,0:T(8,128)(2,1)S(1)} collective-permute-done((bf16[96,1920]{1,0:T(8,128)(2,1)S(1)}, bf16[96,1920]{1,0:T(8,128)(2,1)S(1)}, u32[]{:S(2)}, u32[]{:S(2)}) %collective-permute-start.44) | collective-permute-done | bytes 368672 | tf_op jit(solution)/shard_map/ppermute | solution.py:716
  166.9 1.1 collective-permute-done.45.refs_3_.refs_8_
  169.6 13.3 %collective-permute-done.47.refs_4_ = bf16[160,1920]{1,0:T(8,128)(2,1)S(1)} collective-permute-done((bf16[160,1920]{1,0:T(8,128)(2,1)S(1)}, bf16[160,1920]{1,0:T(8,128)(2,1)S(1)}, u32[]{:S(2)}, u32[]{:S(2)}) %collective-permute-start.47) | collective-permute-done | bytes 614432 | tf_op jit(solution)/shard_map/ppermute | solution.py:716
  183.7 1.2 plane.3.refs_1_
  185.6 1.8 collective-permute-start.48
  187.4 1.1 collective-permute-start.49
  188.5 1.5 collective-permute-start.50
  191.0 1.3 copy.20
  192.3 6.8 %collective-permute-done.48.refs_3_ = bf16[96,1920]{1,0:T(8,128)(2,1)S(1)} collective-permute-done((bf16[96,1920]{1,0:T(8,128)(2,1)S(1)}, bf16[96,1920]{1,0:T(8,128)(2,1)S(1)}, u32[]{:S(2)}, u32[]{:S(2)}) %collective-permute-start.48) | collective-permute-done | bytes 368672 | tf_op jit(solution)/shard_map/ppermute | solution.py:716
  199.1 16.1 %collective-permute-done.49.refs_4_ = bf16[96,1920]{1,0:T(8,128)(2,1)S(1)} collective-permute-done((bf16[96,1920]{1,0:T(8,128)(2,1)S(1)}, bf16[96,1920]{1,0:T(8,128)(2,1)S(1)}, u32[]{:S(2)}, u32[]{:S(2)}) %collective-permute-start.49) | collective-permute-done | bytes 368672 | tf_op jit(solution)/shard_map/ppermute | solution.py:716
  215.2 1.6 whole.1
  (145 shorter events, 24.3 us)
Async XLA Ops:
  0.7 18.3 %collective-permute-start.15 = (bf16[80,1920]{1,0:T(8,128)(2,1)}, bf16[80,1920]{1,0:T(8,128)(2,1)S(1)}, u32[]{:S(2)}, u32[]{:S(2)}) collective-permute-start(bf16[80,1920]{1,0:T(8,128)(2,1)} %bitcast.47), channel_id=1, source_target_pairs={{0,16},{8,24},{16,0},{24,8},{1,17},{9,25},{17,1},{25,9},{2,18},{10... | collective-permute-start | bytes 921608 | tf_op jit(solution)/shard_map/ppermute | solution.py:716
  4.8 14.9 %collective-permute-start.7 = (bf16[80,1920]{1,0:T(8,128)(2,1)}, bf16[80,1920]{1,0:T(8,128)(2,1)S(1)}, u32[]{:S(2)}, u32[]{:S(2)}) collective-permute-start(bf16[80,1920]{1,0:T(8,128)(2,1)} %bitcast.48), channel_id=1, source_target_pairs={{0,8},{8,0},{16,24},{24,16},{1,9},{9,1},{17,25},{25,17},{2,10},{10... | collective-permute-start | bytes 921608 | tf_op jit(solution)/shard_map/ppermute | solution.py:716
  6.3 14.8 %collective-permute-start.3 = (bf16[80,1920]{1,0:T(8,128)(2,1)}, bf16[80,1920]{1,0:T(8,128)(2,1)}, u32[]{:S(2)}, u32[]{:S(2)}) collective-permute-start(bf16[80,1920]{1,0:T(8,128)(2,1)} %bitcast.49), channel_id=1, source_target_pairs={{0,4},{1,5},{2,6},{3,7},{4,0},{5,1},{6,2},{7,3},{8,12},{9,13},{10,... | collective-permute-start | bytes 921608 | tf_op jit(solution)/shard_map/ppermute | solution.py:716
  7.9 14.8 %collective-permute-start.1 = (bf16[80,1920]{1,0:T(8,128)(2,1)}, bf16[80,1920]{1,0:T(8,128)(2,1)}, u32[]{:S(2)}, u32[]{:S(2)}) collective-permute-start(bf16[80,1920]{1,0:T(8,128)(2,1)} %bitcast.50), channel_id=1, source_target_pairs={{0,2},{1,3},{2,0},{3,1},{4,6},{5,7},{6,4},{7,5},{8,10},{9,11},{10,... | collective-permute-start | bytes 921608 | tf_op jit(solution)/shard_map/ppermute | solution.py:716
  9.3 13.3 %collective-permute-start = (bf16[80,1920]{1,0:T(8,128)(2,1)}, bf16[80,1920]{1,0:T(8,128)(2,1)S(1)}, u32[]{:S(2)}, u32[]{:S(2)}) collective-permute-start(bf16[80,1920]{1,0:T(8,128)(2,1)} %bitcast.51), channel_id=1, source_target_pairs={{0,1},{1,0},{2,3},{3,2},{4,5},{5,4},{6,7},{7,6},{8,9},{9,8},{10,11... | collective-permute-start | bytes 921608 | tf_op jit(solution)/shard_map/ppermute | solution.py:716
  18.9 8.5 %collective-permute-start.23 = (bf16[80,1920]{1,0:T(8,128)(2,1)S(1)}, bf16[80,1920]{1,0:T(8,128)(2,1)}, u32[]{:S(2)}, u32[]{:S(2)}) collective-permute-start(bf16[80,1920]{1,0:T(8,128)(2,1)S(1)} %collective-permute-done.15.refs_21_.refs_23_), channel_id=1, source_target_pairs={{0,8},{8,0},{16,24},{24,16},{1,9},{9,1},{17,25},{25,17},{2,10},{10... | collective-permute-start | bytes 921608 | tf_op jit(solution)/shard_map/ppermute | solution.py:716
  19.7 12.5 %collective-permute-start.19 = (bf16[80,1920]{1,0:T(8,128)(2,1)S(1)}, bf16[80,1920]{1,0:T(8,128)(2,1)}, u32[]{:S(2)}, u32[]{:S(2)}) collective-permute-start(bf16[80,1920]{1,0:T(8,128)(2,1)S(1)} %collective-permute-done.15.refs_21_.refs_23_), channel_id=1, source_target_pairs={{0,4},{1,5},{2,6},{3,7},{4,0},{5,1},{6,2},{7,3},{8,12},{9,13},{10,... | collective-permute-start | bytes 921608 | tf_op jit(solution)/shard_map/ppermute | solution.py:716
  21.2 11.1 %collective-permute-start.17 = (bf16[80,1920]{1,0:T(8,128)(2,1)S(1)}, bf16[80,1920]{1,0:T(8,128)(2,1)}, u32[]{:S(2)}, u32[]{:S(2)}) collective-permute-start(bf16[80,1920]{1,0:T(8,128)(2,1)S(1)} %collective-permute-done.15.refs_21_.refs_23_), channel_id=1, source_target_pairs={{0,2},{1,3},{2,0},{3,1},{4,6},{5,7},{6,4},{7,5},{8,10},{9,11},{10,... | collective-permute-start | bytes 921608 | tf_op jit(solution)/shard_map/ppermute | solution.py:716
  22.7 10.4 %collective-permute-start.16 = (bf16[80,1920]{1,0:T(8,128)(2,1)S(1)}, bf16[80,1920]{1,0:T(8,128)(2,1)}, u32[]{:S(2)}, u32[]{:S(2)}) collective-permute-start(bf16[80,1920]{1,0:T(8,128)(2,1)S(1)} %collective-permute-done.15.refs_21_.refs_23_), channel_id=1, source_target_pairs={{0,1},{1,0},{2,3},{3,2},{4,5},{5,4},{6,7},{7,6},{8,9},{9,8},{10,11... | collective-permute-start | bytes 921608 | tf_op jit(solution)/shard_map/ppermute | solution.py:716
  23.4 11.9 %collective-permute-start.11 = (bf16[80,1920]{1,0:T(8,128)(2,1)S(1)}, bf16[80,1920]{1,0:T(8,128)(2,1)}, u32[]{:S(2)}, u32[]{:S(2)}) collective-permute-start(bf16[80,1920]{1,0:T(8,128)(2,1)S(1)} %collective-permute-done.7.refs_13_.refs_15_), channel_id=1, source_target_pairs={{0,4},{1,5},{2,6},{3,7},{4,0},{5,1},{6,2},{7,3},{8,12},{9,13},{10,... | collective-permute-start | bytes 921608 | tf_op jit(solution)/shard_map/ppermute | solution.py:716
  27.4 9.8 %collective-permute-start.9 = (bf16[80,1920]{1,0:T(8,128)(2,1)S(1)}, bf16[80,1920]{1,0:T(8,128)(2,1)}, u32[]{:S(2)}, u32[]{:S(2)}) collective-permute-start(bf16[80,1920]{1,0:T(8,128)(2,1)S(1)} %collective-permute-done.7.refs_13_.refs_15_), channel_id=1, source_target_pairs={{0,2},{1,3},{2,0},{3,1},{4,6},{5,7},{6,4},{7,5},{8,10},{9,11},{10,... | collective-permute-start | bytes 921608 | tf_op jit(solution)/shard_map/ppermute | solution.py:716
  32.2 9.2 %collective-permute-start.8 = (bf16[80,1920]{1,0:T(8,128)(2,1)S(1)}, bf16[80,1920]{1,0:T(8,128)(2,1)S(1)}, u32[]{:S(2)}, u32[]{:S(2)}) collective-permute-start(bf16[80,1920]{1,0:T(8,128)(2,1)S(1)} %collective-permute-done.7.refs_13_.refs_15_), channel_id=1, source_target_pairs={{0,1},{1,0},{2,3},{3,2},{4,5},{5,4},{6,7},{7,6},{8,9},{9,8},{10,11... | collective-permute-start | bytes 921608 | tf_op jit(solution)/shard_map/ppermute | solution.py:716
  32.3 12.0 %collective-permute-start.5 = (bf16[80,1920]{1,0:T(8,128)(2,1)}, bf16[80,1920]{1,0:T(8,128)(2,1)}, u32[]{:S(2)}, u32[]{:S(2)}) collective-permute-start(bf16[80,1920]{1,0:T(8,128)(2,1)} %collective-permute-done.3.refs_9_.refs_11_), channel_id=1, source_target_pairs={{0,2},{1,3},{2,0},{3,1},{4,6},{5,7},{6,4},{7,5},{8,10},{9,11},{10,... | collective-permute-start | bytes 921608 | tf_op jit(solution)/shard_map/ppermute | solution.py:716
  33.1 11.2 %collective-permute-start.4 = (bf16[80,1920]{1,0:T(8,128)(2,1)}, bf16[80,1920]{1,0:T(8,128)(2,1)S(1)}, u32[]{:S(2)}, u32[]{:S(2)}) collective-permute-start(bf16[80,1920]{1,0:T(8,128)(2,1)} %collective-permute-done.3.refs_9_.refs_11_), channel_id=1, source_target_pairs={{0,1},{1,0},{2,3},{3,2},{4,5},{5,4},{6,7},{7,6},{8,9},{9,8},{10,11... | collective-permute-start | bytes 921608 | tf_op jit(solution)/shard_map/ppermute | solution.py:716
  35.3 10.1 %collective-permute-start.2 = (bf16[80,1920]{1,0:T(8,128)(2,1)}, bf16[80,1920]{1,0:T(8,128)(2,1)S(1)}, u32[]{:S(2)}, u32[]{:S(2)}) collective-permute-start(bf16[80,1920]{1,0:T(8,128)(2,1)} %collective-permute-done.1.refs_7_.refs_9_), channel_id=1, source_target_pairs={{0,1},{1,0},{2,3},{3,2},{4,5},{5,4},{6,7},{7,6},{8,9},{9,8},{10,11... | collective-permute-start | bytes 921608 | tf_op jit(solution)/shard_map/ppermute | solution.py:716
  37.3 9.0 %collective-permute-start.27 = (bf16[80,1920]{1,0:T(8,128)(2,1)}, bf16[80,1920]{1,0:T(8,128)(2,1)}, u32[]{:S(2)}, u32[]{:S(2)}) collective-permute-start(bf16[80,1920]{1,0:T(8,128)(2,1)} %collective-permute-done.23.refs_29_.refs_31_), channel_id=1, source_target_pairs={{0,4},{1,5},{2,6},{3,7},{4,0},{5,1},{6,2},{7,3},{8,12},{9,13},{10,... | collective-permute-start | bytes 921608 | tf_op jit(solution)/shard_map/ppermute | solution.py:716
  42.1 10.7 %collective-permute-start.25 = (bf16[80,1920]{1,0:T(8,128)(2,1)}, bf16[80,1920]{1,0:T(8,128)(2,1)}, u32[]{:S(2)}, u32[]{:S(2)}) collective-permute-start(bf16[80,1920]{1,0:T(8,128)(2,1)} %collective-permute-done.23.refs_29_.refs_31_), channel_id=1, source_target_pairs={{0,2},{1,3},{2,0},{3,1},{4,6},{5,7},{6,4},{7,5},{8,10},{9,11},{10,... | collective-permute-start | bytes 921608 | tf_op jit(solution)/shard_map/ppermute | solution.py:716
  44.3 9.5 %collective-permute-start.24 = (bf16[80,1920]{1,0:T(8,128)(2,1)}, bf16[80,1920]{1,0:T(8,128)(2,1)S(1)}, u32[]{:S(2)}, u32[]{:S(2)}) collective-permute-start(bf16[80,1920]{1,0:T(8,128)(2,1)} %collective-permute-done.23.refs_29_.refs_31_), channel_id=1, source_target_pairs={{0,1},{1,0},{2,3},{3,2},{4,5},{5,4},{6,7},{7,6},{8,9},{9,8},{10,11... | collective-permute-start | bytes 921608 | tf_op jit(solution)/shard_map/ppermute | solution.py:716
  45.0 12.9 %collective-permute-start.21 = (bf16[80,1920]{1,0:T(8,128)(2,1)}, bf16[80,1920]{1,0:T(8,128)(2,1)}, u32[]{:S(2)}, u32[]{:S(2)}) collective-permute-start(bf16[80,1920]{1,0:T(8,128)(2,1)} %collective-permute-done.19.refs_25_.refs_27_), channel_id=1, source_target_pairs={{0,2},{1,3},{2,0},{3,1},{4,6},{5,7},{6,4},{7,5},{8,10},{9,11},{10,... | collective-permute-start | bytes 921608 | tf_op jit(solution)/shard_map/ppermute | solution.py:716
  46.0 11.9 %collective-permute-start.20 = (bf16[80,1920]{1,0:T(8,128)(2,1)}, bf16[80,1920]{1,0:T(8,128)(2,1)S(1)}, u32[]{:S(2)}, u32[]{:S(2)}) collective-permute-start(bf16[80,1920]{1,0:T(8,128)(2,1)} %collective-permute-done.19.refs_25_.refs_27_), channel_id=1, source_target_pairs={{0,1},{1,0},{2,3},{3,2},{4,5},{5,4},{6,7},{7,6},{8,9},{9,8},{10,11... | collective-permute-start | bytes 921608 | tf_op jit(solution)/shard_map/ppermute | solution.py:716
  46.3 12.9 %collective-permute-start.18 = (bf16[80,1920]{1,0:T(8,128)(2,1)}, bf16[80,1920]{1,0:T(8,128)(2,1)S(1)}, u32[]{:S(2)}, u32[]{:S(2)}) collective-permute-start(bf16[80,1920]{1,0:T(8,128)(2,1)} %collective-permute-done.17.refs_23_.refs_25_), channel_id=1, source_target_pairs={{0,1},{1,0},{2,3},{3,2},{4,5},{5,4},{6,7},{7,6},{8,9},{9,8},{10,11... | collective-permute-start | bytes 921608 | tf_op jit(solution)/shard_map/ppermute | solution.py:716
  52.8 15.0 %collective-permute-start.13 = (bf16[80,1920]{1,0:T(8,128)(2,1)}, bf16[80,1920]{1,0:T(8,128)(2,1)}, u32[]{:S(2)}, u32[]{:S(2)}) collective-permute-start(bf16[80,1920]{1,0:T(8,128)(2,1)} %collective-permute-done.9.refs_15_.refs_17_), channel_id=1, source_target_pairs={{0,4},{1,5},{2,6},{3,7},{4,0},{5,1},{6,2},{7,3},{8,12},{9,13},{10,... | collective-permute-start | bytes 921608 | tf_op jit(solution)/shard_map/ppermute | solution.py:716
  53.8 14.5 %collective-permute-start.10 = (bf16[80,1920]{1,0:T(8,128)(2,1)}, bf16[80,1920]{1,0:T(8,128)(2,1)}, u32[]{:S(2)}, u32[]{:S(2)}) collective-permute-start(bf16[80,1920]{1,0:T(8,128)(2,1)} %collective-permute-done.9.refs_15_.refs_17_), channel_id=1, source_target_pairs={{0,1},{1,0},{2,3},{3,2},{4,5},{5,4},{6,7},{7,6},{8,9},{9,8},{10,11... | collective-permute-start | bytes 921608 | tf_op jit(solution)/shard_map/ppermute | solution.py:716
  57.9 9.8 %collective-permute-start.12 = (bf16[80,1920]{1,0:T(8,128)(2,1)}, bf16[80,1920]{1,0:T(8,128)(2,1)}, u32[]{:S(2)}, u32[]{:S(2)}) collective-permute-start(bf16[80,1920]{1,0:T(8,128)(2,1)} %collective-permute-done.11.refs_17_.refs_19_), channel_id=1, source_target_pairs={{0,1},{1,0},{2,3},{3,2},{4,5},{5,4},{6,7},{7,6},{8,9},{9,8},{10,11... | collective-permute-start | bytes 921608 | tf_op jit(solution)/shard_map/ppermute | solution.py:716
  58.6 9.8 %collective-permute-start.6 = (bf16[80,1920]{1,0:T(8,128)(2,1)}, bf16[80,1920]{1,0:T(8,128)(2,1)}, u32[]{:S(2)}, u32[]{:S(2)}) collective-permute-start(bf16[80,1920]{1,0:T(8,128)(2,1)} %collective-permute-done.5.refs_11_.refs_13_), channel_id=1, source_target_pairs={{0,1},{1,0},{2,3},{3,2},{4,5},{5,4},{6,7},{7,6},{8,9},{9,8},{10,11... | collective-permute-start | bytes 921608 | tf_op jit(solution)/shard_map/ppermute | solution.py:716
  59.9 9.5 %collective-permute-start.29 = (bf16[80,1920]{1,0:T(8,128)(2,1)}, bf16[80,1920]{1,0:T(8,128)(2,1)}, u32[]{:S(2)}, u32[]{:S(2)}) collective-permute-start(bf16[80,1920]{1,0:T(8,128)(2,1)} %collective-permute-done.25.refs_31_.refs_33_), channel_id=1, source_target_pairs={{0,4},{1,5},{2,6},{3,7},{4,0},{5,1},{6,2},{7,3},{8,12},{9,13},{10,... | collective-permute-start | bytes 921608 | tf_op jit(solution)/shard_map/ppermute | solution.py:716
  67.8 2.3 %collective-permute-start.26 = (bf16[80,1920]{1,0:T(8,128)(2,1)}, bf16[80,1920]{1,0:T(8,128)(2,1)S(1)}, u32[]{:S(2)}, u32[]{:S(2)}) collective-permute-start(bf16[80,1920]{1,0:T(8,128)(2,1)} %collective-permute-done.25.refs_31_.refs_33_), channel_id=1, source_target_pairs={{0,1},{1,0},{2,3},{3,2},{4,5},{5,4},{6,7},{7,6},{8,9},{9,8},{10,11... | collective-permute-start | bytes 921608 | tf_op jit(solution)/shard_map/ppermute | solution.py:716
  68.4 2.5 %collective-permute-start.14 = (bf16[80,1920]{1,0:T(8,128)(2,1)}, bf16[80,1920]{1,0:T(8,128)(2,1)S(1)}, u32[]{:S(2)}, u32[]{:S(2)}) collective-permute-start(bf16[80,1920]{1,0:T(8,128)(2,1)} %collective-permute-done.13.refs_19_.refs_21_), channel_id=1, source_target_pairs={{0,1},{1,0},{2,3},{3,2},{4,5},{5,4},{6,7},{7,6},{8,9},{9,8},{10,11... | collective-permute-start | bytes 921608 | tf_op jit(solution)/shard_map/ppermute | solution.py:716
  89.0 13.7 %collective-permute-start.33 = (f32[16,640]{1,0:T(8,128)S(1)}, f32[16,640]{1,0:T(8,128)S(1)}, u32[]{:S(2)}, u32[]{:S(2)}) collective-permute-start(f32[16,640]{1,0:T(8,128)S(1)} %get-tuple-element.51.refs_10_), channel_id=1, source_target_pairs={{0,24},{8,16},{16,8},{24,0},{1,25},{9,17},{17,9},{25,1},{2,26},{10... | collective-permute-start | bytes 122888 | tf_op jit(solution)/shard_map/ppermute | solution.py:716
  100.5 4.9 %collective-permute-start.32 = (f32[16,640]{1,0:T(8,128)S(1)}, f32[16,640]{1,0:T(8,128)S(1)}, u32[]{:S(2)}, u32[]{:S(2)}) collective-permute-start(f32[16,640]{1,0:T(8,128)S(1)} %get-tuple-element.51.refs_10_), channel_id=1, source_target_pairs={{0,16},{8,24},{16,0},{24,8},{1,17},{9,25},{17,1},{25,9},{2,18},{10... | collective-permute-start | bytes 122888 | tf_op jit(solution)/shard_map/ppermute | solution.py:716
  100.5 4.9 %collective-permute-start.31 = (f32[16,640]{1,0:T(8,128)S(1)}, f32[16,640]{1,0:T(8,128)S(1)}, u32[]{:S(2)}, u32[]{:S(2)}) collective-permute-start(f32[16,640]{1,0:T(8,128)S(1)} %get-tuple-element.51.refs_10_), channel_id=1, source_target_pairs={{0,8},{8,0},{16,24},{24,16},{1,9},{9,1},{17,25},{25,17},{2,10},{10... | collective-permute-start | bytes 122888 | tf_op jit(solution)/shard_map/ppermute | solution.py:716
  113.9 4.7 %collective-permute-start.37 = (bf16[2,4,80,1920]{3,2,1,0:T(8,128)(2,1)S(1)}, bf16[2,4,80,1920]{3,2,1,0:T(8,128)(2,1)S(1)}, u32[]{:S(2)}, u32[]{:S(2)}) collective-permute-start(bf16[2,4,80,1920]{3,2,1,0:T(8,128)(2,1)S(1)} %get-tuple-element.64), channel_id=1, source_target_pairs={{0,1},{1,0},{2,3},{3,2},{4,5},{5,4},{6,7},{7,6},{8,9},{9,8},{10,11... | collective-permute-start | bytes 7372808 | tf_op jit(solution)/shard_map/ppermute | solution.py:716
  118.8 12.3 %collective-permute-start.38 = (bf16[80,1920]{1,0:T(8,128)(2,1)S(1)}, bf16[80,1920]{1,0:T(8,128)(2,1)S(1)}, u32[]{:S(2)}, u32[]{:S(2)}) collective-permute-start(bf16[80,1920]{1,0:T(8,128)(2,1)S(1)} %get-tuple-element.65), channel_id=1, source_target_pairs={{0,2},{1,3},{2,0},{3,1},{4,6},{5,7},{6,4},{7,5},{8,10},{9,11},{10,... | collective-permute-start | bytes 921608 | tf_op jit(solution)/shard_map/ppermute | solution.py:716
  120.5 10.6 %collective-permute-start.39 = (bf16[80,1920]{1,0:T(8,128)(2,1)S(1)}, bf16[80,1920]{1,0:T(8,128)(2,1)S(1)}, u32[]{:S(2)}, u32[]{:S(2)}) collective-permute-start(bf16[80,1920]{1,0:T(8,128)(2,1)S(1)} %get-tuple-element.66), channel_id=1, source_target_pairs={{0,4},{1,5},{2,6},{3,7},{4,0},{5,1},{6,2},{7,3},{8,12},{9,13},{10,... | collective-permute-start | bytes 921608 | tf_op jit(solution)/shard_map/ppermute | solution.py:716
  126.7 5.6 %collective-permute-start.36 = (f32[8,640]{1,0:T(8,128)S(1)}, f32[8,640]{1,0:T(8,128)S(1)}, u32[]{:S(2)}, u32[]{:S(2)}) collective-permute-start(f32[8,640]{1,0:T(8,128)S(1)} %get-tuple-element.62.refs_12_), channel_id=1, source_target_pairs={{0,24},{8,16},{16,8},{24,0},{1,25},{9,17},{17,9},{25,1},{2,26},{10... | collective-permute-start | bytes 61448 | tf_op jit(solution)/shard_map/ppermute | solution.py:716
  128.5 4.7 %collective-permute-start.35 = (f32[8,640]{1,0:T(8,128)S(1)}, f32[8,640]{1,0:T(8,128)S(1)}, u32[]{:S(2)}, u32[]{:S(2)}) collective-permute-start(f32[8,640]{1,0:T(8,128)S(1)} %get-tuple-element.62.refs_12_), channel_id=1, source_target_pairs={{0,16},{8,24},{16,0},{24,8},{1,17},{9,25},{17,1},{25,9},{2,18},{10... | collective-permute-start | bytes 61448 | tf_op jit(solution)/shard_map/ppermute | solution.py:716
  128.8 4.3 %collective-permute-start.34 = (f32[8,640]{1,0:T(8,128)S(1)}, f32[8,640]{1,0:T(8,128)S(1)}, u32[]{:S(2)}, u32[]{:S(2)}) collective-permute-start(f32[8,640]{1,0:T(8,128)S(1)} %get-tuple-element.62.refs_12_), channel_id=1, source_target_pairs={{0,8},{8,0},{16,24},{24,16},{1,9},{9,1},{17,25},{25,17},{2,10},{10... | collective-permute-start | bytes 61448 | tf_op jit(solution)/shard_map/ppermute | solution.py:716
  139.8 16.9 %collective-permute-start.40 = (bf16[2,4,80,1920]{3,2,1,0:T(8,128)(2,1)S(1)}, bf16[2,4,80,1920]{3,2,1,0:T(8,128)(2,1)S(1)}, u32[]{:S(2)}, u32[]{:S(2)}) collective-permute-start(bf16[2,4,80,1920]{3,2,1,0:T(8,128)(2,1)S(1)} %get-tuple-element.73), channel_id=1, source_target_pairs={{0,1},{1,0},{2,3},{3,2},{4,5},{5,4},{6,7},{7,6},{8,9},{9,8},{10,11... | collective-permute-start | bytes 7372808 | tf_op jit(solution)/shard_map/ppermute | solution.py:716
  139.9 16.3 %collective-permute-start.42 = (bf16[160,1920]{1,0:T(8,128)(2,1)S(1)}, bf16[160,1920]{1,0:T(8,128)(2,1)S(1)}, u32[]{:S(2)}, u32[]{:S(2)}) collective-permute-start(bf16[160,1920]{1,0:T(8,128)(2,1)S(1)} %get-tuple-element.67.refs_16_), channel_id=1, source_target_pairs={{0,2},{1,3},{2,0},{3,1},{4,6},{5,7},{6,4},{7,5},{8,10},{9,11},{10,... | collective-permute-start | bytes 1843208 | tf_op jit(solution)/shard_map/ppermute | solution.py:716
  140.4 15.9 %collective-permute-start.43 = (bf16[160,1920]{1,0:T(8,128)(2,1)S(1)}, bf16[160,1920]{1,0:T(8,128)(2,1)S(1)}, u32[]{:S(2)}, u32[]{:S(2)}) collective-permute-start(bf16[160,1920]{1,0:T(8,128)(2,1)S(1)} %get-tuple-element.68.refs_17_), channel_id=1, source_target_pairs={{0,4},{1,5},{2,6},{3,7},{4,0},{5,1},{6,2},{7,3},{8,12},{9,13},{10,... | collective-permute-start | bytes 1843208 | tf_op jit(solution)/shard_map/ppermute | solution.py:716
  140.9 15.8 %collective-permute-start.41 = (f32[16,1920]{1,0:T(8,128)S(1)}, f32[16,1920]{1,0:T(8,128)S(1)}, u32[]{:S(2)}, u32[]{:S(2)}) collective-permute-start(f32[16,1920]{1,0:T(8,128)S(1)} %get-tuple-element.74.refs_2_.refs_5_), channel_id=1, source_target_pairs={{0,1},{1,0},{2,3},{3,2},{4,5},{5,4},{6,7},{7,6},{8,9},{9,8},{10,11... | collective-permute-start | bytes 368648 | tf_op jit(solution)/shard_map/ppermute | solution.py:716
  156.8 10.1 %collective-permute-start.44 = (bf16[96,1920]{1,0:T(8,128)(2,1)S(1)}, bf16[96,1920]{1,0:T(8,128)(2,1)S(1)}, u32[]{:S(2)}, u32[]{:S(2)}) collective-permute-start(bf16[96,1920]{1,0:T(8,128)(2,1)S(1)} %get-tuple-element.75), channel_id=1, source_target_pairs={{0,2},{1,3},{2,0},{3,1},{4,6},{5,7},{6,4},{7,5},{8,10},{9,11},{10,... | collective-permute-start | bytes 1105928 | tf_op jit(solution)/shard_map/ppermute | solution.py:716
  158.5 9.5 %collective-permute-start.45 = (bf16[96,1920]{1,0:T(8,128)(2,1)S(1)}, bf16[96,1920]{1,0:T(8,128)(2,1)S(1)}, u32[]{:S(2)}, u32[]{:S(2)}) collective-permute-start(bf16[96,1920]{1,0:T(8,128)(2,1)S(1)} %get-tuple-element.76), channel_id=1, source_target_pairs={{0,4},{1,5},{2,6},{3,7},{4,0},{5,1},{6,2},{7,3},{8,12},{9,13},{10,... | collective-permute-start | bytes 1105928 | tf_op jit(solution)/shard_map/ppermute | solution.py:716
  168.4 15.3 %collective-permute-start.46 = (bf16[176,1920]{1,0:T(8,128)(2,1)S(1)}, bf16[176,1920]{1,0:T(8,128)(2,1)S(1)}, u32[]{:S(2)}, u32[]{:S(2)}) collective-permute-start(bf16[176,1920]{1,0:T(8,128)(2,1)S(1)} %get-tuple-element.77), channel_id=1, source_target_pairs={{0,2},{1,3},{2,0},{3,1},{4,6},{5,7},{6,4},{7,5},{8,10},{9,11},{10,... | collective-permute-start | bytes 2027528 | tf_op jit(solution)/shard_map/ppermute | solution.py:716
  169.1 13.8 %collective-permute-start.47 = (bf16[160,1920]{1,0:T(8,128)(2,1)S(1)}, bf16[160,1920]{1,0:T(8,128)(2,1)S(1)}, u32[]{:S(2)}, u32[]{:S(2)}) collective-permute-start(bf16[160,1920]{1,0:T(8,128)(2,1)S(1)} %get-tuple-element.78), channel_id=1, source_target_pairs={{0,4},{1,5},{2,6},{3,7},{4,0},{5,1},{6,2},{7,3},{8,12},{9,13},{10,... | collective-permute-start | bytes 1843208 | tf_op jit(solution)/shard_map/ppermute | solution.py:716
  185.6 13.5 %collective-permute-start.48 = (bf16[96,1920]{1,0:T(8,128)(2,1)S(1)}, bf16[96,1920]{1,0:T(8,128)(2,1)S(1)}, u32[]{:S(2)}, u32[]{:S(2)}) collective-permute-start(bf16[96,1920]{1,0:T(8,128)(2,1)S(1)} %get-tuple-element.79), channel_id=1, source_target_pairs={{0,8},{8,0},{16,24},{24,16},{1,9},{9,1},{17,25},{25,17},{2,10},{10... | collective-permute-start | bytes 1105928 | tf_op jit(solution)/shard_map/ppermute | solution.py:716
  187.4 27.8 %collective-permute-start.49 = (bf16[96,1920]{1,0:T(8,128)(2,1)S(1)}, bf16[96,1920]{1,0:T(8,128)(2,1)S(1)}, u32[]{:S(2)}, u32[]{:S(2)}) collective-permute-start(bf16[96,1920]{1,0:T(8,128)(2,1)S(1)} %get-tuple-element.80), channel_id=1, source_target_pairs={{0,16},{8,24},{16,0},{24,8},{1,17},{9,25},{17,1},{25,9},{2,18},{10... | collective-permute-start | bytes 1105928 | tf_op jit(solution)/shard_map/ppermute | solution.py:716
  188.5 26.7 %collective-permute-start.50 = (bf16[96,1920]{1,0:T(8,128)(2,1)S(1)}, bf16[96,1920]{1,0:T(8,128)(2,1)S(1)}, u32[]{:S(2)}, u32[]{:S(2)}) collective-permute-start(bf16[96,1920]{1,0:T(8,128)(2,1)S(1)} %get-tuple-element.81), channel_id=1, source_target_pairs={{0,24},{8,16},{16,8},{24,0},{1,25},{9,17},{17,9},{25,1},{2,26},{10... | collective-permute-start | bytes 1105928 | tf_op jit(solution)/shard_map/ppermute | solution.py:716
  (31 other events, 213.9 us)
where the time goes:
time: 219 us; the launch traced here: 217 us
  waiting for transfers between devices  97.2 us (44%)
  starting transfers between devices  49.9 us (23%)
  Pallas kernels  43.8 us (20%)
  local copies, waits for them, and re-layouts  20.4 us (9%)
  other arithmetic  4.23 us (2%)
    ppermute x51, waiting for transfers between devices, swap(): return lax.ppermute(value, axis, pairs)  97.2 us
    ppermute x51, starting transfers between devices, swap(): return lax.ppermute(value, axis, pairs)  49.9 us
    pallas_call x1, Pallas kernels, per_device(): call(functools.partial(first_forward_kernel, plan, rows, block), [full] *...  9.55 us
    pallas_call x1, Pallas kernels, per_device(): call(functools.partial(second_backward_kernel, rows, quick), [half, wide,...  7.24 us
    pallas_call x1, Pallas kernels, per_device(): call(functools.partial(second_forward_kernel, plan, rows, block), [full]...  6.93 us
    unnamed x56, local copies, waits for them, and re-layouts  6.77 us
    pallas_call x1, Pallas kernels, per_device(): call(functools.partial(first_backward_kernel, rows, quick), [wide, wide,...  6.62 us
    pallas_call x8, Pallas kernels, small_call(): call(kernel, outs, specs + [ANY] * len(ties), [VMEM] * len(outs), list(sc...  4.88 us
  transfers between devices with their start and end apart: 51, of which 24 were waited for; matrix products, arithmetic and copies ran while one was open for 8% of the time, Pallas kernels for 4%

commit v1 on v0

--- a/solution.py
+++ b/solution.py
@@ -12,8 +12,9 @@
 LANES = 128
 SUBS = 8
 BIAS_ROWS = 16
+COST = 100
 UNROLL = 16
-LIMITS = (30, 22, 28, 18, 28, 16)
+LIMITS = (22, 28, 28, 18, 28, 16)
 ANY = pl.BlockSpec(memory_space=pl.ANY)
 HBM = pl.BlockSpec(memory_space=pltpu.HBM)
 VMEM = pl.BlockSpec(memory_space=pltpu.VMEM)
@@ -173,19 +174,17 @@
         self.near, self.far = near, far
 
     def each(self, pieces, act):
-        section, stream = self.place[0], self.place[1]
+        section, core, chip = self.place[0], self.place[1] % 2, self.place[1] // 2
         width = self.target.shape[0] // 2
-        for tap, masks in enumerate(pieces):
-            for mask, piece in enumerate(masks):
-                height = piece.shape[0]
-                slot = (section % 2) ^ tap
-                row = slot * width + (stream ^ mask) * height
-                row = pl.multiple_of(row, 16)
-                act(
-                    pltpu.make_async_copy(
-                        piece, self.target.at[pl.ds(row, height), :], self.sems.at[tap * len(masks) + mask]
-                    )
-                )
+        height = pieces[0].shape[0]
+        places = []
+        for tap in range(2):
+            places += [(tap, chip), (tap, chip ^ (2 - core)), (tap, chip ^ (1 + core))]
+        places += [(core, chip ^ 3), (1 - core, chip ^ 3)]
+        for index, (piece, (tap, rows)) in enumerate(zip(pieces, places, strict=True)):
+            row = ((section % 2) ^ tap) * width + rows * height
+            target = self.target.at[pl.ds(pl.multiple_of(row, 16), height), :]
+            act(pltpu.make_async_copy(piece, target, self.sems.at[index]))
 
     def both(self, act):
         if self.far is None:
@@ -216,121 +215,141 @@
         self.both(lambda copy: copy.wait())
 
 
-def weight_refs(refs, plan):
-    if plan is None:
+def weight_refs(refs, count):
+    if count == 1:
         return refs[0], None
-    near = [refs[tap * plan : (tap + 1) * plan] for tap in range(2)]
-    far = [refs[(2 + tap) * plan : (3 + tap) * plan] for tap in range(2)]
-    return near, far
-
-
-def weight_operands(weights):
-    if isinstance(weights, jax.Array):
-        return [weights], None
-    return [piece for tap in weights for piece in tap], len(weights[0])
-
-
-def first_forward_kernel(plan, rows, block, *refs):
+    return refs[: count // 2], refs[count // 2 : count]
+
+
+def join_kernel(place, own, got, *refs):
+    out = refs[-1]
+    height = own.shape[0]
+    core = place[1] % 2
+    out[pl.ds(pl.multiple_of(core * height, 16), height), :] = own[...]
+    out[pl.ds(pl.multiple_of((1 - core) * height, 16), height), :] = got[...]
+
+
+def pick_kernel(place, first, second, out):
+    @pl.when(place[1] % 2 == 0)
+    def _():
+        out[...] = first[...]
+
+    @pl.when(place[1] % 2 == 1)
+    def _():
+        out[...] = second[...]
+
+
+def before_kernel(*refs):
+    place, x, tail, keep = refs[:4]
+    prev, shifted = refs[-2:]
+    rows, width = x.shape
+    top = jnp.where(place[0] > 0, tail[...].astype(F32)[15:16], 0.0)
+    for tile in range(width // LANES):
+        columns = columns_of(tile)
+        shifted[tile, pl.ds(SUBS, rows), :] = x[:, columns].astype(F32)
+        shifted[tile, group(0), :] = jnp.concatenate(
+            [top[:, columns], shifted[tile, rows : rows + SUBS - 1, :]], axis=0
+        )
+        prev[:, columns] = (shifted[tile, pl.ds(0, rows), :] * keep[...]).astype(BF16)
+
+
+def forward_gates(x, prev, matrix, bias, keep, block, candid_out, forget_out, gate_out, finish=None):
+    rows, width = x.shape
+    tiles = candid_out.shape[0]
+    block_steps = block // SUBS
+
+    def part(index, state):
+        here = pl.ds(pl.multiple_of(index * block, block), block)
+        pre = (
+            jnp.dot(x[here, :], matrix[:width, :], preferred_element_type=F32)
+            + jnp.dot(prev[here, :], matrix[width:, :], preferred_element_type=F32)
+            + bias[...]
+        )
+        store_gates(pre, here, candid_out, forget_out, gate_out)
+        if finish is not None:
+            finish(here)
+        return forward_steps(candid_out, forget_out, keep, index * block_steps, block_steps, *state)
+
+    return lax.fori_loop(0, rows // block, part, ones_and_zeros(tiles))
+
+
+def first_forward_kernel(plan, block, *refs):
     place, x, prev, keep, bias = refs[:5]
-    count = 1 if plan is None else 4 * plan
-    near, far = weight_refs(refs[5 : 5 + count], plan)
+    near, far = weight_refs(refs[5:], plan)
+    candid_out, forget_out, gate_out, summary_out, matrix, weight_sems = refs[5 + plan :]
+    rows, width = x.shape
+    weights = Weights(place, 0, near, far, matrix, weight_sems)
+    weights.start()
+    weights.wait()
+    gains, cells = forward_gates(x, prev, matrix, bias, keep, block, candid_out, forget_out, gate_out)
+    gain_all, cell_all = jnp.ones((1, width), F32), jnp.zeros((1, width), F32)
+    gain, cell = joined(gains), joined(cells)
+    for sub in range(SUBS):
+        cell_all = cell[sub : sub + 1] + gain[sub : sub + 1] * cell_all
+        gain_all = gain[sub : sub + 1] * gain_all
+    last_gate = joined([gate_out[tile, rows - 1 : rows, :] for tile in tiles_of(gate_out)])
+    parts = [gain_all, cell_all, last_gate] + [jnp.zeros((1, width), F32)] * 5
+    summary_out[...] = jnp.concatenate(parts, axis=0)
+
+
+def second_forward_kernel(plan, block, *refs):
+    place, candid, forget, gate, keep, cot, bias = refs[:7]
+    summaries = refs[7:11]
+    near, far = weight_refs(refs[11:], plan)
     (
+        cell_out,
+        hidden,
+        delayed,
+        last,
         candid_out,
         forget_out,
         gate_out,
-        cell_out,
-        hidden_out,
-        delayed_out,
-        last_out,
+        summary_out,
         matrix,
-        delayed,
+        order,
+        emit,
+        shifted,
         weight_sems,
-    ) = refs[-10:]
+    ) = refs[11 + plan :]
     section = place[0]
-    width = x.shape[1]
-    tiles = delayed.shape[0]
-    block_steps = block // SUBS
+    rows, width = hidden.shape
+    tiles = emit.shape[0]
     steps = rows // SUBS
-    weights = Weights(place, 0, near, far, matrix, weight_sems)
-    weights.start()
-    weights.wait()
-
-    def pre_of(row, height, first, last):
-        here = pl.ds(row, height)
-        return (
-            jnp.dot(x[here, :], matrix[:width, first:last], preferred_element_type=F32)
-            + jnp.dot(prev[here, :], matrix[width:, first:last], preferred_element_type=F32)
-            + bias[:, first:last]
-        )
-
-    def earlier(index, carry):
-        chunk = pl.multiple_of(index * rows, rows)
-        keep_chunk = keep.at[pl.ds(chunk, rows), :]
-
-        def part(index, state):
-            base = pl.multiple_of(index * block, block)
-            pre = pre_of(pl.multiple_of(chunk + base, block), block, 0, 2 * width)
-            store_gates(pre, pl.ds(base, block), candid_out, forget_out, None)
-            return forward_steps(candid_out, forget_out, keep_chunk, index * block_steps, block_steps, *state)
-
-        gains, cells = lax.fori_loop(0, rows // block, part, ones_and_zeros(tiles))
-        return forward_entries(gains, cells, carry)[1]
-
-    start = pl.multiple_of(section * rows, rows)
-    keep_own = keep.at[pl.ds(start, rows), :]
-    carry = lax.fori_loop(0, section, earlier, jnp.zeros((1, width), F32))
-    tail = pl.multiple_of(jnp.maximum(start - 16, 0), 16)
-    tail_gate = jax.nn.sigmoid(pre_of(tail, 16, 2 * width, 3 * width))
-    tail_hidden = jnp.where(section > 0, tail_gate[15:16] * carry, 0.0)
-
-    def part(index, state):
-        base = pl.multiple_of(index * block, block)
-        pre = pre_of(pl.multiple_of(start + base, block), block, 0, 3 * width)
-        store_gates(pre, pl.ds(base, block), candid_out, forget_out, gate_out)
-        return forward_steps(candid_out, forget_out, keep_own, index * block_steps, block_steps, *state)
-
-    gains, cells = lax.fori_loop(0, rows // block, part, ones_and_zeros(tiles))
-    entries, carry = forward_entries(gains, cells, carry)
-    forward_fill(candid_out, forget_out, keep_own, steps, entries, cell_out)
-    for tile in range(tiles):
-        delayed[tile, pl.ds(SUBS, rows), :] = gate_out[tile, :, :] * cell_out[tile, pl.ds(SUBS, rows), :]
-        delayed[tile, group(0), :] = jnp.concatenate(
-            [tail_hidden[:, columns_of(tile)], delayed[tile, rows : rows + SUBS - 1, :]], axis=0
-        )
-        hidden_out[:, columns_of(tile)] = delayed[tile, pl.ds(SUBS, rows), :].astype(BF16)
-        delayed_out[:, columns_of(tile)] = (
-            delayed[tile, pl.ds(0, rows), :].astype(BF16).astype(F32) * keep_own[...]
-        ).astype(BF16)
-    last_out[...] = jnp.broadcast_to(carry, last_out.shape)
-
-
-def second_forward_kernel(plan, rows, block, *refs):
-    place, hidden, delayed, keep, cot, bias, last = refs[:7]
-    count = 1 if plan is None else 4 * plan
-    near, far = weight_refs(refs[7 : 7 + count], plan)
-    candid_out, forget_out, gate_out, summary_out, matrix, emit, weight_sems = refs[7 + count :]
-    width = hidden.shape[1]
-    tiles = emit.shape[0]
-    block_steps = block // SUBS
     weights = Weights(place, 1, near, far, matrix, weight_sems)
     weights.start()
+
+    heads = heads_of(order, summaries, section)
+    carry = jnp.zeros((1, width), F32)
+    carries, hiddens = [], [jnp.zeros((1, width), F32)]
+    for head in heads:
+        carries.append(carry)
+        carry = head[1:2] + head[0:1] * carry
+        hiddens.append(head[2:3] * carry)
+    gains, cells = forward_steps(candid, forget, keep, 0, steps, *ones_and_zeros(tiles))
+    entries, carry = forward_entries(gains, cells, pick(carries, section))
+    last[...] = jnp.broadcast_to(carry, last.shape)
+    forward_fill(candid, forget, keep, steps, entries, cell_out)
+    top = pick(hiddens[:-1], section)
+    for tile in range(tiles):
+        columns = columns_of(tile)
+        shifted[tile, pl.ds(SUBS, rows), :] = gate[tile, :, :] * cell_out[tile, pl.ds(SUBS, rows), :]
+        shifted[tile, group(0), :] = jnp.concatenate(
+            [top[:, columns], shifted[tile, rows : rows + SUBS - 1, :]], axis=0
+        )
+        hidden[:, columns] = shifted[tile, pl.ds(SUBS, rows), :].astype(BF16)
+        delayed[:, columns] = (shifted[tile, pl.ds(0, rows), :].astype(BF16).astype(F32) * keep[...]).astype(BF16)
+
     weights.wait()
 
-    def part(index, state):
-        here = pl.ds(pl.multiple_of(index * block, block), block)
-        pre = (
-            jnp.dot(hidden[here, :], matrix[:width, :], preferred_element_type=F32)
-            + jnp.dot(delayed[here, :], matrix[width:, :], preferred_element_type=F32)
-            + bias[...]
-        )
-        store_gates(pre, here, candid_out, forget_out, gate_out)
+    def emitted(here):
         for tile in range(tiles):
             emit[tile, here, :] = cot[here, columns_of(tile)].astype(F32) * gate_out[tile, here, :]
-        return forward_steps(candid_out, forget_out, keep, index * block_steps, block_steps, *state)
-
-    gains, cells = lax.fori_loop(0, rows // block, part, ones_and_zeros(tiles))
+
+    gains, cells = forward_gates(
+        hidden, delayed, matrix, bias, keep, block, candid_out, forget_out, gate_out, emitted
+    )
     cell_all = forward_entries(gains, cells, jnp.zeros((1, width), F32))[1]
-    gain_all, back_all, row_gain, row_value = chunk_backward_summary(forget_out, keep, emit, rows // SUBS)
+    gain_all, back_all, row_gain, row_value = chunk_backward_summary(forget_out, keep, emit, steps)
     parts = [
         gain_all,
         cell_all,
@@ -359,6 +378,12 @@
     for index in range(1, len(values)):
         out = jnp.where(section == index, values[index], out)
     return out
+
+
+def first_weights_kernel(first, *refs):
+    place, x, prev, dpre = refs[:4]
+    kept, sent = refs[-2:]
+    store_weight_grads(place, (x[...], prev[...]), dpre[:, first:], kept, sent)
 
 
 def store_weight_grads(place, lefts, right, kept, sent):
@@ -555,7 +580,7 @@
         (dpre_out, shifted_out, bias_out.at[pl.ds(0, SUBS), :], after),
     )
     bias_out[SUBS:, :] = other_bias[...]
-    store_weight_grads(place, (x[...], prev[...]), dpre_out[...], kept, sent)
+    store_weight_grads(place, (x[...], prev[...]), dpre_out[:, : kept.shape[-1]], kept, sent)
 
 
 def last_kernel(rows, block, *refs):
@@ -596,21 +621,20 @@
     return out
 
 
-def corner_kernel(has_bias, *refs):
-    if has_bias:
-        kept, got, bias, got_bias = refs[:4]
-        rows = bias_rows(bias[...] + got_bias[...])
-    else:
-        kept, got = refs[:2]
+def corner_kernel(columns, *refs):
+    kept, got = refs[:2]
     by_x, by_y = refs[-2:]
     height = kept.shape[2]
     for tap, out in enumerate((by_x, by_y)):
         out[0:height, :] = added(kept[tap, 3], got[tap, 3]).astype(BF16)
-        if has_bias:
+    if columns is not None:
+        bias, got_bias = refs[2:4]
+        rows = bias_rows(bias[:, columns] + got_bias[:, columns])
+        for out in (by_x, by_y):
             out[height:, :] = rows
 
 
-def sides_kernel(has_bias, *refs):
+def sides_kernel(columns, *refs):
     kept, got, from_x, from_y = refs[:4]
     by_x, by_y = refs[-2:]
     height = kept.shape[2]
@@ -620,32 +644,39 @@
         by_x[here, :] = added(*parts).astype(BF16)
         parts = [kept[tap, 2], got[tap, 2]] + ([from_x[0:height, :]] if tap == 0 else [])
         by_y[here, :] = added(*parts).astype(BF16)
-    if has_bias:
+    if columns is not None:
         by_x[2 * height :, :] = from_y[height:, :]
 
 
-def plane_kernel(has_bias, *refs):
-    if has_bias:
-        place, kept, got, from_x, from_y, bias, got_bias, corner_x, corner_y = refs[:9]
-        out, order = refs[-2:]
-    else:
-        kept, got, from_x, from_y = refs[:4]
-        out = refs[-1]
+def plane_sum(place, kept, got, from_x, from_y, tap):
+    here = pl.ds(tap * kept.shape[2], kept.shape[2])
+    return added(kept[tap, 0], got[tap, 0], from_x[here, :], from_y[here, :])
+
+
+def plane_kernel(*refs):
+    kept, got, from_x, from_y = refs[:4]
+    out = refs[-1]
     height = kept.shape[2]
     for tap in range(2):
-        here = pl.ds(tap * height, height)
-        out[here, :] = added(kept[tap, 0], got[tap, 0], from_x[here, :], from_y[here, :]).astype(BF16)
-    if has_bias:
-        parts = [bias_rows(bias[...] + got_bias[...]), corner_x[height:, :], corner_y[height:, :], from_x[2 * height :, :]]
-        whole = sum_in_order(order, [bias_of(part) for part in parts], place[1] // 2)
-        whole = jnp.concatenate([whole[0:1]] * SUBS + [whole[1:2]] * SUBS, axis=0)
-        out[2 * height :, :] = bias_rows(whole)
-
-
-def messages_kernel(*refs):
-    place, first, second = refs[:3]
-    outs = refs[-3:]
-    height = (first.shape[0] - BIAS_ROWS) // 2
+        out[pl.ds(tap * height, height), :] = plane_sum(None, kept, got, from_x, from_y, tap).astype(BF16)
+
+
+def messages_kernel(columns, *refs):
+    place, kept, got, from_x, from_y, bias, got_bias, corner_x, corner_y, second = refs[:10]
+    outs = refs[-5:-2]
+    first, order = refs[-2:]
+    height = kept.shape[2]
+    for tap in range(2):
+        first[pl.ds(tap * height, height), :] = plane_sum(None, kept, got, from_x, from_y, tap).astype(BF16)
+    parts = [
+        bias_rows(bias[:, columns] + got_bias[:, columns]),
+        corner_x[height:, :],
+        corner_y[height:, :],
+        from_x[2 * height :, :],
+    ]
+    whole = sum_in_order(order, [bias_of(part) for part in parts], place[1] // 2)
+    whole = bias_rows(jnp.concatenate([whole[0:1]] * SUBS + [whole[1:2]] * SUBS, axis=0))
+    first[2 * height :, :] = whole
     for index, out in enumerate(outs):
         to = place[0] ^ (index + 1)
         row = pl.ds(pl.multiple_of((to % 2) * height, 16), height)
@@ -656,30 +687,31 @@
 
         @pl.when(to >= 2)
         def _(out=out, row=row):
-            out[0:height, :] = second[row, :]
-
-        out[height:, :] = first[2 * height :, :]
-
-
-def whole_kernel(*refs):
-    place, first, second = refs[:3]
-    got = refs[3:6]
-    out, bias_out, order = refs[-3:]
+            out[0:height, :] = second[row, columns]
+
+        out[height:, :] = whole
+
+
+def whole_kernel(parts, *refs):
+    place, second = refs[:2]
+    out, bias_out, *orders = refs[-2 - len(parts) :]
     section = place[0]
     height = out.shape[0]
     row = pl.ds(pl.multiple_of((section % 2) * height, 16), height)
-    rest = added(*[part[0:height, :] for part in got])
-
-    @pl.when(section < 2)
-    def _():
-        out[...] = first[row, :].astype(F32) + rest
-
-    @pl.when(section >= 2)
-    def _():
-        out[...] = second[row, :].astype(F32) + rest
-
-    parts = [first[2 * height :, :]] + [part[height:, :] for part in got]
-    bias_out[...] = sum_in_order(order, [bias_of(part) for part in parts], section)
+    for index, columns in enumerate(parts):
+        first, *got = refs[2 + 4 * index : 6 + 4 * index]
+        rest = added(*[part[0:height, :] for part in got])
+
+        @pl.when(section < 2)
+        def _(first=first, rest=rest, columns=columns):
+            out[:, columns] = first[row, :].astype(F32) + rest
+
+        @pl.when(section >= 2)
+        def _(rest=rest, columns=columns):
+            out[:, columns] = second[row, columns].astype(F32) + rest
+
+        biases = [first[2 * height :, :]] + [part[height:, :] for part in got]
+        bias_out[:, columns] = sum_in_order(orders[index], [bias_of(part) for part in biases], section)
 
 
 def call(kernel, outs, in_specs, out_specs, scratch, flops, moved, megabytes, name):
@@ -690,7 +722,7 @@
         out_specs=out_specs,
         scratch_shapes=scratch,
         compiler_params=pltpu.CompilerParams(vmem_limit_bytes=megabytes * 2**20),
-        cost_estimate=pl.CostEstimate(flops=flops, bytes_accessed=moved, transcendentals=0),
+        cost_estimate=pl.CostEstimate(flops=flops // COST, bytes_accessed=moved // COST, transcendentals=0),
         name=name,
     )
 
@@ -716,77 +748,86 @@
     return lax.ppermute(value, axis, pairs)
 
 
-def gathered_pieces(shard):
+def moved(value, axis, target):
+    return lax.ppermute(value, axis, [(index, target(index)) for index in range(lax.axis_size(axis))])
+
+
+def gathered_pieces(place, shard, early):
+    height, gates = shard.shape
+    chip = jax.ShapeDtypeStruct((2 * height, gates), shard.dtype)
+
+    def joined_cores(own, ties=()):
+        return small_call(join_kernel, [chip], [place, own, swap(own, "dp", 1)], "join", ties)[0]
+
+    def beside(unit):
+        return moved(unit, "dp", lambda index: index ^ (3 if index % 2 == 0 else 5))
+
+    def opposite(first, second):
+        unit = small_call(pick_kernel, [chip], [place, first, second], "pick")[0]
+        return moved(unit, "dp", lambda index: index ^ (2 if index % 2 == 0 else 4))
+
+    two = swap(shard, "section", 2)
     one = swap(shard, "section", 1)
-    two = swap(shard, "section", 2)
     three = swap(two, "section", 1)
-    taps = []
-    for index, own in enumerate((shard, one, two, three)):
-        by_x = swap(own, "dp", 2)
-        by_y = swap(own, "dp", 4)
-        across_chip = swap(by_y, "dp", 2) if index % 2 == 0 else swap(by_x, "dp", 4)
-        mine = [own, by_x, by_y, across_chip]
-        taps.append([piece for one_piece in mine for piece in (one_piece, swap(one_piece, "dp", 1))])
-    return taps
+    units, got, across = [], [], []
+    for own, ties in ((shard, []), (one, [0]), (two, []), (three, [1])):
+        ties = [got[index] for index in ties] + (early if len(got) == 1 else [])
+        units.append(joined_cores(own, ties))
+        got.append(beside(units[-1]))
+        if len(got) % 2 == 0:
+            across.append(opposite(*got[-2:]))
+    out = []
+    for pair in range(2):
+        for tap in range(2 * pair, 2 * pair + 2):
+            out += [units[tap], got[tap], swap(got[tap], "dp", 1)]
+        out += [across[pair], swap(across[pair], "dp", 1)]
+    return out
 
 
 class LayerSum:
-    def __init__(self, kept, sent, bias=None, place=None):
+    def __init__(self, kept, sent, columns=None, bias=None, got_bias=None, place=None):
         self.kept, self.got = kept, swap(sent, "dp", 1)
-        self.bias, self.place = bias, place
-        self.got_bias = None if bias is None else swap(bias, "dp", 1)
+        self.columns, self.bias, self.got_bias, self.place = columns, bias, got_bias, place
         self.height, self.gates = kept.shape[2], kept.shape[3]
         self.extra = 0 if bias is None else BIAS_ROWS
 
     def rows(self, taps, extra):
         return jax.ShapeDtypeStruct((taps * self.height + extra, self.gates), BF16)
 
-    def has_bias(self):
-        return self.bias is not None
-
     def corners(self, ties=()):
-        operands = [self.kept, self.got] + ([self.bias, self.got_bias] if self.has_bias() else [])
+        operands = [self.kept, self.got] + ([] if self.bias is None else [self.bias, self.got_bias])
         by_x, by_y = small_call(
-            functools.partial(corner_kernel, self.has_bias()), [self.rows(1, self.extra)] * 2, operands, "corners", ties
+            functools.partial(corner_kernel, self.columns), [self.rows(1, self.extra)] * 2, operands, "corners", ties
         )
         self.corner_x, self.corner_y = swap(by_x, "dp", 2), swap(by_y, "dp", 4)
 
     def sides(self, ties=()):
-        by_x, by_y = small_call(
-            functools.partial(sides_kernel, self.has_bias()),
+        self.by = small_call(
+            functools.partial(sides_kernel, self.columns),
             [self.rows(2, self.extra), self.rows(2, 0)],
             [self.kept, self.got, self.corner_x, self.corner_y],
             "sides",
             ties,
         )
-        self.by = (by_x, by_y)
-        self.side_x, self.side_y = swap(by_x, "dp", 2), swap(by_y, "dp", 4)
+        self.side_x, self.side_y = swap(self.by[0], "dp", 2), swap(self.by[1], "dp", 4)
 
     def plane(self, ties=()):
         operands = [self.kept, self.got, self.side_x, self.side_y]
-        scratch = []
-        if self.has_bias():
-            operands = [self.place, *operands, self.bias, self.got_bias, self.corner_x, self.corner_y]
-            scratch = [pltpu.VMEM((4, 2, self.gates), F32)]
-        (out,) = small_call(
-            functools.partial(plane_kernel, self.has_bias()), [self.rows(2, self.extra)], operands, "plane", ties, scratch
+        return small_call(plane_kernel, [self.rows(2, 0)], operands, "plane", ties)[0]
+
+    def messages(self, second, ties=()):
+        *sent, plane = small_call(
+            functools.partial(messages_kernel, self.columns),
+            [self.rows(1, self.extra)] * 3 + [self.rows(2, self.extra)],
+            [
+                self.place, self.kept, self.got, self.side_x, self.side_y, self.bias, self.got_bias,
+                self.corner_x, self.corner_y, second,
+            ],
+            "messages",
+            ties,
+            [pltpu.VMEM((4, 2, self.gates), F32)],
         )
-        return out
-
-
-def whole_sums(place, first, second, ties=()):
-    height = (first.shape[0] - BIAS_ROWS) // 2
-    gates = first.shape[1]
-    message = jax.ShapeDtypeStruct((height + BIAS_ROWS, gates), BF16)
-    sent = small_call(messages_kernel, [message] * 3, [place, first, second], "messages", ties)
-    got = [swap(part, "section", index + 1) for index, part in enumerate(sent)]
-    return small_call(
-        whole_kernel,
-        [jax.ShapeDtypeStruct((height, gates), F32), jax.ShapeDtypeStruct((2, gates), F32)],
-        [place, first, second, *got],
-        "whole",
-        scratch=[pltpu.VMEM((4, 2, gates), F32)],
-    )
+        return [plane] + [swap(part, "section", index + 1) for index, part in enumerate(sent)]
 
 
 def all_sums(value):
@@ -822,29 +863,21 @@
     height = tap_weight.shape[1]
     quick = sections == 4 and streams == 8 and height % 16 == 0
 
-    if quick:
-        near_far = gathered_pieces(tap_weight[0])
-    else:
-        near_far = lax.all_gather(
-            lax.all_gather(tap_weight, "dp", axis=1, tiled=True), "section", axis=0, tiled=True
-        )
-    weights, plan = weight_operands(near_far)
-    weight_count = 1 if plan is None else 2 * plan
-
     def own(value):
         return lax.dynamic_slice_in_dim(value, start, rows, 0)
 
+    def own(value):
+        return lax.dynamic_slice_in_dim(value, start, rows, 0)
+
+    place = jnp.stack([section, stream]).astype(jnp.int32)
     keep = (1 - doc_starts[0]).astype(F32)[:, None]
-    x_before = jnp.concatenate([jnp.zeros_like(tokens_in[0, :1]), tokens_in[0, :-1]], axis=0)
-    x = grouped(tokens_in[0], rows)
-    prev = grouped(x_before * keep.astype(BF16), rows)
-    keep_all = grouped(jnp.broadcast_to(keep, (length, LANES)), rows)
-    keep_firsts = jnp.concatenate([keep_all[::rows], jnp.zeros((8 - sections, LANES), F32)], axis=0)
-    keep_own, x_own, prev_own = own(keep_all), own(x), own(prev)
-    place = jnp.stack([section, stream]).astype(jnp.int32)
-    bias = gate_bias.astype(F32)
+    keep_own = grouped(jnp.broadcast_to(own(keep), (rows, LANES)), rows)
+    keep_firsts = jnp.broadcast_to(jnp.concatenate([keep[::rows], keep[: 8 - sections]], axis=0), (8, LANES))
+    x = grouped(own(tokens_in[0]), rows)
+    tail = lax.dynamic_slice_in_dim(tokens_in[0], jnp.maximum(start - 16, 0), 16, 0)
     cot = grouped(own(cotangent[0]), rows)
     cot_next = lax.dynamic_slice_in_dim(cotangent[0], jnp.minimum(start + rows, length - 16), 16, 0)
+    bias = gate_bias.astype(F32)
 
     def shape(*dims, dtype=F32):
         return jax.ShapeDtypeStruct(dims, dtype)
@@ -860,33 +893,57 @@
     scan = buffer(tiles, rows, LANES)
     matrix = shape(2 * width, gates, dtype=BF16)
 
-    early = [keep_firsts, keep_own, x_own, prev_own, cot, cot_next]
-    candid0, forget0, gate0, cells0, hidden0, delayed0, last0, matrix0 = call(
-        functools.partial(first_forward_kernel, plan, rows, block),
-        [full] * 3 + [shape(tiles, rows + SUBS, LANES)] + [half] * 2 + [shape(8, width), matrix],
-        [SMEM] + [VMEM] * 4 + [HBM] * len(weights) + [ANY] * len(early),
-        [VMEM] * 8,
-        [buffer(tiles, rows + SUBS, LANES), dma((weight_count + 1,))],
-        2 * layer_flops,
+    half = shape(rows, width, dtype=BF16)
+    (prev,) = small_call(
+        before_kernel,
+        [half],
+        [place, x, tail, keep_own],
+        "before",
+        [keep_firsts, cot, cot_next, bias],
+        scratch=[buffer(tiles, rows + SUBS, LANES)],
+    )
+    early = [prev]
+    if quick:
+        weights = gathered_pieces(place, tap_weight[0], early)
+    else:
+        whole = lax.all_gather(tap_weight, "dp", axis=1, tiled=True)
+        weights = [lax.all_gather(whole, "section", axis=0, tiled=True)]
+    plan = len(weights)
+    weight_count = plan
+
+    def exchanged(summary):
+        return [summary] + [swap(summary, "section", index) for index in range(1, sections)]
+
+    candid0, forget0, gate0, summary, matrix0 = call(
+        functools.partial(first_forward_kernel, plan, block),
+        [full] * 3 + [shape(8, width), matrix],
+        [SMEM] + [VMEM] * 4 + [HBM] * len(weights),
+        [VMEM] * 5,
+        [dma((weight_count + 1,))],
+        layer_flops,
         weight_bytes + 30 * rows * width,
         LIMITS[0],
         "first_forward",
-    )(place, x, prev, keep_all, bias[0:1], *weights, *early)
-
-    candid1, forget1, gate1, summary1, matrix1 = call(
-        functools.partial(second_forward_kernel, plan, rows, block),
-        [full] * 3 + [shape(16, width), matrix],
-        [SMEM] + [VMEM] * 6 + [HBM] * len(weights),
-        [VMEM] * 5,
-        [scan, dma((weight_count + 1,))],
+    )(place, x, prev, keep_own, bias[0:1], *weights)
+
+    cells0, hidden0, delayed0, last0, candid1, forget1, gate1, summary1, matrix1 = call(
+        functools.partial(second_forward_kernel, plan, block),
+        [shape(tiles, rows + SUBS, LANES), half, half, shape(8, width)]
+        + [full] * 3
+        + [shape(16, width), matrix],
+        [SMEM] + [VMEM] * 10 + [HBM] * len(weights),
+        [VMEM] * 9,
+        [
+            buffer(sections, 8, width),
+            scan,
+            buffer(tiles, rows + SUBS, LANES),
+            dma((weight_count + 1,)),
+        ],
         layer_flops,
         weight_bytes + 20 * rows * width,
         LIMITS[1],
         "second_forward",
-    )(place, hidden0, delayed0, keep_own, cot, bias[1:2], last0, *weights)
-
-    def exchanged(summary):
-        return [summary] + [swap(summary, "section", index) for index in range(1, sections)]
+    )(place, candid0, forget0, gate0, keep_own, cot, bias[1:2], *exchanged(summary), *weights)
 
     if quick:
         kept_shape = [shape(2, 4, height, gates, dtype=BF16)] * 2
@@ -926,12 +983,15 @@
     )(place, dpre1, shifted1, candid0, forget0, gate0, keep_own, matrix1)
 
     ties = []
+    first_shape, first_columns = kept_shape, gates
     if quick:
         second.sides()
         ties = second.by
+        first_columns = gates // LANES // 2 * LANES
+        first_shape = [shape(2, 4, height, first_columns, dtype=BF16)] * 2
     dpre0, shifted0, bias_both, *kept0 = call(
         functools.partial(first_backward_kernel, rows, quick),
-        [wide, wide, shape(2 * SUBS, gates)] + kept_shape,
+        [wide, wide, shape(2 * SUBS, gates)] + first_shape,
         [SMEM] + [VMEM] * 15 + [ANY] * len(ties),
         [VMEM] * (3 + len(kept_shape)),
         [buffer(sections, 8, width), scan, buffer(3, rows + SUBS, LANES), buffer(SUBS, gates)],
@@ -940,10 +1000,17 @@
         LIMITS[4],
         "first_backward",
     )(
-        place, candid0, forget0, gate0, cells0, last0, x_own, prev_own, keep_own, arriving, keep_firsts, bias1,
+        place, candid0, forget0, gate0, cells0, last0, x, prev, keep_own, arriving, keep_firsts, bias1,
         *exchanged(summary0), *ties,
     )
     if quick:
+        later_shape = shape(2, 4, height, gates - first_columns, dtype=BF16)
+        later = small_call(
+            functools.partial(first_weights_kernel, first_columns),
+            [later_shape] * 2,
+            [place, x, prev, dpre0],
+            "first_weights",
+        )
         plane1 = second.plane()
 
     input_grad = call(
@@ -959,10 +1026,24 @@
     )(dpre0, shifted0, matrix0)
 
     if quick:
-        first = LayerSum(*kept0, bias_both, place)
-        first.corners(ties=[plane1, input_grad])
-        first.sides()
-        weight_grad, bias_grad = whole_sums(place, first.plane(), plane1)
+        got_bias = swap(bias_both, "dp", 1)
+        parts = [slice(0, first_columns), slice(first_columns, gates)]
+        sums = [
+            LayerSum(*pieces, columns, bias_both, got_bias, place)
+            for pieces, columns in zip((kept0, later), parts, strict=True)
+        ]
+        sums[0].corners()
+        sums[1].corners(ties=[input_grad])
+        sums[0].sides(ties=[plane1])
+        sums[1].sides(ties=sums[0].by)
+        got = [part.messages(plane1) for part in sums]
+        weight_grad, bias_grad = small_call(
+            functools.partial(whole_kernel, parts),
+            [shape(height, gates), shape(2, gates)],
+            [place, plane1] + got[0] + got[1],
+            "whole",
+            scratch=[buffer(4, 2, columns.stop - columns.start) for columns in parts],
+        )
         weight_grad = weight_grad[None]
     else:
         bias_grad = all_sums(bias_both[::8])

time: 219 us -> 205 us (0.936)
  local copies, waits for them, and re-layouts: 20.4 us -> 10.9 us
  other arithmetic: 4.23 us -> 0.17 us
  waiting for transfers between devices: 97.2 us -> 95 us
    ppermute x51 -> x44, waiting for transfers between devices: 97.2 us -> 73.8 us  [swap(): return lax.ppermute(value, axis, pairs)]
    ppermute x0 -> x6, waiting for transfers between devices: none -> 21.2 us  [moved(): lax.ppermute(value, axis, [(index, target(index)) for index in range(lax....]
    ppermute x0 -> x6, starting transfers between devices: none -> 8.53 us  [moved(): lax.ppermute(value, axis, [(index, target(index)) for index in range(lax....]
    ppermute x51 -> x44, starting transfers between devices: 49.9 us -> 43.2 us  [swap(): return lax.ppermute(value, axis, pairs)]
    pallas_call x8 -> x18, Pallas kernels: 4.88 us -> 11.3 us  [small_call(): call(kernel, outs, specs + [ANY] * len(ties), [VMEM] * len(outs), list(sc...]
    mul x1 -> x0, other arithmetic: 4.1 us -> none  [per_device(): prev = grouped(x_before * keep.astype(BF16), rows)]
    squeeze x1 -> x0, local copies, waits for them, and re-layouts: 3.43 us -> none  [per_device(): tokens_in[0, :-1]]
    another operation x1, local copies, waits for them, and re-layouts: 3.4 us -> 0.02 us  [grouped(): value.reshape(length // rows, SUBS, rows // SUBS, width).swapaxes(1, 2)]
  transfers between devices with their start and end apart: 51 -> 50, of which waited for: 24 -> 28; matrix products, arithmetic and copies ran while one was open for 8% -> 3% of each run, Pallas kernels for 4% -> 8%
where the time goes in v1:
time: 205 us
  waiting for transfers between devices  95 us (46%)
  starting transfers between devices  51.7 us (25%)
  Pallas kernels  45.9 us (22%)
  local copies, waits for them, and re-layouts  10.9 us (5%)
    ppermute x44, waiting for transfers between devices, swap(): return lax.ppermute(value, axis, pairs)  73.8 us
    ppermute x44, starting transfers between devices, swap(): return lax.ppermute(value, axis, pairs)  43.2 us
    ppermute x6, waiting for transfers between devices, moved(): lax.ppermute(value, axis, [(index, target(index)) for index in range(lax....  21.2 us
    pallas_call x18, Pallas kernels, small_call(): call(kernel, outs, specs + [ANY] * len(ties), [VMEM] * len(outs), list(sc...  11.3 us
    ppermute x6, starting transfers between devices, moved(): lax.ppermute(value, axis, [(index, target(index)) for index in range(lax....  8.53 us
    pallas_call x1, Pallas kernels, per_device(): call(functools.partial(second_forward_kernel, plan, block), [shape(tiles,...  7.63 us
    pallas_call x1, Pallas kernels, per_device(): call(functools.partial(second_backward_kernel, rows, quick), [half, wide,...  7.38 us
    pallas_call x1, Pallas kernels, per_device(): call(functools.partial(first_forward_kernel, plan, block), [full] * 3 + [...  6.08 us
  transfers between devices with their start and end apart: 50, of which 28 were waited for; matrix products, arithmetic and copies ran while one was open for 3% of the time, Pallas kernels for 8%

profile of v1, /device:TPU:0, one launch (start us, length us, event | category | flops | bytes accessed | tf_op | source)
XLA Modules:
  0.0 204.7 jit_solution(1268971057096475291)
XLA Ops:
  0.7 4.1 %collective-permute-start.9 = (bf16[80,1920]{1,0:T(8,128)(2,1)}, bf16[80,1920]{1,0:T(8,128)(2,1)S(1)}, u32[]{:S(2)}, u32[]{:S(2)}) collective-permute-start(bf16[80,1920]{1,0:T(8,128)(2,1)} %bitcast.49), channel_id=1, source_target_pairs={{0,16},{8,24},{16,0},{24,8},{1,17},{9,25},{17,1},{25,9},{2,18},{10... | collective-permute-start | bytes 921608 | tf_op jit(solution)/shard_map/ppermute | solution.py:748
  4.8 1.6 collective-permute-start.3
  6.4 1.4 constant_dynamic-slice_fusion
  8.7 1.4 collective-permute-start.1
  12.0 7.1 %collective-permute-done.3.own = bf16[80,1920]{1,0:T(8,128)(2,1)S(1)} collective-permute-done((bf16[80,1920]{1,0:T(8,128)(2,1)}, bf16[80,1920]{1,0:T(8,128)(2,1)S(1)}, u32[]{:S(2)}, u32[]{:S(2)}) %collective-permute-start.3) | collective-permute-done | bytes 307232 | tf_op jit(solution)/shard_map/ppermute | solution.py:748
  20.2 1.6 collective-permute-start.13
  22.3 1.4 collective-permute-start.5
  24.0 5.9 %collective-permute-done.13.own = bf16[80,1920]{1,0:T(8,128)(2,1)S(1)} collective-permute-done((bf16[80,1920]{1,0:T(8,128)(2,1)S(1)}, bf16[80,1920]{1,0:T(8,128)(2,1)S(1)}, u32[]{:S(2)}, u32[]{:S(2)}) %collective-permute-start.13) | collective-permute-done | bytes 307232 | tf_op jit(solution)/shard_map/ppermute | solution.py:748
  30.5 1.7 collective-permute-start.11
  36.4 3.7 %collective-permute-done.11.first.refs_14_.refs_20_ = bf16[160,1920]{1,0:T(8,128)(2,1)S(1)} collective-permute-done((bf16[160,1920]{1,0:T(8,128)(2,1)S(1)}, bf16[160,1920]{1,0:T(8,128)(2,1)S(1)}, u32[]{:S(2)}, u32[]{:S(2)}) %collective-permute-start.11) | collective-permute-done | bytes 614432 | tf_op jit(solution)/shard_map/ppermute | solution.py:752
  40.1 6.6 %collective-permute-done.15.second.refs_17_.refs_23_ = bf16[160,1920]{1,0:T(8,128)(2,1)S(1)} collective-permute-done((bf16[160,1920]{1,0:T(8,128)(2,1)S(1)}, bf16[160,1920]{1,0:T(8,128)(2,1)S(1)}, u32[]{:S(2)}, u32[]{:S(2)}) %collective-permute-start.15) | collective-permute-done | bytes 614432 | tf_op jit(solution)/shard_map/ppermute | solution.py:752
  47.3 1.6 collective-permute-start.17
  49.7 4.3 %collective-permute-done.7.refs_11_.refs_17_ = bf16[160,1920]{1,0:T(8,128)(2,1)S(1)} collective-permute-done((bf16[160,1920]{1,0:T(8,128)(2,1)S(1)}, bf16[160,1920]{1,0:T(8,128)(2,1)S(1)}, u32[]{:S(2)}, u32[]{:S(2)}) %collective-permute-start.7) | collective-permute-done | bytes 614432 | tf_op jit(solution)/shard_map/ppermute | solution.py:752
  54.0 6.6 %collective-permute-done.17.refs_19_.refs_25_ = bf16[160,1920]{1,0:T(8,128)(2,1)S(1)} collective-permute-done((bf16[160,1920]{1,0:T(8,128)(2,1)S(1)}, bf16[160,1920]{1,0:T(8,128)(2,1)S(1)}, u32[]{:S(2)}, u32[]{:S(2)}) %collective-permute-start.17) | collective-permute-done | bytes 614432 | tf_op jit(solution)/shard_map/ppermute | solution.py:752
  60.6 2.0 collective-permute-done.18.refs_20_.refs_26_
  62.6 6.1 %first_forward.1 = (f32[5,512,128]{2,1,0:T(8,128)S(1)}, f32[5,512,128]{2,1,0:T(8,128)S(1)}, f32[5,512,128]{2,1,0:T(8,128)S(1)}, f32[8,640]{1,0:T(8,128)S(1)}, bf16[1280,1920]{1,0:T(8,128)(2,1)S(1)}) custom-call(s32[2]{0:T(128)S(1)} %pad_add_fusion.refs_0_.place, bf16[512,640]{1,0:T(8,128)(2,1)S(1)} %bitcast.39, ...), custom_call_target="tpu_custom_call" | custom-call | flops 25165824 | bytes 147456 | tf_op jit(solution)/shard_map/first_forward/pallas_call | solution.py:917
  68.7 2.2 %copy-done = bf16[1280,1920]{1,0:T(8,128)(2,1)} copy-done((bf16[1280,1920]{1,0:T(8,128)(2,1)}, bf16[1280,1920]{1,0:T(8,128)(2,1)S(1)}, u32[]{:S(2)}) %copy-start) | copy-done | bytes 4915224
  70.9 1.6 collective-permute-start.21
  73.9 1.4 collective-permute-start.19
  77.7 7.6 %second_forward.1 = (f32[5,520,128]{2,1,0:T(8,128)S(1)}, bf16[512,640]{1,0:T(8,128)(2,1)S(1)}, bf16[512,640]{1,0:T(8,128)(2,1)S(1)}, f32[8,640]{1,0:T(8,128)S(1)...) custom-call(s32[2]{0:T(128)S(1)} %pad_add_fusion.refs_0_.place, ...), custom_call_target="tpu_custom_call" | custom-call | flops 25165824 | bytes 114688 | tf_op jit(solution)/shard_map/second_forward/pallas_call | solution.py:929
  87.2 1.9 collective-permute-start.24
  90.1 1.5 collective-permute-start.22
  91.6 1.5 collective-permute-done.24.refs_13_
  95.6 7.4 %second_backward.1 = (bf16[512,640]{1,0:T(8,128)(2,1)S(1)}, bf16[512,1920]{1,0:T(8,128)(2,1)S(1)}, bf16[512,1920]{1,0:T(8,128)(2,1)S(1)}, f32[8,1920]{1,0:T(8,12...) custom-call(s32[2]{0:T(128)S(1)} %pad_add_fusion.refs_0_.place, ...), custom_call_target="tpu_custom_call" | custom-call | flops 25165824 | bytes 147456 | tf_op jit(solution)/shard_map/second_backward/pallas_call | solution.py:954
  103.0 4.7 %collective-permute-done.28.refs_1_ = bf16[2,4,80,1920]{3,2,1,0:T(8,128)(2,1)S(1)} collective-permute-done((bf16[2,4,80,1920]{3,2,1,0:T(8,128)(2,1)S(1)}, bf16[2,4,80,1920]{3,2,1,0:T(8,128)(2,1)S(1)}, u32[]{:S(2)}, u32[]{:S(2)}) %collective-permute-start.28) | collective-permute-done | bytes 2457632 | tf_op jit(solution)/shard_map/ppermute | solution.py:748
  107.8 1.6 collective-permute-start.29
  109.4 1.5 collective-permute-start.30
  110.9 4.6 %middle.1 = (bf16[512,640]{1,0:T(8,128)(2,1)S(1)}, f32[8,640]{1,0:T(8,128)S(1)}) custom-call(s32[2]{0:T(128)S(1)} %pad_add_fusion.refs_0_.place, bf16[512,1920]{1,0:T(8,128)(2,1)S(1)} %get-tuple-element.70.refs_1_, bf16[512,1920]{1,0:T(8,128)(2,1)S(1)} %get-tuple-element.71.refs_2_, f32[5,512,128]{2,1,0:T(8,128)S(1)} %get-tuple-element.57.refs_1_.refs_3_, ...), custom_call_target="tpu_custom_call" | custom-call | flops 25165824 | bytes 114688 | tf_op jit(solution)/shard_map/middle/pallas_call | solution.py:973
  115.5 2.0 collective-permute-start.27
  118.2 1.8 collective-permute-start.25
  122.2 5.3 %first_backward.1 = (bf16[512,1920]{1,0:T(8,128)(2,1)S(1)}, bf16[512,1920]{1,0:T(8,128)(2,1)S(1)}, f32[16,1920]{1,0:T(8,128)S(1)}, bf16[2,4,80,896]{3,2,1,0:T(8,128)(2,1)S(1)}, bf16[2,4,80,896]{3,2,1,0:T(8,128)(2,1)S(1)}) custom-call(s32[2]{0:T(128)S(1)} %pad_add_fusion.refs_0_.place, f32[5,512,128]{2,1,0:T(8,128)S(1)} %get-tuple-element.57.refs_1_.refs_3_, ...), custom_call_target="tpu_custom_call" | custom-call | flops 25165824 | bytes 147456 | tf_op jit(solution)/shard_map/first_backward/pallas_call | solution.py:992
  127.5 2.1 %first_weights.1 = (bf16[2,4,80,1024]{3,2,1,0:T(8,128)(2,1)S(1)}, bf16[2,4,80,1024]{3,2,1,0:T(8,128)(2,1)S(1)}) custom-call(s32[2]{0:T(128)S(1)} %pad_add_fusion.refs_0_.place, bf16[512,640]{1,0:T(8,128)(2,1)S(1)} %bitcast.41, bf16[512,640]{1,0:T(8,128)(2,1)S(1)} %before.1.refs_1_.refs_2_.refs_7_, bf16[512,1920]{1,0:T(8,128)(2,1)S(1)} %get-tuple-element.82.refs_0_.refs_3_), custom_call_target="tpu_custom_call" | custom-call | flops 10000 | bytes 10000 | tf_op jit(solution)/shard_map/first_weights/pallas_call | solution.py:733
  131.3 3.3 %collective-permute-done.34.refs_3_.refs_6_ = f32[16,1920]{1,0:T(8,128)S(1)} collective-permute-done((f32[16,1920]{1,0:T(8,128)S(1)}, f32[16,1920]{1,0:T(8,128)S(1)}, u32[]{:S(2)}, u32[]{:S(2)}) %collective-permute-start.34) | collective-permute-done | bytes 122912 | tf_op jit(solution)/shard_map/ppermute | solution.py:748
  135.8 3.7 %last.1.refs_4_ = f32[512,640]{1,0:T(8,128)S(1)} custom-call(bf16[512,1920]{1,0:T(8,128)(2,1)S(1)} %get-tuple-element.82.refs_0_.refs_3_, bf16[512,1920]{1,0:T(8,128)(2,1)S(1)} %get-tuple-element.83.refs_1_, bf16[1280,1920]{1,0:T(8,128)(2,1)S(1)} %bitcast.47), custom_call_target="tpu_custom_call" | custom-call | flops 25165824 | bytes 114688 | tf_op jit(solution)/shard_map/last/pallas_call | solution.py:1016
  139.6 1.5 collective-permute-start.43
  141.1 5.8 %collective-permute-done.31.refs_2_ = bf16[160,1920]{1,0:T(8,128)(2,1)S(1)} collective-permute-done((bf16[160,1920]{1,0:T(8,128)(2,1)S(1)}, bf16[160,1920]{1,0:T(8,128)(2,1)S(1)}, u32[]{:S(2)}, u32[]{:S(2)}) %collective-permute-start.31) | collective-permute-done | bytes 614432 | tf_op jit(solution)/shard_map/ppermute | solution.py:748
  147.8 2.8 %collective-permute-done.35.refs_2_.refs_7_ = bf16[96,896]{1,0:T(8,128)(2,1)S(1)} collective-permute-done((bf16[96,896]{1,0:T(8,128)(2,1)S(1)}, bf16[96,896]{1,0:T(8,128)(2,1)S(1)}, u32[]{:S(2)}, u32[]{:S(2)}) %collective-permute-start.35) | collective-permute-done | bytes 172064 | tf_op jit(solution)/shard_map/ppermute | solution.py:748
  151.4 1.6 collective-permute-start.37
  153.5 1.4 collective-permute-done.43.refs_2_.refs_7_
  155.6 1.6 collective-permute-start.45
  157.7 5.0 %collective-permute-done.38.refs_4_ = bf16[160,896]{1,0:T(8,128)(2,1)S(1)} collective-permute-done((bf16[160,896]{1,0:T(8,128)(2,1)S(1)}, bf16[160,896]{1,0:T(8,128)(2,1)S(1)}, u32[]{:S(2)}, u32[]{:S(2)}) %collective-permute-start.38) | collective-permute-done | bytes 286752 | tf_op jit(solution)/shard_map/ppermute | solution.py:748
  163.6 1.6 collective-permute-start.39
  165.2 2.2 %collective-permute-done.46.refs_4_ = bf16[160,1024]{1,0:T(8,128)(2,1)S(1)} collective-permute-done((bf16[160,1024]{1,0:T(8,128)(2,1)S(1)}, bf16[160,1024]{1,0:T(8,128)(2,1)S(1)}, u32[]{:S(2)}, u32[]{:S(2)}) %collective-permute-start.46) | collective-permute-done | bytes 327712 | tf_op jit(solution)/shard_map/ppermute | solution.py:748
  169.4 1.6 collective-permute-start.47
  172.0 1.9 collective-permute-start.49
  175.0 1.9 collective-permute-start.41
  179.1 24.0 %collective-permute-done.40.refs_4_ = bf16[96,896]{1,0:T(8,128)(2,1)S(1)} collective-permute-done((bf16[96,896]{1,0:T(8,128)(2,1)S(1)}, bf16[96,896]{1,0:T(8,128)(2,1)S(1)}, u32[]{:S(2)}, u32[]{:S(2)}) %collective-permute-start.40) | collective-permute-done | bytes 172064 | tf_op jit(solution)/shard_map/ppermute | solution.py:748
  203.1 1.6 whole.1
  (115 shorter events, 36.5 us)
Async XLA Ops:
  0.7 19.5 %collective-permute-start.9 = (bf16[80,1920]{1,0:T(8,128)(2,1)}, bf16[80,1920]{1,0:T(8,128)(2,1)S(1)}, u32[]{:S(2)}, u32[]{:S(2)}) collective-permute-start(bf16[80,1920]{1,0:T(8,128)(2,1)} %bitcast.49), channel_id=1, source_target_pairs={{0,16},{8,24},{16,0},{24,8},{1,17},{9,25},{17,1},{25,9},{2,18},{10... | collective-permute-start | bytes 921608 | tf_op jit(solution)/shard_map/ppermute | solution.py:748
  4.8 14.4 %collective-permute-start.3 = (bf16[80,1920]{1,0:T(8,128)(2,1)}, bf16[80,1920]{1,0:T(8,128)(2,1)S(1)}, u32[]{:S(2)}, u32[]{:S(2)}) collective-permute-start(bf16[80,1920]{1,0:T(8,128)(2,1)} %bitcast.50), channel_id=1, source_target_pairs={{0,8},{8,0},{16,24},{24,16},{1,9},{9,1},{17,25},{25,17},{2,10},{10... | collective-permute-start | bytes 921608 | tf_op jit(solution)/shard_map/ppermute | solution.py:748
  8.7 13.0 %collective-permute-start.1 = (bf16[160,1920]{1,0:T(8,128)(2,1)S(1)}, bf16[160,1920]{1,0:T(8,128)(2,1)S(1)}, u32[]{:S(2)}, u32[]{:S(2)}) collective-permute-start(bf16[160,1920]{1,0:T(8,128)(2,1)S(1)} %join.4.refs_5_.refs_11_), channel_id=1, source_target_pairs={{0,3},{1,4},{2,1},{3,6},{4,7},{5,0},{6,5},{7,2},{8,11},{9,12},{10,... | collective-permute-start | bytes 1843208 | tf_op jit(solution)/shard_map/ppermute | solution.py:752
  19.1 2.6 %collective-permute-start.4 = (bf16[80,1920]{1,0:T(8,128)(2,1)S(1)}, bf16[80,1920]{1,0:T(8,128)(2,1)S(1)}, u32[]{:S(2)}, u32[]{:S(2)}) collective-permute-start(bf16[80,1920]{1,0:T(8,128)(2,1)S(1)} %collective-permute-done.3.own), channel_id=1, source_target_pairs={{0,1},{1,0},{2,3},{3,2},{4,5},{5,4},{6,7},{7,6},{8,9},{9,8},{10,11... | collective-permute-start | bytes 921608 | tf_op jit(solution)/shard_map/ppermute | solution.py:748
  20.2 9.7 %collective-permute-start.13 = (bf16[80,1920]{1,0:T(8,128)(2,1)S(1)}, bf16[80,1920]{1,0:T(8,128)(2,1)S(1)}, u32[]{:S(2)}, u32[]{:S(2)}) collective-permute-start(bf16[80,1920]{1,0:T(8,128)(2,1)S(1)} %collective-permute-done.9.own), channel_id=1, source_target_pairs={{0,8},{8,0},{16,24},{24,16},{1,9},{9,1},{17,25},{25,17},{2,10},{10... | collective-permute-start | bytes 921608 | tf_op jit(solution)/shard_map/ppermute | solution.py:748
  22.3 9.9 %collective-permute-start.5 = (bf16[160,1920]{1,0:T(8,128)(2,1)S(1)}, bf16[160,1920]{1,0:T(8,128)(2,1)S(1)}, u32[]{:S(2)}, u32[]{:S(2)}) collective-permute-start(bf16[160,1920]{1,0:T(8,128)(2,1)S(1)} %join.5.refs_8_.refs_14_), channel_id=1, source_target_pairs={{0,3},{1,4},{2,1},{3,6},{4,7},{5,0},{6,5},{7,2},{8,11},{9,12},{10,... | collective-permute-start | bytes 1843208 | tf_op jit(solution)/shard_map/ppermute | solution.py:752
  23.7 6.2 %collective-permute-start.10 = (bf16[80,1920]{1,0:T(8,128)(2,1)S(1)}, bf16[80,1920]{1,0:T(8,128)(2,1)S(1)}, u32[]{:S(2)}, u32[]{:S(2)}) collective-permute-start(bf16[80,1920]{1,0:T(8,128)(2,1)S(1)} %collective-permute-done.9.own), channel_id=1, source_target_pairs={{0,1},{1,0},{2,3},{3,2},{4,5},{5,4},{6,7},{7,6},{8,9},{9,8},{10,11... | collective-permute-start | bytes 921608 | tf_op jit(solution)/shard_map/ppermute | solution.py:748
  29.9 2.3 %collective-permute-start.14 = (bf16[80,1920]{1,0:T(8,128)(2,1)S(1)}, bf16[80,1920]{1,0:T(8,128)(2,1)S(1)}, u32[]{:S(2)}, u32[]{:S(2)}) collective-permute-start(bf16[80,1920]{1,0:T(8,128)(2,1)S(1)} %collective-permute-done.13.own), channel_id=1, source_target_pairs={{0,1},{1,0},{2,3},{3,2},{4,5},{5,4},{6,7},{7,6},{8,9},{9,8},{10,11... | collective-permute-start | bytes 921608 | tf_op jit(solution)/shard_map/ppermute | solution.py:748
  30.5 9.6 %collective-permute-start.11 = (bf16[160,1920]{1,0:T(8,128)(2,1)S(1)}, bf16[160,1920]{1,0:T(8,128)(2,1)S(1)}, u32[]{:S(2)}, u32[]{:S(2)}) collective-permute-start(bf16[160,1920]{1,0:T(8,128)(2,1)S(1)} %join.6.refs_13_.refs_19_), channel_id=1, source_target_pairs={{0,3},{1,4},{2,1},{3,6},{4,7},{5,0},{6,5},{7,2},{8,11},{9,12},{10,... | collective-permute-start | bytes 1843208 | tf_op jit(solution)/shard_map/ppermute | solution.py:752
  32.8 13.9 %collective-permute-start.15 = (bf16[160,1920]{1,0:T(8,128)(2,1)S(1)}, bf16[160,1920]{1,0:T(8,128)(2,1)S(1)}, u32[]{:S(2)}, u32[]{:S(2)}) collective-permute-start(bf16[160,1920]{1,0:T(8,128)(2,1)S(1)} %join.7.refs_16_.refs_22_), channel_id=1, source_target_pairs={{0,3},{1,4},{2,1},{3,6},{4,7},{5,0},{6,5},{7,2},{8,11},{9,12},{10,... | collective-permute-start | bytes 1843208 | tf_op jit(solution)/shard_map/ppermute | solution.py:752
  34.0 15.4 %collective-permute-start.2 = (bf16[160,1920]{1,0:T(8,128)(2,1)S(1)}, bf16[160,1920]{1,0:T(8,128)(2,1)S(1)}, u32[]{:S(2)}, u32[]{:S(2)}) collective-permute-start(bf16[160,1920]{1,0:T(8,128)(2,1)S(1)} %collective-permute-done.1.refs_0_.first.refs_6_.refs_12_), channel_id=1, source_target_pairs={{0,1},{1,0},{2,3},{3,2},{4,5},{5,4},{6,7},{7,6},{8,9},{9,8},{10,11... | collective-permute-start | bytes 1843208 | tf_op jit(solution)/shard_map/ppermute | solution.py:748
  35.1 18.9 %collective-permute-start.7 = (bf16[160,1920]{1,0:T(8,128)(2,1)S(1)}, bf16[160,1920]{1,0:T(8,128)(2,1)S(1)}, u32[]{:S(2)}, u32[]{:S(2)}) collective-permute-start(bf16[160,1920]{1,0:T(8,128)(2,1)S(1)} %pick.2), channel_id=1, source_target_pairs={{0,2},{1,5},{2,0},{3,7},{4,6},{5,1},{6,4},{7,3},{8,10},{9,13},{10,... | collective-permute-start | bytes 1843208 | tf_op jit(solution)/shard_map/ppermute | solution.py:752
  47.3 13.2 %collective-permute-start.17 = (bf16[160,1920]{1,0:T(8,128)(2,1)S(1)}, bf16[160,1920]{1,0:T(8,128)(2,1)S(1)}, u32[]{:S(2)}, u32[]{:S(2)}) collective-permute-start(bf16[160,1920]{1,0:T(8,128)(2,1)S(1)} %pick.3), channel_id=1, source_target_pairs={{0,2},{1,5},{2,0},{3,7},{4,6},{5,1},{6,4},{7,3},{8,10},{9,13},{10,... | collective-permute-start | bytes 1843208 | tf_op jit(solution)/shard_map/ppermute | solution.py:752
  48.9 11.7 %collective-permute-start.12 = (bf16[160,1920]{1,0:T(8,128)(2,1)S(1)}, bf16[160,1920]{1,0:T(8,128)(2,1)S(1)}, u32[]{:S(2)}, u32[]{:S(2)}) collective-permute-start(bf16[160,1920]{1,0:T(8,128)(2,1)S(1)} %collective-permute-done.11.first.refs_14_.refs_20_), channel_id=1, source_target_pairs={{0,1},{1,0},{2,3},{3,2},{4,5},{5,4},{6,7},{7,6},{8,9},{9,8},{10,11... | collective-permute-start | bytes 1843208 | tf_op jit(solution)/shard_map/ppermute | solution.py:748
  49.2 11.4 %collective-permute-start.6 = (bf16[160,1920]{1,0:T(8,128)(2,1)S(1)}, bf16[160,1920]{1,0:T(8,128)(2,1)S(1)}, u32[]{:S(2)}, u32[]{:S(2)}) collective-permute-start(bf16[160,1920]{1,0:T(8,128)(2,1)S(1)} %collective-permute-done.5.second.refs_0_.refs_9_.refs_15_), channel_id=1, source_target_pairs={{0,1},{1,0},{2,3},{3,2},{4,5},{5,4},{6,7},{7,6},{8,9},{9,8},{10,11... | collective-permute-start | bytes 1843208 | tf_op jit(solution)/shard_map/ppermute | solution.py:748
  49.5 11.2 %collective-permute-start.16 = (bf16[160,1920]{1,0:T(8,128)(2,1)S(1)}, bf16[160,1920]{1,0:T(8,128)(2,1)S(1)}, u32[]{:S(2)}, u32[]{:S(2)}) collective-permute-start(bf16[160,1920]{1,0:T(8,128)(2,1)S(1)} %collective-permute-done.15.second.refs_17_.refs_23_), channel_id=1, source_target_pairs={{0,1},{1,0},{2,3},{3,2},{4,5},{5,4},{6,7},{7,6},{8,9},{9,8},{10,11... | collective-permute-start | bytes 1843208 | tf_op jit(solution)/shard_map/ppermute | solution.py:748
  54.0 6.6 %collective-permute-start.8 = (bf16[160,1920]{1,0:T(8,128)(2,1)S(1)}, bf16[160,1920]{1,0:T(8,128)(2,1)S(1)}, u32[]{:S(2)}, u32[]{:S(2)}) collective-permute-start(bf16[160,1920]{1,0:T(8,128)(2,1)S(1)} %collective-permute-done.7.refs_11_.refs_17_), channel_id=1, source_target_pairs={{0,1},{1,0},{2,3},{3,2},{4,5},{5,4},{6,7},{7,6},{8,9},{9,8},{10,11... | collective-permute-start | bytes 1843208 | tf_op jit(solution)/shard_map/ppermute | solution.py:748
  70.9 5.7 %collective-permute-start.21 = (f32[8,640]{1,0:T(8,128)S(1)}, f32[8,640]{1,0:T(8,128)S(1)}, u32[]{:S(2)}, u32[]{:S(2)}) collective-permute-start(f32[8,640]{1,0:T(8,128)S(1)} %get-tuple-element.60.refs_7_), channel_id=1, source_target_pairs={{0,24},{8,16},{16,8},{24,0},{1,25},{9,17},{17,9},{25,1},{2,26},{10... | collective-permute-start | bytes 61448 | tf_op jit(solution)/shard_map/ppermute | solution.py:748
  72.6 4.7 %collective-permute-start.20 = (f32[8,640]{1,0:T(8,128)S(1)}, f32[8,640]{1,0:T(8,128)S(1)}, u32[]{:S(2)}, u32[]{:S(2)}) collective-permute-start(f32[8,640]{1,0:T(8,128)S(1)} %get-tuple-element.60.refs_7_), channel_id=1, source_target_pairs={{0,16},{8,24},{16,0},{24,8},{1,17},{9,25},{17,1},{25,9},{2,18},{10... | collective-permute-start | bytes 61448 | tf_op jit(solution)/shard_map/ppermute | solution.py:748
  73.9 3.8 %collective-permute-start.19 = (f32[8,640]{1,0:T(8,128)S(1)}, f32[8,640]{1,0:T(8,128)S(1)}, u32[]{:S(2)}, u32[]{:S(2)}) collective-permute-start(f32[8,640]{1,0:T(8,128)S(1)} %get-tuple-element.60.refs_7_), channel_id=1, source_target_pairs={{0,8},{8,0},{16,24},{24,16},{1,9},{9,1},{17,25},{25,17},{2,10},{10... | collective-permute-start | bytes 61448 | tf_op jit(solution)/shard_map/ppermute | solution.py:748
  87.2 5.9 %collective-permute-start.24 = (f32[16,640]{1,0:T(8,128)S(1)}, f32[16,640]{1,0:T(8,128)S(1)}, u32[]{:S(2)}, u32[]{:S(2)}) collective-permute-start(f32[16,640]{1,0:T(8,128)S(1)} %get-tuple-element.66.refs_10_), channel_id=1, source_target_pairs={{0,24},{8,16},{16,8},{24,0},{1,25},{9,17},{17,9},{25,1},{2,26},{10... | collective-permute-start | bytes 122888 | tf_op jit(solution)/shard_map/ppermute | solution.py:748
  89.1 5.0 %collective-permute-start.23 = (f32[16,640]{1,0:T(8,128)S(1)}, f32[16,640]{1,0:T(8,128)S(1)}, u32[]{:S(2)}, u32[]{:S(2)}) collective-permute-start(f32[16,640]{1,0:T(8,128)S(1)} %get-tuple-element.66.refs_10_), channel_id=1, source_target_pairs={{0,16},{8,24},{16,0},{24,8},{1,17},{9,25},{17,1},{25,9},{2,18},{10... | collective-permute-start | bytes 122888 | tf_op jit(solution)/shard_map/ppermute | solution.py:748
  90.1 4.4 %collective-permute-start.22 = (f32[16,640]{1,0:T(8,128)S(1)}, f32[16,640]{1,0:T(8,128)S(1)}, u32[]{:S(2)}, u32[]{:S(2)}) collective-permute-start(f32[16,640]{1,0:T(8,128)S(1)} %get-tuple-element.66.refs_10_), channel_id=1, source_target_pairs={{0,8},{8,0},{16,24},{24,16},{1,9},{9,1},{17,25},{25,17},{2,10},{10... | collective-permute-start | bytes 122888 | tf_op jit(solution)/shard_map/ppermute | solution.py:748
  103.0 4.7 %collective-permute-start.28 = (bf16[2,4,80,1920]{3,2,1,0:T(8,128)(2,1)S(1)}, bf16[2,4,80,1920]{3,2,1,0:T(8,128)(2,1)S(1)}, u32[]{:S(2)}, u32[]{:S(2)}) collective-permute-start(bf16[2,4,80,1920]{3,2,1,0:T(8,128)(2,1)S(1)} %get-tuple-element.77), channel_id=1, source_target_pairs={{0,1},{1,0},{2,3},{3,2},{4,5},{5,4},{6,7},{7,6},{8,9},{9,8},{10,11... | collective-permute-start | bytes 7372808 | tf_op jit(solution)/shard_map/ppermute | solution.py:748
  107.8 12.2 %collective-permute-start.29 = (bf16[80,1920]{1,0:T(8,128)(2,1)S(1)}, bf16[80,1920]{1,0:T(8,128)(2,1)S(1)}, u32[]{:S(2)}, u32[]{:S(2)}) collective-permute-start(bf16[80,1920]{1,0:T(8,128)(2,1)S(1)} %get-tuple-element.78), channel_id=1, source_target_pairs={{0,2},{1,3},{2,0},{3,1},{4,6},{5,7},{6,4},{7,5},{8,10},{9,11},{10,... | collective-permute-start | bytes 921608 | tf_op jit(solution)/shard_map/ppermute | solution.py:748
  109.4 10.6 %collective-permute-start.30 = (bf16[80,1920]{1,0:T(8,128)(2,1)S(1)}, bf16[80,1920]{1,0:T(8,128)(2,1)S(1)}, u32[]{:S(2)}, u32[]{:S(2)}) collective-permute-start(bf16[80,1920]{1,0:T(8,128)(2,1)S(1)} %get-tuple-element.79), channel_id=1, source_target_pairs={{0,4},{1,5},{2,6},{3,7},{4,0},{5,1},{6,2},{7,3},{8,12},{9,13},{10,... | collective-permute-start | bytes 921608 | tf_op jit(solution)/shard_map/ppermute | solution.py:748
  115.5 5.6 %collective-permute-start.27 = (f32[8,640]{1,0:T(8,128)S(1)}, f32[8,640]{1,0:T(8,128)S(1)}, u32[]{:S(2)}, u32[]{:S(2)}) collective-permute-start(f32[8,640]{1,0:T(8,128)S(1)} %get-tuple-element.75.refs_12_), channel_id=1, source_target_pairs={{0,24},{8,16},{16,8},{24,0},{1,25},{9,17},{17,9},{25,1},{2,26},{10... | collective-permute-start | bytes 61448 | tf_op jit(solution)/shard_map/ppermute | solution.py:748
  117.5 4.7 %collective-permute-start.26 = (f32[8,640]{1,0:T(8,128)S(1)}, f32[8,640]{1,0:T(8,128)S(1)}, u32[]{:S(2)}, u32[]{:S(2)}) collective-permute-start(f32[8,640]{1,0:T(8,128)S(1)} %get-tuple-element.75.refs_12_), channel_id=1, source_target_pairs={{0,16},{8,24},{16,0},{24,8},{1,17},{9,25},{17,1},{25,9},{2,18},{10... | collective-permute-start | bytes 61448 | tf_op jit(solution)/shard_map/ppermute | solution.py:748
  118.2 4.0 %collective-permute-start.25 = (f32[8,640]{1,0:T(8,128)S(1)}, f32[8,640]{1,0:T(8,128)S(1)}, u32[]{:S(2)}, u32[]{:S(2)}) collective-permute-start(f32[8,640]{1,0:T(8,128)S(1)} %get-tuple-element.75.refs_12_), channel_id=1, source_target_pairs={{0,8},{8,0},{16,24},{24,16},{1,9},{9,1},{17,25},{25,17},{2,10},{10... | collective-permute-start | bytes 61448 | tf_op jit(solution)/shard_map/ppermute | solution.py:748
  129.7 9.8 %collective-permute-start.42 = (bf16[2,4,80,1024]{3,2,1,0:T(8,128)(2,1)S(1)}, bf16[2,4,80,1024]{3,2,1,0:T(8,128)(2,1)S(1)}, u32[]{:S(2)}, u32[]{:S(2)}) collective-permute-start(bf16[2,4,80,1024]{3,2,1,0:T(8,128)(2,1)S(1)} %get-tuple-element.97), channel_id=1, source_target_pairs={{0,1},{1,0},{2,3},{3,2},{4,5},{5,4},{6,7},{7,6},{8,9},{9,8},{10,11... | collective-permute-start | bytes 3932168 | tf_op jit(solution)/shard_map/ppermute | solution.py:748
  129.7 4.8 %collective-permute-start.33 = (bf16[2,4,80,896]{3,2,1,0:T(8,128)(2,1)S(1)}, bf16[2,4,80,896]{3,2,1,0:T(8,128)(2,1)S(1)}, u32[]{:S(2)}, u32[]{:S(2)}) collective-permute-start(bf16[2,4,80,896]{3,2,1,0:T(8,128)(2,1)S(1)} %get-tuple-element.86), channel_id=1, source_target_pairs={{0,1},{1,0},{2,3},{3,2},{4,5},{5,4},{6,7},{7,6},{8,9},{9,8},{10,11... | collective-permute-start | bytes 3440648 | tf_op jit(solution)/shard_map/ppermute | solution.py:748
  130.2 16.7 %collective-permute-start.31 = (bf16[160,1920]{1,0:T(8,128)(2,1)S(1)}, bf16[160,1920]{1,0:T(8,128)(2,1)S(1)}, u32[]{:S(2)}, u32[]{:S(2)}) collective-permute-start(bf16[160,1920]{1,0:T(8,128)(2,1)S(1)} %get-tuple-element.80.refs_16_), channel_id=1, source_target_pairs={{0,2},{1,3},{2,0},{3,1},{4,6},{5,7},{6,4},{7,5},{8,10},{9,11},{10,... | collective-permute-start | bytes 1843208 | tf_op jit(solution)/shard_map/ppermute | solution.py:748
  130.8 16.7 %collective-permute-start.32 = (bf16[160,1920]{1,0:T(8,128)(2,1)S(1)}, bf16[160,1920]{1,0:T(8,128)(2,1)S(1)}, u32[]{:S(2)}, u32[]{:S(2)}) collective-permute-start(bf16[160,1920]{1,0:T(8,128)(2,1)S(1)} %get-tuple-element.81.refs_17_), channel_id=1, source_target_pairs={{0,4},{1,5},{2,6},{3,7},{4,0},{5,1},{6,2},{7,3},{8,12},{9,13},{10,... | collective-permute-start | bytes 1843208 | tf_op jit(solution)/shard_map/ppermute | solution.py:748
  131.3 3.3 %collective-permute-start.34 = (f32[16,1920]{1,0:T(8,128)S(1)}, f32[16,1920]{1,0:T(8,128)S(1)}, u32[]{:S(2)}, u32[]{:S(2)}) collective-permute-start(f32[16,1920]{1,0:T(8,128)S(1)} %get-tuple-element.87.refs_2_.refs_5_), channel_id=1, source_target_pairs={{0,1},{1,0},{2,3},{3,2},{4,5},{5,4},{6,7},{7,6},{8,9},{9,8},{10,11... | collective-permute-start | bytes 368648 | tf_op jit(solution)/shard_map/ppermute | solution.py:748
  134.7 16.0 %collective-permute-start.35 = (bf16[96,896]{1,0:T(8,128)(2,1)S(1)}, bf16[96,896]{1,0:T(8,128)(2,1)S(1)}, u32[]{:S(2)}, u32[]{:S(2)}) collective-permute-start(bf16[96,896]{1,0:T(8,128)(2,1)S(1)} %get-tuple-element.88), channel_id=1, source_target_pairs={{0,2},{1,3},{2,0},{3,1},{4,6},{5,7},{6,4},{7,5},{8,10},{9,11},{10,... | collective-permute-start | bytes 516104 | tf_op jit(solution)/shard_map/ppermute | solution.py:748
  135.3 15.9 %collective-permute-start.36 = (bf16[96,896]{1,0:T(8,128)(2,1)S(1)}, bf16[96,896]{1,0:T(8,128)(2,1)S(1)}, u32[]{:S(2)}, u32[]{:S(2)}) collective-permute-start(bf16[96,896]{1,0:T(8,128)(2,1)S(1)} %get-tuple-element.89), channel_id=1, source_target_pairs={{0,4},{1,5},{2,6},{3,7},{4,0},{5,1},{6,2},{7,3},{8,12},{9,13},{10,... | collective-permute-start | bytes 516104 | tf_op jit(solution)/shard_map/ppermute | solution.py:748
  139.6 15.3 %collective-permute-start.43 = (bf16[96,1024]{1,0:T(8,128)(2,1)S(1)}, bf16[96,1024]{1,0:T(8,128)(2,1)S(1)}, u32[]{:S(2)}, u32[]{:S(2)}) collective-permute-start(bf16[96,1024]{1,0:T(8,128)(2,1)S(1)} %get-tuple-element.98), channel_id=1, source_target_pairs={{0,2},{1,3},{2,0},{3,1},{4,6},{5,7},{6,4},{7,5},{8,10},{9,11},{10,... | collective-permute-start | bytes 589832 | tf_op jit(solution)/shard_map/ppermute | solution.py:748
  147.0 8.5 %collective-permute-start.44 = (bf16[96,1024]{1,0:T(8,128)(2,1)S(1)}, bf16[96,1024]{1,0:T(8,128)(2,1)S(1)}, u32[]{:S(2)}, u32[]{:S(2)}) collective-permute-start(bf16[96,1024]{1,0:T(8,128)(2,1)S(1)} %get-tuple-element.99), channel_id=1, source_target_pairs={{0,4},{1,5},{2,6},{3,7},{4,0},{5,1},{6,2},{7,3},{8,12},{9,13},{10,... | collective-permute-start | bytes 589832 | tf_op jit(solution)/shard_map/ppermute | solution.py:748
  151.4 11.3 %collective-permute-start.37 = (bf16[176,896]{1,0:T(8,128)(2,1)S(1)}, bf16[176,896]{1,0:T(8,128)(2,1)S(1)}, u32[]{:S(2)}, u32[]{:S(2)}) collective-permute-start(bf16[176,896]{1,0:T(8,128)(2,1)S(1)} %get-tuple-element.90.refs_4_), channel_id=1, source_target_pairs={{0,2},{1,3},{2,0},{3,1},{4,6},{5,7},{6,4},{7,5},{8,10},{9,11},{10,... | collective-permute-start | bytes 946184 | tf_op jit(solution)/shard_map/ppermute | solution.py:748
  152.9 9.8 %collective-permute-start.38 = (bf16[160,896]{1,0:T(8,128)(2,1)S(1)}, bf16[160,896]{1,0:T(8,128)(2,1)S(1)}, u32[]{:S(2)}, u32[]{:S(2)}) collective-permute-start(bf16[160,896]{1,0:T(8,128)(2,1)S(1)} %get-tuple-element.91.refs_5_), channel_id=1, source_target_pairs={{0,4},{1,5},{2,6},{3,7},{4,0},{5,1},{6,2},{7,3},{8,12},{9,13},{10,... | collective-permute-start | bytes 860168 | tf_op jit(solution)/shard_map/ppermute | solution.py:748
  155.6 12.8 %collective-permute-start.45 = (bf16[176,1024]{1,0:T(8,128)(2,1)S(1)}, bf16[176,1024]{1,0:T(8,128)(2,1)S(1)}, u32[]{:S(2)}, u32[]{:S(2)}) collective-permute-start(bf16[176,1024]{1,0:T(8,128)(2,1)S(1)} %get-tuple-element.100), channel_id=1, source_target_pairs={{0,2},{1,3},{2,0},{3,1},{4,6},{5,7},{6,4},{7,5},{8,10},{9,11},{10,... | collective-permute-start | bytes 1081352 | tf_op jit(solution)/shard_map/ppermute | solution.py:748
  157.2 10.2 %collective-permute-start.46 = (bf16[160,1024]{1,0:T(8,128)(2,1)S(1)}, bf16[160,1024]{1,0:T(8,128)(2,1)S(1)}, u32[]{:S(2)}, u32[]{:S(2)}) collective-permute-start(bf16[160,1024]{1,0:T(8,128)(2,1)S(1)} %get-tuple-element.101), channel_id=1, source_target_pairs={{0,4},{1,5},{2,6},{3,7},{4,0},{5,1},{6,2},{7,3},{8,12},{9,13},{10,... | collective-permute-start | bytes 983048 | tf_op jit(solution)/shard_map/ppermute | solution.py:748
  163.6 11.3 %collective-permute-start.39 = (bf16[96,896]{1,0:T(8,128)(2,1)S(1)}, bf16[96,896]{1,0:T(8,128)(2,1)S(1)}, u32[]{:S(2)}, u32[]{:S(2)}) collective-permute-start(bf16[96,896]{1,0:T(8,128)(2,1)S(1)} %get-tuple-element.93), channel_id=1, source_target_pairs={{0,8},{8,0},{16,24},{24,16},{1,9},{9,1},{17,25},{25,17},{2,10},{10... | collective-permute-start | bytes 516104 | tf_op jit(solution)/shard_map/ppermute | solution.py:748
  169.4 33.7 %collective-permute-start.47 = (bf16[96,1024]{1,0:T(8,128)(2,1)S(1)}, bf16[96,1024]{1,0:T(8,128)(2,1)S(1)}, u32[]{:S(2)}, u32[]{:S(2)}) collective-permute-start(bf16[96,1024]{1,0:T(8,128)(2,1)S(1)} %get-tuple-element.103), channel_id=1, source_target_pairs={{0,8},{8,0},{16,24},{24,16},{1,9},{9,1},{17,25},{25,17},{2,10},{10... | collective-permute-start | bytes 589832 | tf_op jit(solution)/shard_map/ppermute | solution.py:748
  171.0 32.0 %collective-permute-start.48 = (bf16[96,1024]{1,0:T(8,128)(2,1)S(1)}, bf16[96,1024]{1,0:T(8,128)(2,1)S(1)}, u32[]{:S(2)}, u32[]{:S(2)}) collective-permute-start(bf16[96,1024]{1,0:T(8,128)(2,1)S(1)} %get-tuple-element.104), channel_id=1, source_target_pairs={{0,16},{8,24},{16,0},{24,8},{1,17},{9,25},{17,1},{25,9},{2,18},{10... | collective-permute-start | bytes 589832 | tf_op jit(solution)/shard_map/ppermute | solution.py:748
  172.0 31.1 %collective-permute-start.49 = (bf16[96,1024]{1,0:T(8,128)(2,1)S(1)}, bf16[96,1024]{1,0:T(8,128)(2,1)S(1)}, u32[]{:S(2)}, u32[]{:S(2)}) collective-permute-start(bf16[96,1024]{1,0:T(8,128)(2,1)S(1)} %get-tuple-element.105), channel_id=1, source_target_pairs={{0,24},{8,16},{16,8},{24,0},{1,25},{9,17},{17,9},{25,1},{2,26},{10... | collective-permute-start | bytes 589832 | tf_op jit(solution)/shard_map/ppermute | solution.py:748
  173.9 29.2 %collective-permute-start.40 = (bf16[96,896]{1,0:T(8,128)(2,1)S(1)}, bf16[96,896]{1,0:T(8,128)(2,1)S(1)}, u32[]{:S(2)}, u32[]{:S(2)}) collective-permute-start(bf16[96,896]{1,0:T(8,128)(2,1)S(1)} %get-tuple-element.94), channel_id=1, source_target_pairs={{0,16},{8,24},{16,0},{24,8},{1,17},{9,25},{17,1},{25,9},{2,18},{10... | collective-permute-start | bytes 516104 | tf_op jit(solution)/shard_map/ppermute | solution.py:748
  175.0 28.1 %collective-permute-start.41 = (bf16[96,896]{1,0:T(8,128)(2,1)S(1)}, bf16[96,896]{1,0:T(8,128)(2,1)S(1)}, u32[]{:S(2)}, u32[]{:S(2)}) collective-permute-start(bf16[96,896]{1,0:T(8,128)(2,1)S(1)} %get-tuple-element.95), channel_id=1, source_target_pairs={{0,24},{8,16},{16,8},{24,0},{1,25},{9,17},{17,9},{25,1},{2,26},{10... | collective-permute-start | bytes 516104 | tf_op jit(solution)/shard_map/ppermute | solution.py:748
  (12 other events, 62.2 us)

commit v2 on v1

--- a/solution.py
+++ b/solution.py
@@ -14,7 +14,7 @@
 BIAS_ROWS = 16
 COST = 100
 UNROLL = 16
-LIMITS = (22, 28, 28, 18, 28, 16)
+LIMITS = (16, 20, 20, 14, 20, 14)
 ANY = pl.BlockSpec(memory_space=pl.ANY)
 HBM = pl.BlockSpec(memory_space=pltpu.HBM)
 VMEM = pl.BlockSpec(memory_space=pltpu.VMEM)
@@ -381,25 +381,28 @@
 
 
 def first_weights_kernel(first, *refs):
-    place, x, prev, dpre = refs[:4]
-    kept, sent = refs[-2:]
-    store_weight_grads(place, (x[...], prev[...]), dpre[:, first:], kept, sent)
-
-
-def store_weight_grads(place, lefts, right, kept, sent):
+    place, x, prev, dpre, bias = refs[:5]
+    store_weight_grads(place, (x[...], prev[...]), dpre[:, first:], refs[-2:], bias[:, first:])
+
+
+def store_weight_grads(place, lefts, right, outs, bias=None):
     for tap, left in enumerate(lefts):
         grads = lax.dot_general(left, right, (((0,), (0,)), ((), ())), preferred_element_type=F32).astype(BF16)
-        if sent is None:
-            kept[tap] = grads
+        if len(outs) == 1:
+            outs[0][tap] = grads
             continue
-        chips, height = kept.shape[1], kept.shape[2]
-        stream = place[1]
-        odd = stream % 2 == 1
-        for chip in range(chips):
-            even_rows = grads[2 * chip * height : (2 * chip + 1) * height]
-            odd_rows = grads[(2 * chip + 1) * height : (2 * chip + 2) * height]
-            kept[tap, chip ^ (stream // 2)] = jnp.where(odd, odd_rows, even_rows)
-            sent[tap, chip ^ (stream // 2)] = jnp.where(odd, even_rows, odd_rows)
+        kept, sent = outs
+        height = tap_rows(kept)
+        chip, odd = place[1] // 2, place[1] % 2 == 1
+        for index in range(4):
+            even_rows = grads[2 * index * height : (2 * index + 1) * height]
+            odd_rows = grads[(2 * index + 1) * height : (2 * index + 2) * height]
+            here = block_of(tap, index ^ chip, height)
+            kept[here, :] = jnp.where(odd, odd_rows, even_rows)
+            sent[here, :] = jnp.where(odd, even_rows, odd_rows)
+    if bias is not None and len(outs) > 1:
+        for out in outs:
+            out[8 * tap_rows(out) :, :] = bias_rows(bias)
 
 
 def heads_of(order, summaries, section):
@@ -487,9 +490,9 @@
     (place, candid, forget, gate, hidden, delayed, keep, cot, cot_next, keep_firsts) = refs[:10]
     summaries = refs[10:14]
     outs = refs[14:]
-    hidden_out, dpre_out, shifted_out, bias_out, last_out, kept = outs[:6]
-    sent = outs[6] if has_sent else None
-    order, cells, dcells, shifted, after = outs[7 if has_sent else 6 :]
+    hidden_out, dpre_out, shifted_out, bias_out, last_out = outs[:5]
+    grads = outs[5 : 7 if has_sent else 6]
+    order, cells, dcells, shifted, after = refs[-5:]
     section = place[0]
     width = hidden.shape[1]
     tiles = dcells.shape[0]
@@ -519,7 +522,7 @@
         rows, dcells, cells, candid, forget, gate, cot, keep, next_first, extra, shifted,
         (dpre_out, shifted_out, bias_out, after),
     )
-    store_weight_grads(place, (hidden[...], delayed[...]), dpre_out[...], kept, sent)
+    store_weight_grads(place, (hidden[...], delayed[...]), dpre_out[...], grads)
 
 
 def input_grad_tile(dpre, shifted, matrix, here):
@@ -563,8 +566,7 @@
     summaries = refs[12:16]
     order, dcells, shifted, after = refs[-4:]
     outs = refs[-9:-4] if has_sent else refs[-8:-4]
-    dpre_out, shifted_out, bias_out, kept = outs[:4]
-    sent = outs[4] if has_sent else None
+    dpre_out, shifted_out, bias_out, *grads = outs
     section = place[0]
     steps = rows // SUBS
     heads = heads_of(order, summaries, section)
@@ -580,18 +582,24 @@
         (dpre_out, shifted_out, bias_out.at[pl.ds(0, SUBS), :], after),
     )
     bias_out[SUBS:, :] = other_bias[...]
-    store_weight_grads(place, (x[...], prev[...]), dpre_out[:, : kept.shape[-1]], kept, sent)
-
-
-def last_kernel(rows, block, *refs):
-    dpre, shifted, matrix, out = refs
+    columns = slice(0, grads[0].shape[-1])
+    store_weight_grads(place, (x[...], prev[...]), dpre_out[:, columns], grads, bias_out[:, columns])
+
+
+def last_kernel(plan, block, *refs):
+    place, dpre, shifted = refs[:3]
+    near, far = weight_refs(refs[3:], plan)
+    out, matrix, weight_sems = refs[-3:]
+    weights = Weights(place, 0, near, far, matrix, weight_sems)
+    weights.start()
+    weights.wait()
 
     def part(index, carry):
         here = pl.ds(pl.multiple_of(index * block, block), block)
         out[here, :] = input_grad_tile(dpre, shifted, matrix, here)
         return carry
 
-    lax.fori_loop(0, rows // block, part, 0)
+    lax.fori_loop(0, dpre.shape[0] // block, part, 0)
 
 
 def added(*parts):
@@ -621,97 +629,100 @@
     return out
 
 
-def corner_kernel(columns, *refs):
+def tap_rows(kept):
+    return kept.shape[0] // 8 // 16 * 16
+
+
+def block_of(tap, chip, height):
+    row = (tap * 4 + chip) * height
+    return pl.ds(row if isinstance(row, int) else pl.multiple_of(row, 16), height)
+
+
+def chip_sum(kept, got, tap, chip, *more):
+    height = tap_rows(kept)
+    here = block_of(tap, chip, height)
+    return added(kept[here, :], got[here, :], *more)
+
+
+def chip_bias(kept, got):
+    height = tap_rows(kept)
+    whole = bias_of(kept[8 * height :, :]) + bias_of(got[8 * height :, :])
+    return bias_rows(jnp.concatenate([whole[0:1]] * SUBS + [whole[1:2]] * SUBS, axis=0))
+
+
+def corner_kernel(split, *refs):
     kept, got = refs[:2]
     by_x, by_y = refs[-2:]
-    height = kept.shape[2]
-    for tap, out in enumerate((by_x, by_y)):
-        out[0:height, :] = added(kept[tap, 3], got[tap, 3]).astype(BF16)
-    if columns is not None:
-        bias, got_bias = refs[2:4]
-        rows = bias_rows(bias[:, columns] + got_bias[:, columns])
-        for out in (by_x, by_y):
-            out[height:, :] = rows
-
-
-def sides_kernel(columns, *refs):
+    height = tap_rows(kept)
+    for tap, (out, chip) in enumerate(((by_x, 1), (by_y, 2))):
+        out[0:height, :] = chip_sum(kept, got, tap, 3).astype(BF16)
+        if split:
+            out[height : 2 * height, :] = chip_sum(kept, got, tap, chip).astype(BF16)
+            out[2 * height :, :] = chip_bias(kept, got)
+
+
+def sides_kernel(split, *refs):
     kept, got, from_x, from_y = refs[:4]
     by_x, by_y = refs[-2:]
-    height = kept.shape[2]
-    for tap in range(2):
-        here = pl.ds(tap * height, height)
-        parts = [kept[tap, 1], got[tap, 1]] + ([from_y[0:height, :]] if tap == 1 else [])
-        by_x[here, :] = added(*parts).astype(BF16)
-        parts = [kept[tap, 2], got[tap, 2]] + ([from_x[0:height, :]] if tap == 0 else [])
-        by_y[here, :] = added(*parts).astype(BF16)
-    if columns is not None:
-        by_x[2 * height :, :] = from_y[height:, :]
-
-
-def plane_sum(place, kept, got, from_x, from_y, tap):
-    here = pl.ds(tap * kept.shape[2], kept.shape[2])
-    return added(kept[tap, 0], got[tap, 0], from_x[here, :], from_y[here, :])
-
-
-def plane_kernel(*refs):
-    kept, got, from_x, from_y = refs[:4]
-    out = refs[-1]
-    height = kept.shape[2]
-    for tap in range(2):
-        out[pl.ds(tap * height, height), :] = plane_sum(None, kept, got, from_x, from_y, tap).astype(BF16)
-
-
-def messages_kernel(columns, *refs):
-    place, kept, got, from_x, from_y, bias, got_bias, corner_x, corner_y, second = refs[:10]
-    outs = refs[-5:-2]
-    first, order = refs[-2:]
-    height = kept.shape[2]
-    for tap in range(2):
-        first[pl.ds(tap * height, height), :] = plane_sum(None, kept, got, from_x, from_y, tap).astype(BF16)
-    parts = [
-        bias_rows(bias[:, columns] + got_bias[:, columns]),
-        corner_x[height:, :],
-        corner_y[height:, :],
-        from_x[2 * height :, :],
+    height = tap_rows(kept)
+    by_x[0:height, :] = chip_sum(kept, got, 1, 1, from_y[0:height, :]).astype(BF16)
+    by_y[0:height, :] = chip_sum(kept, got, 0, 2, from_x[0:height, :]).astype(BF16)
+    if split:
+        by_x[height:, :] = from_y[2 * height :, :]
+    else:
+        by_x[height:, :] = chip_sum(kept, got, 0, 1).astype(BF16)
+        by_y[height:, :] = chip_sum(kept, got, 1, 2).astype(BF16)
+
+
+def plane_kernel(split, *refs):
+    place, kept, got, from_x, from_y, corner_x, corner_y = refs[:7]
+    height = tap_rows(kept)
+    beside = pl.ds(height, height)
+    direct = (corner_x, corner_y) if split else (from_x, from_y)
+    sums = [
+        chip_sum(kept, got, 0, 0, direct[0][beside, :], from_y[0:height, :]),
+        chip_sum(kept, got, 1, 0, direct[1][beside, :], from_x[0:height, :]),
     ]
-    whole = sum_in_order(order, [bias_of(part) for part in parts], place[1] // 2)
+    if split:
+        mine, other, order = refs[-3:]
+        parts = [chip_bias(kept, got), corner_x[2 * height :, :], corner_y[2 * height :, :], from_x[height:, :]]
+        whole = sum_in_order(order, [bias_of(part) for part in parts], place[1] // 2)
+        whole = bias_rows(jnp.concatenate([whole[0:1]] * SUBS + [whole[1:2]] * SUBS, axis=0))
+        mine[height:, :] = whole.astype(F32)
+        other[height:, :] = whole
+    else:
+        mine, other = refs[-2:]
+    odd = place[0] % 2 == 1
+    mine[0:height, :] = jnp.where(odd, sums[1], sums[0])
+    other[0:height, :] = jnp.where(odd, sums[0], sums[1]).astype(BF16)
+
+
+def pair_kernel(*refs):
+    mine, got, *_, out = refs
+    out[...] = added(mine[...], got[...])
+
+
+def crossing_kernel(columns, *refs):
+    place, mine, got, second = refs[:4]
+    kept, out = refs[-2:]
+    height = second.shape[0]
+    sums = (added(mine[0:height, :], got[0:height, :]), second[:, columns])
+    upper = place[0] >= 2
+    kept[0:height, :] = jnp.where(upper, sums[1], sums[0])
+    out[0:height, :] = jnp.where(upper, sums[0], sums[1]).astype(BF16)
+    whole = bias_of(mine[height:, :]) + bias_of(got[height:, :])
     whole = bias_rows(jnp.concatenate([whole[0:1]] * SUBS + [whole[1:2]] * SUBS, axis=0))
-    first[2 * height :, :] = whole
-    for index, out in enumerate(outs):
-        to = place[0] ^ (index + 1)
-        row = pl.ds(pl.multiple_of((to % 2) * height, 16), height)
-
-        @pl.when(to < 2)
-        def _(out=out, row=row):
-            out[0:height, :] = first[row, :]
-
-        @pl.when(to >= 2)
-        def _(out=out, row=row):
-            out[0:height, :] = second[row, columns]
-
-        out[height:, :] = whole
+    kept[height:, :] = whole.astype(F32)
+    out[height:, :] = whole
 
 
 def whole_kernel(parts, *refs):
-    place, second = refs[:2]
-    out, bias_out, *orders = refs[-2 - len(parts) :]
-    section = place[0]
+    out, bias_out = refs[-2:]
     height = out.shape[0]
-    row = pl.ds(pl.multiple_of((section % 2) * height, 16), height)
     for index, columns in enumerate(parts):
-        first, *got = refs[2 + 4 * index : 6 + 4 * index]
-        rest = added(*[part[0:height, :] for part in got])
-
-        @pl.when(section < 2)
-        def _(first=first, rest=rest, columns=columns):
-            out[:, columns] = first[row, :].astype(F32) + rest
-
-        @pl.when(section >= 2)
-        def _(rest=rest, columns=columns):
-            out[:, columns] = second[row, columns].astype(F32) + rest
-
-        biases = [first[2 * height :, :]] + [part[height:, :] for part in got]
-        bias_out[:, columns] = sum_in_order(orders[index], [bias_of(part) for part in biases], section)
+        kept, got = refs[2 * index : 2 + 2 * index]
+        out[:, columns] = added(kept[0:height, :], got[0:height, :])
+        bias_out[:, columns] = bias_of(kept[height:, :]) + bias_of(got[height:, :])
 
 
 def call(kernel, outs, in_specs, out_specs, scratch, flops, moved, megabytes, name):
@@ -785,26 +796,29 @@
 
 
 class LayerSum:
-    def __init__(self, kept, sent, columns=None, bias=None, got_bias=None, place=None):
-        self.kept, self.got = kept, swap(sent, "dp", 1)
-        self.columns, self.bias, self.got_bias, self.place = columns, bias, got_bias, place
-        self.height, self.gates = kept.shape[2], kept.shape[3]
-        self.extra = 0 if bias is None else BIAS_ROWS
-
-    def rows(self, taps, extra):
-        return jax.ShapeDtypeStruct((taps * self.height + extra, self.gates), BF16)
+    def __init__(self, place, kept, sent):
+        self.place, self.kept, self.got = place, kept, swap(sent, "dp", 1)
+        self.height, self.gates = tap_rows(kept), kept.shape[1]
+        self.extra = kept.shape[0] - 8 * self.height
+
+    def rows(self, taps, extra, dtype=BF16):
+        return jax.ShapeDtypeStruct((taps * self.height + extra, self.gates), dtype)
 
     def corners(self, ties=()):
-        operands = [self.kept, self.got] + ([] if self.bias is None else [self.bias, self.got_bias])
         by_x, by_y = small_call(
-            functools.partial(corner_kernel, self.columns), [self.rows(1, self.extra)] * 2, operands, "corners", ties
+            functools.partial(corner_kernel, self.extra > 0),
+            [self.rows(2 if self.extra else 1, self.extra)] * 2,
+            [self.kept, self.got],
+            "corners",
+            ties,
         )
+        self.corner_sent = by_x
         self.corner_x, self.corner_y = swap(by_x, "dp", 2), swap(by_y, "dp", 4)
 
     def sides(self, ties=()):
         self.by = small_call(
-            functools.partial(sides_kernel, self.columns),
-            [self.rows(2, self.extra), self.rows(2, 0)],
+            functools.partial(sides_kernel, self.extra > 0),
+            [self.rows(1, self.extra), self.rows(1, 0)] if self.extra else [self.rows(2, 0)] * 2,
             [self.kept, self.got, self.corner_x, self.corner_y],
             "sides",
             ties,
@@ -812,22 +826,32 @@
         self.side_x, self.side_y = swap(self.by[0], "dp", 2), swap(self.by[1], "dp", 4)
 
     def plane(self, ties=()):
-        operands = [self.kept, self.got, self.side_x, self.side_y]
-        return small_call(plane_kernel, [self.rows(2, 0)], operands, "plane", ties)[0]
-
-    def messages(self, second, ties=()):
-        *sent, plane = small_call(
-            functools.partial(messages_kernel, self.columns),
-            [self.rows(1, self.extra)] * 3 + [self.rows(2, self.extra)],
-            [
-                self.place, self.kept, self.got, self.side_x, self.side_y, self.bias, self.got_bias,
-                self.corner_x, self.corner_y, second,
-            ],
-            "messages",
+        operands = [self.place, self.kept, self.got, self.side_x, self.side_y, self.corner_x, self.corner_y]
+        scratch = []
+        if self.extra > 0:
+            scratch = [pltpu.VMEM((4, 2, self.gates), F32)]
+        self.mine, other = small_call(
+            functools.partial(plane_kernel, self.extra > 0),
+            [self.rows(1, self.extra, F32), self.rows(1, self.extra)],
+            operands,
+            "plane",
             ties,
-            [pltpu.VMEM((4, 2, self.gates), F32)],
+            scratch,
         )
-        return [plane] + [swap(part, "section", index + 1) for index, part in enumerate(sent)]
+        self.near = swap(other, "section", 1)
+
+    def paired(self):
+        return small_call(pair_kernel, [self.rows(1, 0, F32)], [self.mine, self.near], "paired")[0]
+
+    def crossing(self, second, columns, ties=()):
+        self.pair, sent = small_call(
+            functools.partial(crossing_kernel, columns),
+            [self.rows(1, self.extra, F32), self.rows(1, self.extra)],
+            [self.place, self.mine, self.near, second],
+            "crossing",
+            ties,
+        )
+        self.got_pair = swap(sent, "section", 2)
 
 
 def all_sums(value):
@@ -914,12 +938,12 @@
     def exchanged(summary):
         return [summary] + [swap(summary, "section", index) for index in range(1, sections)]
 
-    candid0, forget0, gate0, summary, matrix0 = call(
+    candid0, forget0, gate0, summary = call(
         functools.partial(first_forward_kernel, plan, block),
-        [full] * 3 + [shape(8, width), matrix],
+        [full] * 3 + [shape(8, width)],
         [SMEM] + [VMEM] * 4 + [HBM] * len(weights),
-        [VMEM] * 5,
-        [dma((weight_count + 1,))],
+        [VMEM] * 4,
+        [buffer(2 * width, gates, dtype=BF16), dma((weight_count + 1,))],
         layer_flops,
         weight_bytes + 30 * rows * width,
         LIMITS[0],
@@ -946,7 +970,11 @@
     )(place, candid0, forget0, gate0, keep_own, cot, bias[1:2], *exchanged(summary), *weights)
 
     if quick:
-        kept_shape = [shape(2, 4, height, gates, dtype=BF16)] * 2
+
+        def kept_and_sent(columns, extra):
+            return [shape(8 * height + extra, columns, dtype=BF16)] * 2
+
+        kept_shape = kept_and_sent(gates, 0)
     else:
         kept_shape = [shape(2, width, gates, dtype=BF16)]
     wide = shape(rows, gates, dtype=BF16)
@@ -966,10 +994,6 @@
         *exchanged(summary1),
     )
 
-    if quick:
-        second = LayerSum(*kept1)
-        second.corners()
-
     arriving, summary0 = call(
         functools.partial(middle_kernel, rows, block),
         [half, shape(8, width)],
@@ -982,13 +1006,16 @@
         "middle",
     )(place, dpre1, shifted1, candid0, forget0, gate0, keep_own, matrix1)
 
+    summaries = exchanged(summary0)
     ties = []
     first_shape, first_columns = kept_shape, gates
     if quick:
-        second.sides()
+        second = LayerSum(place, *kept1)
+        second.corners(ties=[arriving])
+        second.sides(ties=summaries[1:])
         ties = second.by
-        first_columns = gates // LANES // 2 * LANES
-        first_shape = [shape(2, 4, height, first_columns, dtype=BF16)] * 2
+        first_columns = gates // LANES * 3 // 5 * LANES
+        first_shape = kept_and_sent(first_columns, BIAS_ROWS)
     dpre0, shifted0, bias_both, *kept0 = call(
         functools.partial(first_backward_kernel, rows, quick),
         [wide, wide, shape(2 * SUBS, gates)] + first_shape,
@@ -1001,48 +1028,47 @@
         "first_backward",
     )(
         place, candid0, forget0, gate0, cells0, last0, x, prev, keep_own, arriving, keep_firsts, bias1,
-        *exchanged(summary0), *ties,
+        *summaries, *ties,
     )
     if quick:
-        later_shape = shape(2, 4, height, gates - first_columns, dtype=BF16)
         later = small_call(
             functools.partial(first_weights_kernel, first_columns),
-            [later_shape] * 2,
-            [place, x, prev, dpre0],
+            kept_and_sent(gates - first_columns, BIAS_ROWS),
+            [place, x, prev, dpre0, bias_both],
             "first_weights",
         )
-        plane1 = second.plane()
+        parts = [slice(0, first_columns), slice(first_columns, gates)]
+        sums = [LayerSum(place, *pieces) for pieces in (kept0, later)]
+        sums[0].corners()
+        ties = [sums[0].corner_sent]
 
     input_grad = call(
-        functools.partial(last_kernel, rows, block),
+        functools.partial(last_kernel, plan, block),
         shape(rows, width),
-        [VMEM] * 3,
+        [SMEM] + [VMEM] * 2 + [HBM] * len(weights) + [ANY] * len(ties),
         VMEM,
-        [],
-        layer_flops,
-        weight_bytes + 20 * rows * width,
+        [buffer(2 * width, gates, dtype=BF16), dma((weight_count + 1,))],
+        COST * layer_flops,
+        COST * weight_bytes,
         LIMITS[5],
         "last",
-    )(dpre0, shifted0, matrix0)
+    )(place, dpre0, shifted0, *weights, *ties)
 
     if quick:
-        got_bias = swap(bias_both, "dp", 1)
-        parts = [slice(0, first_columns), slice(first_columns, gates)]
-        sums = [
-            LayerSum(*pieces, columns, bias_both, got_bias, place)
-            for pieces, columns in zip((kept0, later), parts, strict=True)
-        ]
-        sums[0].corners()
-        sums[1].corners(ties=[input_grad])
-        sums[0].sides(ties=[plane1])
-        sums[1].sides(ties=sums[0].by)
-        got = [part.messages(plane1) for part in sums]
+        second.plane(ties=[input_grad])
+        sums[1].corners(ties=[second.mine])
+        sums[0].sides(ties=[sums[1].corner_sent])
+        pair = second.paired()
+        sums[0].plane()
+        sums[1].sides(ties=[sums[0].mine])
+        sums[0].crossing(pair, parts[0])
+        sums[1].plane(ties=[sums[0].pair])
+        sums[1].crossing(pair, parts[1], ties=[sums[0].got_pair])
         weight_grad, bias_grad = small_call(
             functools.partial(whole_kernel, parts),
             [shape(height, gates), shape(2, gates)],
-            [place, plane1] + got[0] + got[1],
+            [value for part in sums for value in (part.pair, part.got_pair)],
             "whole",
-            scratch=[buffer(4, 2, columns.stop - columns.start) for columns in parts],
         )
         weight_grad = weight_grad[None]
     else:

time: 205 us -> 184 us (0.90)
  waiting for transfers between devices: 95 us -> 76.9 us
  local copies, waits for them, and re-layouts: 10.9 us -> 5.65 us
  Pallas kernels: 45.9 us -> 49.5 us
    ppermute x44 -> x42, waiting for transfers between devices: 73.8 us -> 55.7 us  [swap(): return lax.ppermute(value, axis, pairs)]
    unnamed x20 -> x6, local copies, waits for them, and re-layouts: 5.25 us -> 0.01 us
    ppermute x44 -> x42, starting transfers between devices: 43.2 us -> 41.9 us  [swap(): return lax.ppermute(value, axis, pairs)]
    pallas_call x18 -> x21, Pallas kernels: 11.3 us -> 12.5 us  [small_call(): call(kernel, outs, specs + [ANY] * len(ties), [VMEM] * len(outs), list(sc...]
  transfers between devices with their start and end apart: 50 -> 48, of which waited for: 28 -> 27; matrix products, arithmetic and copies ran while one was open for 3% -> 3% of each run, Pallas kernels for 8% -> 11%
where the time goes in v2:
time: 184 us
  waiting for transfers between devices  76.9 us (42%)
  starting transfers between devices  50.4 us (27%)
  Pallas kernels  49.5 us (27%)
  local copies, waits for them, and re-layouts  5.65 us (3%)
    ppermute x42, waiting for transfers between devices, swap(): return lax.ppermute(value, axis, pairs)  55.7 us
    ppermute x42, starting transfers between devices, swap(): return lax.ppermute(value, axis, pairs)  41.9 us
    ppermute x6, waiting for transfers between devices, moved(): lax.ppermute(value, axis, [(index, target(index)) for index in range(lax....  21.2 us
    pallas_call x21, Pallas kernels, small_call(): call(kernel, outs, specs + [ANY] * len(ties), [VMEM] * len(outs), list(sc...  12.5 us
    ppermute x6, starting transfers between devices, moved(): lax.ppermute(value, axis, [(index, target(index)) for index in range(lax....  8.53 us
    pallas_call x1, Pallas kernels, per_device(): call(functools.partial(second_forward_kernel, plan, block), [shape(tiles,...  7.59 us
    pallas_call x1, Pallas kernels, per_device(): call(functools.partial(second_backward_kernel, rows, quick), [half, wide,...  7.3 us
    pallas_call x1, Pallas kernels, per_device(): call(functools.partial(first_forward_kernel, plan, block), [full] * 3 + [...  6.04 us
  transfers between devices with their start and end apart: 48, of which 27 were waited for; matrix products, arithmetic and copies ran while one was open for 3% of the time, Pallas kernels for 11%

profile of v2, /device:TPU:0, one launch (start us, length us, event | category | flops | bytes accessed | tf_op | source)
XLA Modules:
  0.0 183.6 jit_solution(10416616597950432921)
XLA Ops:
  0.7 4.1 %collective-permute-start.9 = (bf16[80,1920]{1,0:T(8,128)(2,1)}, bf16[80,1920]{1,0:T(8,128)(2,1)S(1)}, u32[]{:S(2)}, u32[]{:S(2)}) collective-permute-start(bf16[80,1920]{1,0:T(8,128)(2,1)} %bitcast.47), channel_id=1, source_target_pairs={{0,16},{8,24},{16,0},{24,8},{1,17},{9,25},{17,1},{25,9},{2,18},{10... | collective-permute-start | bytes 921608 | tf_op jit(solution)/shard_map/ppermute | solution.py:759
  4.8 1.6 collective-permute-start.3
  6.4 1.4 constant_dynamic-slice_fusion
  8.7 1.4 collective-permute-start.1
  12.0 7.1 %collective-permute-done.3.own = bf16[80,1920]{1,0:T(8,128)(2,1)S(1)} collective-permute-done((bf16[80,1920]{1,0:T(8,128)(2,1)}, bf16[80,1920]{1,0:T(8,128)(2,1)S(1)}, u32[]{:S(2)}, u32[]{:S(2)}) %collective-permute-start.3) | collective-permute-done | bytes 307232 | tf_op jit(solution)/shard_map/ppermute | solution.py:759
  20.2 1.6 collective-permute-start.13
  22.3 1.4 collective-permute-start.5
  24.0 5.9 %collective-permute-done.13.own = bf16[80,1920]{1,0:T(8,128)(2,1)S(1)} collective-permute-done((bf16[80,1920]{1,0:T(8,128)(2,1)S(1)}, bf16[80,1920]{1,0:T(8,128)(2,1)S(1)}, u32[]{:S(2)}, u32[]{:S(2)}) %collective-permute-start.13) | collective-permute-done | bytes 307232 | tf_op jit(solution)/shard_map/ppermute | solution.py:759
  30.5 1.7 collective-permute-start.11
  35.1 1.3 collective-permute-start.7
  36.4 3.7 %collective-permute-done.11.first.refs_14_.refs_20_.refs_12_ = bf16[160,1920]{1,0:T(8,128)(2,1)S(1)} collective-permute-done((bf16[160,1920]{1,0:T(8,128)(2,1)S(1)}, bf16[160,1920]{1,0:T(8,128)(2,1)S(1)}, u32[]{:S(2)}, u32[]{:S(2)}) %collective-permute-start.11) | collective-permute-done | bytes 614432 | tf_op jit(solution)/shard_map/ppermute | solution.py:763
  40.1 6.6 %collective-permute-done.15.second.refs_17_.refs_23_.refs_15_ = bf16[160,1920]{1,0:T(8,128)(2,1)S(1)} collective-permute-done((bf16[160,1920]{1,0:T(8,128)(2,1)S(1)}, bf16[160,1920]{1,0:T(8,128)(2,1)S(1)}, u32[]{:S(2)}, u32[]{:S(2)}) %collective-permute-start.15) | collective-permute-done | bytes 614432 | tf_op jit(solution)/shard_map/ppermute | solution.py:763
  47.3 1.6 collective-permute-start.17
  49.7 4.3 %collective-permute-done.7.refs_11_.refs_17_.refs_9_ = bf16[160,1920]{1,0:T(8,128)(2,1)S(1)} collective-permute-done((bf16[160,1920]{1,0:T(8,128)(2,1)S(1)}, bf16[160,1920]{1,0:T(8,128)(2,1)S(1)}, u32[]{:S(2)}, u32[]{:S(2)}) %collective-permute-start.7) | collective-permute-done | bytes 614432 | tf_op jit(solution)/shard_map/ppermute | solution.py:763
  54.0 6.6 %collective-permute-done.17.refs_19_.refs_25_.refs_17_ = bf16[160,1920]{1,0:T(8,128)(2,1)S(1)} collective-permute-done((bf16[160,1920]{1,0:T(8,128)(2,1)S(1)}, bf16[160,1920]{1,0:T(8,128)(2,1)S(1)}, u32[]{:S(2)}, u32[]{:S(2)}) %collective-permute-start.17) | collective-permute-done | bytes 614432 | tf_op jit(solution)/shard_map/ppermute | solution.py:763
  60.6 2.0 %collective-permute-done.18.refs_20_.refs_26_.refs_18_ = bf16[160,1920]{1,0:T(8,128)(2,1)S(1)} collective-permute-done((bf16[160,1920]{1,0:T(8,128)(2,1)S(1)}, bf16[160,1920]{1,0:T(8,128)(2,1)S(1)}, u32[]{:S(2)}, u32[]{:S(2)}) %collective-permute-start.18) | collective-permute-done | bytes 614432 | tf_op jit(solution)/shard_map/ppermute | solution.py:759
  62.6 6.0 %first_forward.1 = (f32[5,512,128]{2,1,0:T(8,128)S(1)}, f32[5,512,128]{2,1,0:T(8,128)S(1)}, f32[5,512,128]{2,1,0:T(8,128)S(1)}, f32[8,640]{1,0:T(8,128)S(1)}) custom-call(s32[2]{0:T(128)S(1)} %pad_add_fusion.refs_0_.place, bf16[512,640]{1,0:T(8,128)(2,1)S(1)} %bitcast.39, bf16[512,640]{1,0:T(8,128)(2,1)S(1)} %before.1.refs_1_.refs_2_.refs_7_, ...), custom_call_target="tpu_custom_call" | custom-call | flops 25165824 | bytes 147456 | tf_op jit(solution)/shard_map/first_forward/pallas_call | solution.py:941
  68.7 1.7 collective-permute-start.21
  70.4 1.3 collective-permute-start.20
  71.7 1.4 collective-permute-start.19
  73.1 1.3 collective-permute-done.21.refs_10_
  75.5 7.6 %second_forward.1 = (f32[5,520,128]{2,1,0:T(8,128)S(1)}, bf16[512,640]{1,0:T(8,128)(2,1)S(1)}, bf16[512,640]{1,0:T(8,128)(2,1)S(1)}, f32[8,640]{1,0:T(8,128)S(1)...) custom-call(s32[2]{0:T(128)S(1)} %pad_add_fusion.refs_0_.place, ...), custom_call_target="tpu_custom_call" | custom-call | flops 25165824 | bytes 114688 | tf_op jit(solution)/shard_map/second_forward/pallas_call | solution.py:953
  83.1 1.9 %collective-permute-start.24 = (f32[16,640]{1,0:T(8,128)S(1)}, f32[16,640]{1,0:T(8,128)S(1)}, u32[]{:S(2)}, u32[]{:S(2)}) collective-permute-start(f32[16,640]{1,0:T(8,128)S(1)} %get-tuple-element.67.refs_10_), channel_id=1, source_target_pairs={{0,24},{8,16},{16,8},{24,0},{1,25},{9,17},{17,9},{25,1},{2,26},{10... | collective-permute-start | bytes 122888 | tf_op jit(solution)/shard_map/ppermute | solution.py:759
  86.0 1.5 collective-permute-start.22
  87.5 1.5 collective-permute-done.24.refs_13_
  90.4 7.3 %second_backward.1 = (bf16[512,640]{1,0:T(8,128)(2,1)S(1)}, bf16[512,1920]{1,0:T(8,128)(2,1)S(1)}, bf16[512,1920]{1,0:T(8,128)(2,1)S(1)}, f32[8,1920]{1,0:T(8,12...) custom-call(s32[2]{0:T(128)S(1)} %pad_add_fusion.refs_0_.place, ...), custom_call_target="tpu_custom_call" | custom-call | flops 25165824 | bytes 147456 | tf_op jit(solution)/shard_map/second_backward/pallas_call | solution.py:982
  97.8 4.6 %middle.1 = (bf16[512,640]{1,0:T(8,128)(2,1)S(1)}, f32[8,640]{1,0:T(8,128)S(1)}) custom-call(s32[2]{0:T(128)S(1)} %pad_add_fusion.refs_0_.place, bf16[512,1920]{1,0:T(8,128)(2,1)S(1)} %get-tuple-element.71.refs_1_, bf16[512,1920]{1,0:T(8,128)(2,1)S(1)} %get-tuple-element.72.refs_2_, f32[5,512,128]{2,1,0:T(8,128)S(1)} %get-tuple-element.58.refs_1_.refs_3_, ...), custom_call_target="tpu_custom_call" | custom-call | flops 25165824 | bytes 114688 | tf_op jit(solution)/shard_map/middle/pallas_call | solution.py:997
  102.6 1.6 collective-permute-start.29
  104.2 1.5 collective-permute-start.30
  105.7 1.9 %collective-permute-start.27 = (f32[8,640]{1,0:T(8,128)S(1)}, f32[8,640]{1,0:T(8,128)S(1)}, u32[]{:S(2)}, u32[]{:S(2)}) collective-permute-start(f32[8,640]{1,0:T(8,128)S(1)} %get-tuple-element.76.refs_12_), channel_id=1, source_target_pairs={{0,24},{8,16},{16,8},{24,0},{1,25},{9,17},{17,9},{25,1},{2,26},{10... | collective-permute-start | bytes 61448 | tf_op jit(solution)/shard_map/ppermute | solution.py:759
  108.2 1.8 collective-permute-start.25
  112.3 1.2 collective-permute-done.30.refs_3_.refs_6_
  113.9 5.8 %first_backward.1 = (bf16[512,1920]{1,0:T(8,128)(2,1)S(1)}, bf16[512,1920]{1,0:T(8,128)(2,1)S(1)}, f32[16,1920]{1,0:T(8,128)S(1)}, bf16[656,1152]{1,0:T(8,128)(2,1)S(1)}, bf16[656,1152]{1,0:T(8,128)(2,1)S(1)}) custom-call(s32[2]{0:T(128)S(1)} %pad_add_fusion.refs_0_.place, f32[5,512,128]{2,1,0:T(8,128)S(1)} %get-tuple-element.58.refs_1_.refs_3_, ...), custom_call_target="tpu_custom_call" | custom-call | flops 25165824 | bytes 147456 | tf_op jit(solution)/shard_map/first_backward/pallas_call | solution.py:1019
  119.8 1.8 first_weights.1
  122.7 1.5 collective-permute-start.36
  125.1 1.5 collective-permute-start.32
  126.6 5.7 %last.1.refs_7_ = f32[512,640]{1,0:T(8,128)S(1)} custom-call(s32[2]{0:T(128)S(1)} %pad_add_fusion.refs_0_.place, bf16[512,1920]{1,0:T(8,128)(2,1)S(1)} %get-tuple-element.83.refs_1_.refs_3_, bf16[512,1920]{1,0:T(8,128)(2,1)S(1)} %get-tuple-element.84.refs_2_, bf16[160,1920]{1,0:T(8,128)(2,1)S(1)} %join.4.refs_5_.refs_11_.refs_3_, ...), custom_call_target="tpu_custom_call" | custom-call | flops 2516582400 | bytes 4915200 | tf_op jit(solution)/shard_map/last/pallas_call | solution.py:1045
  132.3 6.6 %collective-permute-done.35.refs_3_ = bf16[160,1920]{1,0:T(8,128)(2,1)S(1)} collective-permute-done((bf16[160,1920]{1,0:T(8,128)(2,1)S(1)}, bf16[160,1920]{1,0:T(8,128)(2,1)S(1)}, u32[]{:S(2)}, u32[]{:S(2)}) %collective-permute-start.35) | collective-permute-done | bytes 614432 | tf_op jit(solution)/shard_map/ppermute | solution.py:759
  140.5 6.4 %collective-permute-done.33.refs_3_.refs_6_ = bf16[176,1152]{1,0:T(8,128)(2,1)S(1)} collective-permute-done((bf16[176,1152]{1,0:T(8,128)(2,1)S(1)}, bf16[176,1152]{1,0:T(8,128)(2,1)S(1)}, u32[]{:S(2)}, u32[]{:S(2)}) %collective-permute-start.33) | collective-permute-done | bytes 405536 | tf_op jit(solution)/shard_map/ppermute | solution.py:759
  147.1 1.6 collective-permute-start.37
  148.7 1.5 collective-permute-start.38
  152.3 3.9 %collective-permute-done.38.refs_4_ = bf16[80,1152]{1,0:T(8,128)(2,1)S(1)} collective-permute-done((bf16[80,1152]{1,0:T(8,128)(2,1)S(1)}, bf16[80,1152]{1,0:T(8,128)(2,1)S(1)}, u32[]{:S(2)}, u32[]{:S(2)}) %collective-permute-start.38) | collective-permute-done | bytes 184352 | tf_op jit(solution)/shard_map/ppermute | solution.py:759
  158.4 1.2 collective-permute-done.43.refs_3_.refs_6_
  160.9 1.5 collective-permute-start.45
  163.9 1.6 collective-permute-start.41
  167.8 6.5 %collective-permute-done.46.refs_2_ = bf16[96,768]{1,0:T(8,128)(2,1)S(1)} collective-permute-done((bf16[96,768]{1,0:T(8,128)(2,1)S(1)}, bf16[96,768]{1,0:T(8,128)(2,1)S(1)}, u32[]{:S(2)}, u32[]{:S(2)}) %collective-permute-start.46) | collective-permute-done | bytes 147488 | tf_op jit(solution)/shard_map/ppermute | solution.py:759
  176.0 1.3 copy.16
  177.3 5.4 %collective-permute-done.47.refs_3_ = bf16[96,768]{1,0:T(8,128)(2,1)S(1)} collective-permute-done((bf16[96,768]{1,0:T(8,128)(2,1)S(1)}, bf16[96,768]{1,0:T(8,128)(2,1)S(1)}, u32[]{:S(2)}, u32[]{:S(2)}) %collective-permute-start.47) | collective-permute-done | bytes 147488 | tf_op jit(solution)/shard_map/ppermute | solution.py:759
  (99 shorter events, 32.3 us)
Async XLA Ops:
  0.7 19.5 %collective-permute-start.9 = (bf16[80,1920]{1,0:T(8,128)(2,1)}, bf16[80,1920]{1,0:T(8,128)(2,1)S(1)}, u32[]{:S(2)}, u32[]{:S(2)}) collective-permute-start(bf16[80,1920]{1,0:T(8,128)(2,1)} %bitcast.47), channel_id=1, source_target_pairs={{0,16},{8,24},{16,0},{24,8},{1,17},{9,25},{17,1},{25,9},{2,18},{10... | collective-permute-start | bytes 921608 | tf_op jit(solution)/shard_map/ppermute | solution.py:759
  4.8 14.4 %collective-permute-start.3 = (bf16[80,1920]{1,0:T(8,128)(2,1)}, bf16[80,1920]{1,0:T(8,128)(2,1)S(1)}, u32[]{:S(2)}, u32[]{:S(2)}) collective-permute-start(bf16[80,1920]{1,0:T(8,128)(2,1)} %bitcast.48), channel_id=1, source_target_pairs={{0,8},{8,0},{16,24},{24,16},{1,9},{9,1},{17,25},{25,17},{2,10},{10... | collective-permute-start | bytes 921608 | tf_op jit(solution)/shard_map/ppermute | solution.py:759
  6.3 1.8 collective-permute-start
  8.7 13.0 %collective-permute-start.1 = (bf16[160,1920]{1,0:T(8,128)(2,1)S(1)}, bf16[160,1920]{1,0:T(8,128)(2,1)S(1)}, u32[]{:S(2)}, u32[]{:S(2)}) collective-permute-start(bf16[160,1920]{1,0:T(8,128)(2,1)S(1)} %join.4.refs_5_.refs_11_.refs_3_), channel_id=1, source_target_pairs={{0,3},{1,4},{2,1},{3,6},{4,7},{5,0},{6,5},{7,2},{8,11},{9,12},{10,... | collective-permute-start | bytes 1843208 | tf_op jit(solution)/shard_map/ppermute | solution.py:763
  19.1 2.6 %collective-permute-start.4 = (bf16[80,1920]{1,0:T(8,128)(2,1)S(1)}, bf16[80,1920]{1,0:T(8,128)(2,1)S(1)}, u32[]{:S(2)}, u32[]{:S(2)}) collective-permute-start(bf16[80,1920]{1,0:T(8,128)(2,1)S(1)} %collective-permute-done.3.own), channel_id=1, source_target_pairs={{0,1},{1,0},{2,3},{3,2},{4,5},{5,4},{6,7},{7,6},{8,9},{9,8},{10,11... | collective-permute-start | bytes 921608 | tf_op jit(solution)/shard_map/ppermute | solution.py:759
  20.2 9.7 %collective-permute-start.13 = (bf16[80,1920]{1,0:T(8,128)(2,1)S(1)}, bf16[80,1920]{1,0:T(8,128)(2,1)S(1)}, u32[]{:S(2)}, u32[]{:S(2)}) collective-permute-start(bf16[80,1920]{1,0:T(8,128)(2,1)S(1)} %collective-permute-done.9.own), channel_id=1, source_target_pairs={{0,8},{8,0},{16,24},{24,16},{1,9},{9,1},{17,25},{25,17},{2,10},{10... | collective-permute-start | bytes 921608 | tf_op jit(solution)/shard_map/ppermute | solution.py:759
  22.3 9.9 %collective-permute-start.5 = (bf16[160,1920]{1,0:T(8,128)(2,1)S(1)}, bf16[160,1920]{1,0:T(8,128)(2,1)S(1)}, u32[]{:S(2)}, u32[]{:S(2)}) collective-permute-start(bf16[160,1920]{1,0:T(8,128)(2,1)S(1)} %join.5.refs_8_.refs_14_.refs_6_), channel_id=1, source_target_pairs={{0,3},{1,4},{2,1},{3,6},{4,7},{5,0},{6,5},{7,2},{8,11},{9,12},{10,... | collective-permute-start | bytes 1843208 | tf_op jit(solution)/shard_map/ppermute | solution.py:763
  23.7 6.2 %collective-permute-start.10 = (bf16[80,1920]{1,0:T(8,128)(2,1)S(1)}, bf16[80,1920]{1,0:T(8,128)(2,1)S(1)}, u32[]{:S(2)}, u32[]{:S(2)}) collective-permute-start(bf16[80,1920]{1,0:T(8,128)(2,1)S(1)} %collective-permute-done.9.own), channel_id=1, source_target_pairs={{0,1},{1,0},{2,3},{3,2},{4,5},{5,4},{6,7},{7,6},{8,9},{9,8},{10,11... | collective-permute-start | bytes 921608 | tf_op jit(solution)/shard_map/ppermute | solution.py:759
  29.9 2.3 %collective-permute-start.14 = (bf16[80,1920]{1,0:T(8,128)(2,1)S(1)}, bf16[80,1920]{1,0:T(8,128)(2,1)S(1)}, u32[]{:S(2)}, u32[]{:S(2)}) collective-permute-start(bf16[80,1920]{1,0:T(8,128)(2,1)S(1)} %collective-permute-done.13.own), channel_id=1, source_target_pairs={{0,1},{1,0},{2,3},{3,2},{4,5},{5,4},{6,7},{7,6},{8,9},{9,8},{10,11... | collective-permute-start | bytes 921608 | tf_op jit(solution)/shard_map/ppermute | solution.py:759
  30.5 9.6 %collective-permute-start.11 = (bf16[160,1920]{1,0:T(8,128)(2,1)S(1)}, bf16[160,1920]{1,0:T(8,128)(2,1)S(1)}, u32[]{:S(2)}, u32[]{:S(2)}) collective-permute-start(bf16[160,1920]{1,0:T(8,128)(2,1)S(1)} %join.6.refs_13_.refs_19_.refs_11_), channel_id=1, source_target_pairs={{0,3},{1,4},{2,1},{3,6},{4,7},{5,0},{6,5},{7,2},{8,11},{9,12},{10,... | collective-permute-start | bytes 1843208 | tf_op jit(solution)/shard_map/ppermute | solution.py:763
  32.8 13.9 %collective-permute-start.15 = (bf16[160,1920]{1,0:T(8,128)(2,1)S(1)}, bf16[160,1920]{1,0:T(8,128)(2,1)S(1)}, u32[]{:S(2)}, u32[]{:S(2)}) collective-permute-start(bf16[160,1920]{1,0:T(8,128)(2,1)S(1)} %join.7.refs_16_.refs_22_.refs_14_), channel_id=1, source_target_pairs={{0,3},{1,4},{2,1},{3,6},{4,7},{5,0},{6,5},{7,2},{8,11},{9,12},{10,... | collective-permute-start | bytes 1843208 | tf_op jit(solution)/shard_map/ppermute | solution.py:763
  34.0 15.4 %collective-permute-start.2 = (bf16[160,1920]{1,0:T(8,128)(2,1)S(1)}, bf16[160,1920]{1,0:T(8,128)(2,1)S(1)}, u32[]{:S(2)}, u32[]{:S(2)}) collective-permute-start(bf16[160,1920]{1,0:T(8,128)(2,1)S(1)} %collective-permute-done.1.refs_0_.first.refs_6_.refs_12_.refs_4_), channel_id=1, source_target_pairs={{0,1},{1,0},{2,3},{3,2},{4,5},{5,4},{6,7},{7,6},{8,9},{9,8},{10,11... | collective-permute-start | bytes 1843208 | tf_op jit(solution)/shard_map/ppermute | solution.py:759
  35.1 18.9 %collective-permute-start.7 = (bf16[160,1920]{1,0:T(8,128)(2,1)S(1)}, bf16[160,1920]{1,0:T(8,128)(2,1)S(1)}, u32[]{:S(2)}, u32[]{:S(2)}) collective-permute-start(bf16[160,1920]{1,0:T(8,128)(2,1)S(1)} %pick.2), channel_id=1, source_target_pairs={{0,2},{1,5},{2,0},{3,7},{4,6},{5,1},{6,4},{7,3},{8,10},{9,13},{10,... | collective-permute-start | bytes 1843208 | tf_op jit(solution)/shard_map/ppermute | solution.py:763
  47.3 13.2 %collective-permute-start.17 = (bf16[160,1920]{1,0:T(8,128)(2,1)S(1)}, bf16[160,1920]{1,0:T(8,128)(2,1)S(1)}, u32[]{:S(2)}, u32[]{:S(2)}) collective-permute-start(bf16[160,1920]{1,0:T(8,128)(2,1)S(1)} %pick.3), channel_id=1, source_target_pairs={{0,2},{1,5},{2,0},{3,7},{4,6},{5,1},{6,4},{7,3},{8,10},{9,13},{10,... | collective-permute-start | bytes 1843208 | tf_op jit(solution)/shard_map/ppermute | solution.py:763
  48.9 11.7 %collective-permute-start.12 = (bf16[160,1920]{1,0:T(8,128)(2,1)S(1)}, bf16[160,1920]{1,0:T(8,128)(2,1)S(1)}, u32[]{:S(2)}, u32[]{:S(2)}) collective-permute-start(bf16[160,1920]{1,0:T(8,128)(2,1)S(1)} %collective-permute-done.11.first.refs_14_.refs_20_.refs_12_), channel_id=1, source_target_pairs={{0,1},{1,0},{2,3},{3,2},{4,5},{5,4},{6,7},{7,6},{8,9},{9,8},{10,11... | collective-permute-start | bytes 1843208 | tf_op jit(solution)/shard_map/ppermute | solution.py:759
  49.2 11.4 %collective-permute-start.6 = (bf16[160,1920]{1,0:T(8,128)(2,1)S(1)}, bf16[160,1920]{1,0:T(8,128)(2,1)S(1)}, u32[]{:S(2)}, u32[]{:S(2)}) collective-permute-start(bf16[160,1920]{1,0:T(8,128)(2,1)S(1)} %collective-permute-done.5.second.refs_0_.refs_9_.refs_15_.refs_7_), channel_id=1, source_target_pairs={{0,1},{1,0},{2,3},{3,2},{4,5},{5,4},{6,7},{7,6},{8,9},{9,8},{10,11... | collective-permute-start | bytes 1843208 | tf_op jit(solution)/shard_map/ppermute | solution.py:759
  49.5 11.2 %collective-permute-start.16 = (bf16[160,1920]{1,0:T(8,128)(2,1)S(1)}, bf16[160,1920]{1,0:T(8,128)(2,1)S(1)}, u32[]{:S(2)}, u32[]{:S(2)}) collective-permute-start(bf16[160,1920]{1,0:T(8,128)(2,1)S(1)} %collective-permute-done.15.second.refs_17_.refs_23_.refs_15_), channel_id=1, source_target_pairs={{0,1},{1,0},{2,3},{3,2},{4,5},{5,4},{6,7},{7,6},{8,9},{9,8},{10,11... | collective-permute-start | bytes 1843208 | tf_op jit(solution)/shard_map/ppermute | solution.py:759
  54.0 6.6 %collective-permute-start.8 = (bf16[160,1920]{1,0:T(8,128)(2,1)S(1)}, bf16[160,1920]{1,0:T(8,128)(2,1)S(1)}, u32[]{:S(2)}, u32[]{:S(2)}) collective-permute-start(bf16[160,1920]{1,0:T(8,128)(2,1)S(1)} %collective-permute-done.7.refs_11_.refs_17_.refs_9_), channel_id=1, source_target_pairs={{0,1},{1,0},{2,3},{3,2},{4,5},{5,4},{6,7},{7,6},{8,9},{9,8},{10,11... | collective-permute-start | bytes 1843208 | tf_op jit(solution)/shard_map/ppermute | solution.py:759
  60.6 2.0 %collective-permute-start.18 = (bf16[160,1920]{1,0:T(8,128)(2,1)S(1)}, bf16[160,1920]{1,0:T(8,128)(2,1)S(1)}, u32[]{:S(2)}, u32[]{:S(2)}) collective-permute-start(bf16[160,1920]{1,0:T(8,128)(2,1)S(1)} %collective-permute-done.17.refs_19_.refs_25_.refs_17_), channel_id=1, source_target_pairs={{0,1},{1,0},{2,3},{3,2},{4,5},{5,4},{6,7},{7,6},{8,9},{9,8},{10,11... | collective-permute-start | bytes 1843208 | tf_op jit(solution)/shard_map/ppermute | solution.py:759
  68.7 5.8 %collective-permute-start.21 = (f32[8,640]{1,0:T(8,128)S(1)}, f32[8,640]{1,0:T(8,128)S(1)}, u32[]{:S(2)}, u32[]{:S(2)}) collective-permute-start(f32[8,640]{1,0:T(8,128)S(1)} %get-tuple-element.61.refs_7_), channel_id=1, source_target_pairs={{0,24},{8,16},{16,8},{24,0},{1,25},{9,17},{17,9},{25,1},{2,26},{10... | collective-permute-start | bytes 61448 | tf_op jit(solution)/shard_map/ppermute | solution.py:759
  70.4 4.7 %collective-permute-start.20 = (f32[8,640]{1,0:T(8,128)S(1)}, f32[8,640]{1,0:T(8,128)S(1)}, u32[]{:S(2)}, u32[]{:S(2)}) collective-permute-start(f32[8,640]{1,0:T(8,128)S(1)} %get-tuple-element.61.refs_7_), channel_id=1, source_target_pairs={{0,16},{8,24},{16,0},{24,8},{1,17},{9,25},{17,1},{25,9},{2,18},{10... | collective-permute-start | bytes 61448 | tf_op jit(solution)/shard_map/ppermute | solution.py:759
  71.7 3.8 %collective-permute-start.19 = (f32[8,640]{1,0:T(8,128)S(1)}, f32[8,640]{1,0:T(8,128)S(1)}, u32[]{:S(2)}, u32[]{:S(2)}) collective-permute-start(f32[8,640]{1,0:T(8,128)S(1)} %get-tuple-element.61.refs_7_), channel_id=1, source_target_pairs={{0,8},{8,0},{16,24},{24,16},{1,9},{9,1},{17,25},{25,17},{2,10},{10... | collective-permute-start | bytes 61448 | tf_op jit(solution)/shard_map/ppermute | solution.py:759
  83.1 6.0 %collective-permute-start.24 = (f32[16,640]{1,0:T(8,128)S(1)}, f32[16,640]{1,0:T(8,128)S(1)}, u32[]{:S(2)}, u32[]{:S(2)}) collective-permute-start(f32[16,640]{1,0:T(8,128)S(1)} %get-tuple-element.67.refs_10_), channel_id=1, source_target_pairs={{0,24},{8,16},{16,8},{24,0},{1,25},{9,17},{17,9},{25,1},{2,26},{10... | collective-permute-start | bytes 122888 | tf_op jit(solution)/shard_map/ppermute | solution.py:759
  85.0 5.0 %collective-permute-start.23 = (f32[16,640]{1,0:T(8,128)S(1)}, f32[16,640]{1,0:T(8,128)S(1)}, u32[]{:S(2)}, u32[]{:S(2)}) collective-permute-start(f32[16,640]{1,0:T(8,128)S(1)} %get-tuple-element.67.refs_10_), channel_id=1, source_target_pairs={{0,16},{8,24},{16,0},{24,8},{1,17},{9,25},{17,1},{25,9},{2,18},{10... | collective-permute-start | bytes 122888 | tf_op jit(solution)/shard_map/ppermute | solution.py:759
  86.0 4.4 %collective-permute-start.22 = (f32[16,640]{1,0:T(8,128)S(1)}, f32[16,640]{1,0:T(8,128)S(1)}, u32[]{:S(2)}, u32[]{:S(2)}) collective-permute-start(f32[16,640]{1,0:T(8,128)S(1)} %get-tuple-element.67.refs_10_), channel_id=1, source_target_pairs={{0,8},{8,0},{16,24},{24,16},{1,9},{9,1},{17,25},{25,17},{2,10},{10... | collective-permute-start | bytes 122888 | tf_op jit(solution)/shard_map/ppermute | solution.py:759
  97.7 4.7 %collective-permute-start.28 = (bf16[640,1920]{1,0:T(8,128)(2,1)S(1)}, bf16[640,1920]{1,0:T(8,128)(2,1)S(1)}, u32[]{:S(2)}, u32[]{:S(2)}) collective-permute-start(bf16[640,1920]{1,0:T(8,128)(2,1)S(1)} %get-tuple-element.78), channel_id=1, source_target_pairs={{0,1},{1,0},{2,3},{3,2},{4,5},{5,4},{6,7},{7,6},{8,9},{9,8},{10,11... | collective-permute-start | bytes 7372808 | tf_op jit(solution)/shard_map/ppermute | solution.py:759
  102.6 9.7 %collective-permute-start.29 = (bf16[80,1920]{1,0:T(8,128)(2,1)S(1)}, bf16[80,1920]{1,0:T(8,128)(2,1)S(1)}, u32[]{:S(2)}, u32[]{:S(2)}) collective-permute-start(bf16[80,1920]{1,0:T(8,128)(2,1)S(1)} %get-tuple-element.79), channel_id=1, source_target_pairs={{0,2},{1,3},{2,0},{3,1},{4,6},{5,7},{6,4},{7,5},{8,10},{9,11},{10,... | collective-permute-start | bytes 921608 | tf_op jit(solution)/shard_map/ppermute | solution.py:759
  104.2 9.4 %collective-permute-start.30 = (bf16[80,1920]{1,0:T(8,128)(2,1)S(1)}, bf16[80,1920]{1,0:T(8,128)(2,1)S(1)}, u32[]{:S(2)}, u32[]{:S(2)}) collective-permute-start(bf16[80,1920]{1,0:T(8,128)(2,1)S(1)} %get-tuple-element.80), channel_id=1, source_target_pairs={{0,4},{1,5},{2,6},{3,7},{4,0},{5,1},{6,2},{7,3},{8,12},{9,13},{10,... | collective-permute-start | bytes 921608 | tf_op jit(solution)/shard_map/ppermute | solution.py:759
  105.7 5.6 %collective-permute-start.27 = (f32[8,640]{1,0:T(8,128)S(1)}, f32[8,640]{1,0:T(8,128)S(1)}, u32[]{:S(2)}, u32[]{:S(2)}) collective-permute-start(f32[8,640]{1,0:T(8,128)S(1)} %get-tuple-element.76.refs_12_), channel_id=1, source_target_pairs={{0,24},{8,16},{16,8},{24,0},{1,25},{9,17},{17,9},{25,1},{2,26},{10... | collective-permute-start | bytes 61448 | tf_op jit(solution)/shard_map/ppermute | solution.py:759
  107.6 4.7 %collective-permute-start.26 = (f32[8,640]{1,0:T(8,128)S(1)}, f32[8,640]{1,0:T(8,128)S(1)}, u32[]{:S(2)}, u32[]{:S(2)}) collective-permute-start(f32[8,640]{1,0:T(8,128)S(1)} %get-tuple-element.76.refs_12_), channel_id=1, source_target_pairs={{0,16},{8,24},{16,0},{24,8},{1,17},{9,25},{17,1},{25,9},{2,18},{10... | collective-permute-start | bytes 61448 | tf_op jit(solution)/shard_map/ppermute | solution.py:759
  108.2 4.0 %collective-permute-start.25 = (f32[8,640]{1,0:T(8,128)S(1)}, f32[8,640]{1,0:T(8,128)S(1)}, u32[]{:S(2)}, u32[]{:S(2)}) collective-permute-start(f32[8,640]{1,0:T(8,128)S(1)} %get-tuple-element.76.refs_12_), channel_id=1, source_target_pairs={{0,8},{8,0},{16,24},{24,16},{1,9},{9,1},{17,25},{25,17},{2,10},{10... | collective-permute-start | bytes 61448 | tf_op jit(solution)/shard_map/ppermute | solution.py:759
  119.7 4.5 %collective-permute-start.31 = (bf16[656,1152]{1,0:T(8,128)(2,1)S(1)}, bf16[656,1152]{1,0:T(8,128)(2,1)S(1)}, u32[]{:S(2)}, u32[]{:S(2)}) collective-permute-start(bf16[656,1152]{1,0:T(8,128)(2,1)S(1)} %get-tuple-element.86), channel_id=1, source_target_pairs={{0,1},{1,0},{2,3},{3,2},{4,5},{5,4},{6,7},{7,6},{8,9},{9,8},{10,11... | collective-permute-start | bytes 4534280 | tf_op jit(solution)/shard_map/ppermute | solution.py:759
  121.6 18.7 %collective-permute-start.34 = (bf16[656,768]{1,0:T(8,128)(2,1)S(1)}, bf16[656,768]{1,0:T(8,128)(2,1)S(1)}, u32[]{:S(2)}, u32[]{:S(2)}) collective-permute-start(bf16[656,768]{1,0:T(8,128)(2,1)S(1)} %get-tuple-element.91), channel_id=1, source_target_pairs={{0,1},{1,0},{2,3},{3,2},{4,5},{5,4},{6,7},{7,6},{8,9},{9,8},{10,11... | collective-permute-start | bytes 3022856 | tf_op jit(solution)/shard_map/ppermute | solution.py:759
  122.2 16.7 %collective-permute-start.35 = (bf16[160,1920]{1,0:T(8,128)(2,1)S(1)}, bf16[160,1920]{1,0:T(8,128)(2,1)S(1)}, u32[]{:S(2)}, u32[]{:S(2)}) collective-permute-start(bf16[160,1920]{1,0:T(8,128)(2,1)S(1)} %get-tuple-element.81.refs_16_), channel_id=1, source_target_pairs={{0,2},{1,3},{2,0},{3,1},{4,6},{5,7},{6,4},{7,5},{8,10},{9,11},{10,... | collective-permute-start | bytes 1843208 | tf_op jit(solution)/shard_map/ppermute | solution.py:759
  122.7 16.7 %collective-permute-start.36 = (bf16[160,1920]{1,0:T(8,128)(2,1)S(1)}, bf16[160,1920]{1,0:T(8,128)(2,1)S(1)}, u32[]{:S(2)}, u32[]{:S(2)}) collective-permute-start(bf16[160,1920]{1,0:T(8,128)(2,1)S(1)} %get-tuple-element.82.refs_17_), channel_id=1, source_target_pairs={{0,4},{1,5},{2,6},{3,7},{4,0},{5,1},{6,2},{7,3},{8,12},{9,13},{10,... | collective-permute-start | bytes 1843208 | tf_op jit(solution)/shard_map/ppermute | solution.py:759
  124.5 22.4 %collective-permute-start.33 = (bf16[176,1152]{1,0:T(8,128)(2,1)S(1)}, bf16[176,1152]{1,0:T(8,128)(2,1)S(1)}, u32[]{:S(2)}, u32[]{:S(2)}) collective-permute-start(bf16[176,1152]{1,0:T(8,128)(2,1)S(1)} %get-tuple-element.88), channel_id=1, source_target_pairs={{0,4},{1,5},{2,6},{3,7},{4,0},{5,1},{6,2},{7,3},{8,12},{9,13},{10,... | collective-permute-start | bytes 1216520 | tf_op jit(solution)/shard_map/ppermute | solution.py:759
  125.1 21.9 %collective-permute-start.32 = (bf16[176,1152]{1,0:T(8,128)(2,1)S(1)}, bf16[176,1152]{1,0:T(8,128)(2,1)S(1)}, u32[]{:S(2)}, u32[]{:S(2)}) collective-permute-start(bf16[176,1152]{1,0:T(8,128)(2,1)S(1)} %get-tuple-element.87.refs_19_), channel_id=1, source_target_pairs={{0,2},{1,3},{2,0},{3,1},{4,6},{5,7},{6,4},{7,5},{8,10},{9,11},{10,... | collective-permute-start | bytes 1216520 | tf_op jit(solution)/shard_map/ppermute | solution.py:759
  147.1 9.1 %collective-permute-start.37 = (bf16[96,1152]{1,0:T(8,128)(2,1)S(1)}, bf16[96,1152]{1,0:T(8,128)(2,1)S(1)}, u32[]{:S(2)}, u32[]{:S(2)}) collective-permute-start(bf16[96,1152]{1,0:T(8,128)(2,1)S(1)} %get-tuple-element.94), channel_id=1, source_target_pairs={{0,2},{1,3},{2,0},{3,1},{4,6},{5,7},{6,4},{7,5},{8,10},{9,11},{10,... | collective-permute-start | bytes 663560 | tf_op jit(solution)/shard_map/ppermute | solution.py:759
  148.7 7.6 %collective-permute-start.38 = (bf16[80,1152]{1,0:T(8,128)(2,1)S(1)}, bf16[80,1152]{1,0:T(8,128)(2,1)S(1)}, u32[]{:S(2)}, u32[]{:S(2)}) collective-permute-start(bf16[80,1152]{1,0:T(8,128)(2,1)S(1)} %get-tuple-element.95), channel_id=1, source_target_pairs={{0,4},{1,5},{2,6},{3,7},{4,0},{5,1},{6,2},{7,3},{8,12},{9,13},{10,... | collective-permute-start | bytes 552968 | tf_op jit(solution)/shard_map/ppermute | solution.py:759
  150.2 9.4 %collective-permute-start.43 = (bf16[176,768]{1,0:T(8,128)(2,1)S(1)}, bf16[176,768]{1,0:T(8,128)(2,1)S(1)}, u32[]{:S(2)}, u32[]{:S(2)}) collective-permute-start(bf16[176,768]{1,0:T(8,128)(2,1)S(1)} %get-tuple-element.101), channel_id=1, source_target_pairs={{0,4},{1,5},{2,6},{3,7},{4,0},{5,1},{6,2},{7,3},{8,12},{9,13},{10,... | collective-permute-start | bytes 811016 | tf_op jit(solution)/shard_map/ppermute | solution.py:759
  150.7 9.0 %collective-permute-start.42 = (bf16[176,768]{1,0:T(8,128)(2,1)S(1)}, bf16[176,768]{1,0:T(8,128)(2,1)S(1)}, u32[]{:S(2)}, u32[]{:S(2)}) collective-permute-start(bf16[176,768]{1,0:T(8,128)(2,1)S(1)} %get-tuple-element.93.refs_4_), channel_id=1, source_target_pairs={{0,2},{1,3},{2,0},{3,1},{4,6},{5,7},{6,4},{7,5},{8,10},{9,11},{10,... | collective-permute-start | bytes 811016 | tf_op jit(solution)/shard_map/ppermute | solution.py:759
  151.2 11.2 %collective-permute-start.40 = (bf16[80,1920]{1,0:T(8,128)(2,1)S(1)}, bf16[80,1920]{1,0:T(8,128)(2,1)S(1)}, u32[]{:S(2)}, u32[]{:S(2)}) collective-permute-start(bf16[80,1920]{1,0:T(8,128)(2,1)S(1)} %get-tuple-element.98), channel_id=1, source_target_pairs={{0,8},{8,0},{16,24},{24,16},{1,9},{9,1},{17,25},{25,17},{2,10},{10... | collective-permute-start | bytes 921608 | tf_op jit(solution)/shard_map/ppermute | solution.py:759
  157.2 6.0 %collective-permute-start.39 = (bf16[96,1152]{1,0:T(8,128)(2,1)S(1)}, bf16[96,1152]{1,0:T(8,128)(2,1)S(1)}, u32[]{:S(2)}, u32[]{:S(2)}) collective-permute-start(bf16[96,1152]{1,0:T(8,128)(2,1)S(1)} %get-tuple-element.97), channel_id=1, source_target_pairs={{0,8},{8,0},{16,24},{24,16},{1,9},{9,1},{17,25},{25,17},{2,10},{10... | collective-permute-start | bytes 663560 | tf_op jit(solution)/shard_map/ppermute | solution.py:759
  159.7 6.0 %collective-permute-start.44 = (bf16[96,768]{1,0:T(8,128)(2,1)S(1)}, bf16[96,768]{1,0:T(8,128)(2,1)S(1)}, u32[]{:S(2)}, u32[]{:S(2)}) collective-permute-start(bf16[96,768]{1,0:T(8,128)(2,1)S(1)} %get-tuple-element.102), channel_id=1, source_target_pairs={{0,2},{1,3},{2,0},{3,1},{4,6},{5,7},{6,4},{7,5},{8,10},{9,11},{10,... | collective-permute-start | bytes 442376 | tf_op jit(solution)/shard_map/ppermute | solution.py:759
  160.9 4.9 %collective-permute-start.45 = (bf16[80,768]{1,0:T(8,128)(2,1)S(1)}, bf16[80,768]{1,0:T(8,128)(2,1)S(1)}, u32[]{:S(2)}, u32[]{:S(2)}) collective-permute-start(bf16[80,768]{1,0:T(8,128)(2,1)S(1)} %get-tuple-element.103), channel_id=1, source_target_pairs={{0,4},{1,5},{2,6},{3,7},{4,0},{5,1},{6,2},{7,3},{8,12},{9,13},{10,... | collective-permute-start | bytes 368648 | tf_op jit(solution)/shard_map/ppermute | solution.py:759
  163.9 10.4 %collective-permute-start.41 = (bf16[96,1152]{1,0:T(8,128)(2,1)S(1)}, bf16[96,1152]{1,0:T(8,128)(2,1)S(1)}, u32[]{:S(2)}, u32[]{:S(2)}) collective-permute-start(bf16[96,1152]{1,0:T(8,128)(2,1)S(1)} %get-tuple-element.100), channel_id=1, source_target_pairs={{0,16},{8,24},{16,0},{24,8},{1,17},{9,25},{17,1},{25,9},{2,18},{10... | collective-permute-start | bytes 663560 | tf_op jit(solution)/shard_map/ppermute | solution.py:759
  166.6 7.7 %collective-permute-start.46 = (bf16[96,768]{1,0:T(8,128)(2,1)S(1)}, bf16[96,768]{1,0:T(8,128)(2,1)S(1)}, u32[]{:S(2)}, u32[]{:S(2)}) collective-permute-start(bf16[96,768]{1,0:T(8,128)(2,1)S(1)} %get-tuple-element.105), channel_id=1, source_target_pairs={{0,8},{8,0},{16,24},{24,16},{1,9},{9,1},{17,25},{25,17},{2,10},{10... | collective-permute-start | bytes 442376 | tf_op jit(solution)/shard_map/ppermute | solution.py:759
  175.0 7.7 %collective-permute-start.47 = (bf16[96,768]{1,0:T(8,128)(2,1)S(1)}, bf16[96,768]{1,0:T(8,128)(2,1)S(1)}, u32[]{:S(2)}, u32[]{:S(2)}) collective-permute-start(bf16[96,768]{1,0:T(8,128)(2,1)S(1)} %get-tuple-element.107), channel_id=1, source_target_pairs={{0,16},{8,24},{16,0},{24,8},{1,17},{9,25},{17,1},{25,9},{2,18},{10... | collective-permute-start | bytes 442376 | tf_op jit(solution)/shard_map/ppermute | solution.py:759
  (3 other events, 19.2 us)

commit v3 on v2

--- a/solution.py
+++ b/solution.py
@@ -13,8 +13,8 @@
 SUBS = 8
 BIAS_ROWS = 16
 COST = 100
-UNROLL = 16
-LIMITS = (16, 20, 20, 14, 20, 14)
+UNROLL = 32
+LIMITS = (14, 16, 16, 12, 16, 12)
 ANY = pl.BlockSpec(memory_space=pl.ANY)
 HBM = pl.BlockSpec(memory_space=pltpu.HBM)
 VMEM = pl.BlockSpec(memory_space=pltpu.VMEM)
@@ -565,7 +565,7 @@
     (place, candid, forget, gate, cells, last, x, prev, keep, arriving, keep_firsts, other_bias) = refs[:12]
     summaries = refs[12:16]
     order, dcells, shifted, after = refs[-4:]
-    outs = refs[-9:-4] if has_sent else refs[-8:-4]
+    outs = refs[-11:-4] if has_sent else refs[-8:-4]
     dpre_out, shifted_out, bias_out, *grads = outs
     section = place[0]
     steps = rows // SUBS
@@ -582,8 +582,13 @@
         (dpre_out, shifted_out, bias_out.at[pl.ds(0, SUBS), :], after),
     )
     bias_out[SUBS:, :] = other_bias[...]
-    columns = slice(0, grads[0].shape[-1])
-    store_weight_grads(place, (x[...], prev[...]), dpre_out[:, columns], grads, bias_out[:, columns])
+    done = 0
+    for part in range(0, len(grads), 2):
+        columns = slice(done, done + grads[part].shape[-1])
+        store_weight_grads(
+            place, (x[...], prev[...]), dpre_out[:, columns], grads[part : part + 2], bias_out[:, columns]
+        )
+        done = columns.stop
 
 
 def last_kernel(plan, block, *refs):
@@ -738,7 +743,7 @@
     )
 
 
-def small_call(kernel, outs, operands, name, ties=(), scratch=()):
+def small_call(kernel, outs, operands, name, ties=(), scratch=(), flops=1000000):
     has_place = operands[0].dtype == jnp.int32
     specs = [SMEM if has_place and index == 0 else VMEM for index in range(len(operands))]
     return call(
@@ -747,7 +752,7 @@
         specs + [ANY] * len(ties),
         [VMEM] * len(outs),
         list(scratch),
-        1000000,
+        flops,
         1000000,
         12,
         name,
@@ -825,7 +830,7 @@
         )
         self.side_x, self.side_y = swap(self.by[0], "dp", 2), swap(self.by[1], "dp", 4)
 
-    def plane(self, ties=()):
+    def plane(self, ties=(), flops=1000000):
         operands = [self.place, self.kept, self.got, self.side_x, self.side_y, self.corner_x, self.corner_y]
         scratch = []
         if self.extra > 0:
@@ -837,6 +842,7 @@
             "plane",
             ties,
             scratch,
+            flops,
         )
         self.near = swap(other, "section", 1)
 
@@ -882,7 +888,7 @@
     gates = 3 * width
     tiles = width // LANES
     rows = length // sections
-    block = 256
+    block = 512
     start = section * rows
     height = tap_weight.shape[1]
     quick = sections == 4 and streams == 8 and height % 16 == 0
@@ -1014,13 +1020,13 @@
         second.corners(ties=[arriving])
         second.sides(ties=summaries[1:])
         ties = second.by
-        first_columns = gates // LANES * 3 // 5 * LANES
-        first_shape = kept_and_sent(first_columns, BIAS_ROWS)
+        first_columns = gates // LANES * 8 // 15 * LANES
+        first_shape = kept_and_sent(first_columns, BIAS_ROWS) + kept_and_sent(gates - first_columns, BIAS_ROWS)
     dpre0, shifted0, bias_both, *kept0 = call(
         functools.partial(first_backward_kernel, rows, quick),
         [wide, wide, shape(2 * SUBS, gates)] + first_shape,
         [SMEM] + [VMEM] * 15 + [ANY] * len(ties),
-        [VMEM] * (3 + len(kept_shape)),
+        [VMEM] * (3 + len(first_shape)),
         [buffer(sections, 8, width), scan, buffer(3, rows + SUBS, LANES), buffer(SUBS, gates)],
         layer_flops,
         weight_bytes + 30 * rows * width,
@@ -1030,33 +1036,24 @@
         place, candid0, forget0, gate0, cells0, last0, x, prev, keep_own, arriving, keep_firsts, bias1,
         *summaries, *ties,
     )
-    if quick:
-        later = small_call(
-            functools.partial(first_weights_kernel, first_columns),
-            kept_and_sent(gates - first_columns, BIAS_ROWS),
-            [place, x, prev, dpre0, bias_both],
-            "first_weights",
-        )
-        parts = [slice(0, first_columns), slice(first_columns, gates)]
-        sums = [LayerSum(place, *pieces) for pieces in (kept0, later)]
-        sums[0].corners()
-        ties = [sums[0].corner_sent]
-
     input_grad = call(
         functools.partial(last_kernel, plan, block),
         shape(rows, width),
-        [SMEM] + [VMEM] * 2 + [HBM] * len(weights) + [ANY] * len(ties),
+        [SMEM] + [VMEM] * 2 + [HBM] * len(weights),
         VMEM,
         [buffer(2 * width, gates, dtype=BF16), dma((weight_count + 1,))],
         COST * layer_flops,
         COST * weight_bytes,
         LIMITS[5],
         "last",
-    )(place, dpre0, shifted0, *weights, *ties)
+    )(place, dpre0, shifted0, *weights)
 
     if quick:
-        second.plane(ties=[input_grad])
-        sums[1].corners(ties=[second.mine])
+        second.plane(ties=[input_grad], flops=COST * 3 * 10**10)
+        parts = [slice(0, first_columns), slice(first_columns, gates)]
+        sums = [LayerSum(place, *kept0[:2]), LayerSum(place, *kept0[2:])]
+        sums[0].corners(ties=[second.mine])
+        sums[1].corners(ties=[sums[0].corner_sent])
         sums[0].sides(ties=[sums[1].corner_sent])
         pair = second.paired()
         sums[0].plane()

time: 184 us -> 178 us (0.967)
  waiting for transfers between devices: 76.9 us -> 71.7 us
    ppermute x42, waiting for transfers between devices: 55.7 us -> 50.5 us  [swap(): return lax.ppermute(value, axis, pairs)]
    pallas_call x21 -> x20, Pallas kernels: 12.5 us -> 10.6 us  [small_call(): call(kernel, outs, specs + [ANY] * len(ties), [VMEM] * len(outs), list(sc...]
  transfers between devices with their start and end apart: 48 -> 48, of which waited for: 27 -> 25; matrix products, arithmetic and copies ran while one was open for 3% -> 3% of each run, Pallas kernels for 11% -> 14%
where the time goes in v3:
time: 178 us; the launch traced here: 177 us
  waiting for transfers between devices  71.7 us (40%)
  starting transfers between devices  50.8 us (29%)
  Pallas kernels  47.7 us (27%)
  local copies, waits for them, and re-layouts  5.65 us (3%)
    ppermute x42, waiting for transfers between devices, swap(): return lax.ppermute(value, axis, pairs)  50.5 us
    ppermute x42, starting transfers between devices, swap(): return lax.ppermute(value, axis, pairs)  42.3 us
    ppermute x6, waiting for transfers between devices, moved(): lax.ppermute(value, axis, [(index, target(index)) for index in range(lax....  21.2 us
    pallas_call x20, Pallas kernels, small_call(): call(kernel, outs, specs + [ANY] * len(ties), [VMEM] * len(outs), list(sc...  10.6 us
    ppermute x6, starting transfers between devices, moved(): lax.ppermute(value, axis, [(index, target(index)) for index in range(lax....  8.53 us
    pallas_call x1, Pallas kernels, per_device(): call(functools.partial(second_forward_kernel, plan, block), [shape(tiles,...  7.4 us
    pallas_call x1, Pallas kernels, per_device(): call(functools.partial(second_backward_kernel, rows, quick), [half, wide,...  7.13 us
    pallas_call x1, Pallas kernels, per_device(): call(functools.partial(first_backward_kernel, rows, quick), [wide, wide,...  7.12 us
  transfers between devices with their start and end apart: 48, of which 25 were waited for; matrix products, arithmetic and copies ran while one was open for 3% of the time, Pallas kernels for 14%

profile of v3, /device:TPU:0, one launch (start us, length us, event | category | flops | bytes accessed | tf_op | source)
XLA Modules:
  0.0 177.0 jit_solution(11366826406853903536)
XLA Ops:
  0.7 4.1 %collective-permute-start.9 = (bf16[80,1920]{1,0:T(8,128)(2,1)}, bf16[80,1920]{1,0:T(8,128)(2,1)S(1)}, u32[]{:S(2)}, u32[]{:S(2)}) collective-permute-start(bf16[80,1920]{1,0:T(8,128)(2,1)} %bitcast.46), channel_id=1, source_target_pairs={{0,16},{8,24},{16,0},{24,8},{1,17},{9,25},{17,1},{25,9},{2,18},{10... | collective-permute-start | bytes 921608 | tf_op jit(solution)/shard_map/ppermute | solution.py:764
  4.8 1.6 collective-permute-start.3
  6.4 1.4 constant_dynamic-slice_fusion
  8.7 1.4 collective-permute-start.1
  12.0 7.1 %collective-permute-done.3.own = bf16[80,1920]{1,0:T(8,128)(2,1)S(1)} collective-permute-done((bf16[80,1920]{1,0:T(8,128)(2,1)}, bf16[80,1920]{1,0:T(8,128)(2,1)S(1)}, u32[]{:S(2)}, u32[]{:S(2)}) %collective-permute-start.3) | collective-permute-done | bytes 307232 | tf_op jit(solution)/shard_map/ppermute | solution.py:764
  20.2 1.6 collective-permute-start.13
  22.3 1.4 collective-permute-start.5
  24.0 5.9 %collective-permute-done.13.own = bf16[80,1920]{1,0:T(8,128)(2,1)S(1)} collective-permute-done((bf16[80,1920]{1,0:T(8,128)(2,1)S(1)}, bf16[80,1920]{1,0:T(8,128)(2,1)S(1)}, u32[]{:S(2)}, u32[]{:S(2)}) %collective-permute-start.13) | collective-permute-done | bytes 307232 | tf_op jit(solution)/shard_map/ppermute | solution.py:764
  30.5 1.7 collective-permute-start.11
  35.1 1.3 collective-permute-start.7
  36.4 3.7 %collective-permute-done.11.first.refs_14_.refs_20_.refs_12_ = bf16[160,1920]{1,0:T(8,128)(2,1)S(1)} collective-permute-done((bf16[160,1920]{1,0:T(8,128)(2,1)S(1)}, bf16[160,1920]{1,0:T(8,128)(2,1)S(1)}, u32[]{:S(2)}, u32[]{:S(2)}) %collective-permute-start.11) | collective-permute-done | bytes 614432 | tf_op jit(solution)/shard_map/ppermute | solution.py:768
  40.1 6.6 %collective-permute-done.15.second.refs_17_.refs_23_.refs_15_ = bf16[160,1920]{1,0:T(8,128)(2,1)S(1)} collective-permute-done((bf16[160,1920]{1,0:T(8,128)(2,1)S(1)}, bf16[160,1920]{1,0:T(8,128)(2,1)S(1)}, u32[]{:S(2)}, u32[]{:S(2)}) %collective-permute-start.15) | collective-permute-done | bytes 614432 | tf_op jit(solution)/shard_map/ppermute | solution.py:768
  47.3 1.6 collective-permute-start.17
  49.7 4.3 %collective-permute-done.7.refs_11_.refs_17_.refs_9_ = bf16[160,1920]{1,0:T(8,128)(2,1)S(1)} collective-permute-done((bf16[160,1920]{1,0:T(8,128)(2,1)S(1)}, bf16[160,1920]{1,0:T(8,128)(2,1)S(1)}, u32[]{:S(2)}, u32[]{:S(2)}) %collective-permute-start.7) | collective-permute-done | bytes 614432 | tf_op jit(solution)/shard_map/ppermute | solution.py:768
  54.0 6.6 %collective-permute-done.17.refs_19_.refs_25_.refs_17_ = bf16[160,1920]{1,0:T(8,128)(2,1)S(1)} collective-permute-done((bf16[160,1920]{1,0:T(8,128)(2,1)S(1)}, bf16[160,1920]{1,0:T(8,128)(2,1)S(1)}, u32[]{:S(2)}, u32[]{:S(2)}) %collective-permute-start.17) | collective-permute-done | bytes 614432 | tf_op jit(solution)/shard_map/ppermute | solution.py:768
  60.6 2.0 %collective-permute-done.18.refs_20_.refs_26_.refs_18_ = bf16[160,1920]{1,0:T(8,128)(2,1)S(1)} collective-permute-done((bf16[160,1920]{1,0:T(8,128)(2,1)S(1)}, bf16[160,1920]{1,0:T(8,128)(2,1)S(1)}, u32[]{:S(2)}, u32[]{:S(2)}) %collective-permute-start.18) | collective-permute-done | bytes 614432 | tf_op jit(solution)/shard_map/ppermute | solution.py:764
  62.6 5.9 %first_forward.1 = (f32[5,512,128]{2,1,0:T(8,128)S(1)}, f32[5,512,128]{2,1,0:T(8,128)S(1)}, f32[5,512,128]{2,1,0:T(8,128)S(1)}, f32[8,640]{1,0:T(8,128)S(1)}) custom-call(s32[2]{0:T(128)S(1)} %pad_add_fusion.refs_0_.place, bf16[512,640]{1,0:T(8,128)(2,1)S(1)} %bitcast.42, bf16[512,640]{1,0:T(8,128)(2,1)S(1)} %before.1.refs_1_.refs_2_.refs_7_, ...), custom_call_target="tpu_custom_call" | custom-call | flops 25165824 | bytes 147456 | tf_op jit(solution)/shard_map/first_forward/pallas_call | solution.py:947
  68.5 1.7 collective-permute-start.21
  70.2 1.3 collective-permute-start.20
  71.5 1.4 collective-permute-start.19
  72.9 1.3 collective-permute-done.21.refs_10_
  75.3 7.4 %second_forward.1 = (f32[5,520,128]{2,1,0:T(8,128)S(1)}, bf16[512,640]{1,0:T(8,128)(2,1)S(1)}, bf16[512,640]{1,0:T(8,128)(2,1)S(1)}, f32[8,640]{1,0:T(8,128)S(1)...) custom-call(s32[2]{0:T(128)S(1)} %pad_add_fusion.refs_0_.place, ...), custom_call_target="tpu_custom_call" | custom-call | flops 25165824 | bytes 114688 | tf_op jit(solution)/shard_map/second_forward/pallas_call | solution.py:959
  82.7 1.9 %collective-permute-start.24 = (f32[16,640]{1,0:T(8,128)S(1)}, f32[16,640]{1,0:T(8,128)S(1)}, u32[]{:S(2)}, u32[]{:S(2)}) collective-permute-start(f32[16,640]{1,0:T(8,128)S(1)} %get-tuple-element.66.refs_10_), channel_id=1, source_target_pairs={{0,24},{8,16},{16,8},{24,0},{1,25},{9,17},{17,9},{25,1},{2,26},{10... | collective-permute-start | bytes 122888 | tf_op jit(solution)/shard_map/ppermute | solution.py:764
  85.7 1.5 collective-permute-start.22
  87.1 1.5 collective-permute-done.24.refs_13_
  90.0 7.1 %second_backward.1 = (bf16[512,640]{1,0:T(8,128)(2,1)S(1)}, bf16[512,1920]{1,0:T(8,128)(2,1)S(1)}, bf16[512,1920]{1,0:T(8,128)(2,1)S(1)}, f32[8,1920]{1,0:T(8,12...) custom-call(s32[2]{0:T(128)S(1)} %pad_add_fusion.refs_0_.place, ...), custom_call_target="tpu_custom_call" | custom-call | flops 25165824 | bytes 147456 | tf_op jit(solution)/shard_map/second_backward/pallas_call | solution.py:988
  97.3 4.2 %middle.1 = (bf16[512,640]{1,0:T(8,128)(2,1)S(1)}, f32[8,640]{1,0:T(8,128)S(1)}) custom-call(s32[2]{0:T(128)S(1)} %pad_add_fusion.refs_0_.place, bf16[512,1920]{1,0:T(8,128)(2,1)S(1)} %get-tuple-element.70.refs_1_, bf16[512,1920]{1,0:T(8,128)(2,1)S(1)} %get-tuple-element.71.refs_2_, f32[5,512,128]{2,1,0:T(8,128)S(1)} %get-tuple-element.57.refs_1_.refs_3_, ...), custom_call_target="tpu_custom_call" | custom-call | flops 25165824 | bytes 114688 | tf_op jit(solution)/shard_map/middle/pallas_call | solution.py:1003
  102.1 1.6 collective-permute-start.29
  103.6 1.5 collective-permute-start.30
  105.1 1.9 %collective-permute-start.27 = (f32[8,640]{1,0:T(8,128)S(1)}, f32[8,640]{1,0:T(8,128)S(1)}, u32[]{:S(2)}, u32[]{:S(2)}) collective-permute-start(f32[8,640]{1,0:T(8,128)S(1)} %get-tuple-element.75.refs_12_), channel_id=1, source_target_pairs={{0,24},{8,16},{16,8},{24,0},{1,25},{9,17},{17,9},{25,1},{2,26},{10... | collective-permute-start | bytes 61448 | tf_op jit(solution)/shard_map/ppermute | solution.py:764
  107.7 1.8 %collective-permute-start.25 = (f32[8,640]{1,0:T(8,128)S(1)}, f32[8,640]{1,0:T(8,128)S(1)}, u32[]{:S(2)}, u32[]{:S(2)}) collective-permute-start(f32[8,640]{1,0:T(8,128)S(1)} %get-tuple-element.75.refs_12_), channel_id=1, source_target_pairs={{0,8},{8,0},{16,24},{24,16},{1,9},{9,1},{17,25},{25,17},{2,10},{10... | collective-permute-start | bytes 61448 | tf_op jit(solution)/shard_map/ppermute | solution.py:764
  109.5 1.2 collective-permute-done.27.refs_6_.refs_15_
  113.6 1.5 collective-permute-start.33
  115.2 7.1 %first_backward.1 = (bf16[512,1920]{1,0:T(8,128)(2,1)S(1)}, bf16[512,1920]{1,0:T(8,128)(2,1)S(1)}, f32[16,1920]{1,0:T(8,128)}, bf16[656,1024]{1,0:T(8,128)(2,1)S...) custom-call(s32[2]{0:T(128)S(1)} %pad_add_fusion.refs_0_.place, ...), custom_call_target="tpu_custom_call" | custom-call | flops 25165824 | bytes 147456 | tf_op jit(solution)/shard_map/first_backward/pallas_call | solution.py:1025
  122.8 5.4 %last.1.refs_7_ = f32[512,640]{1,0:T(8,128)S(1)} custom-call(s32[2]{0:T(128)S(1)} %pad_add_fusion.refs_0_.place, bf16[512,1920]{1,0:T(8,128)(2,1)S(1)} %get-tuple-element.82.refs_1_, bf16[512,1920]{1,0:T(8,128)(2,1)S(1)} %get-tuple-element.83.refs_2_, bf16[160,1920]{1,0:T(8,128)(2,1)S(1)} %join.4.refs_5_.refs_11_.refs_3_, ...), custom_call_target="tpu_custom_call" | custom-call | flops 2516582400 | bytes 4915200 | tf_op jit(solution)/shard_map/last/pallas_call | solution.py:1039
  129.4 1.5 collective-permute-start.35
  131.0 1.4 collective-permute-start.34
  133.9 6.9 %collective-permute-done.35.refs_3_.refs_6_ = bf16[176,1024]{1,0:T(8,128)(2,1)S(1)} collective-permute-done((bf16[176,1024]{1,0:T(8,128)(2,1)S(1)}, bf16[176,1024]{1,0:T(8,128)(2,1)S(1)}, u32[]{:S(2)}, u32[]{:S(2)}) %collective-permute-start.35) | collective-permute-done | bytes 360480 | tf_op jit(solution)/shard_map/ppermute | solution.py:764
  140.8 1.5 collective-permute-done.34.refs_2_.refs_5_
  142.4 1.5 collective-permute-start.37
  145.6 4.5 %collective-permute-done.38.refs_4_ = bf16[80,1024]{1,0:T(8,128)(2,1)S(1)} collective-permute-done((bf16[80,1024]{1,0:T(8,128)(2,1)S(1)}, bf16[80,1024]{1,0:T(8,128)(2,1)S(1)}, u32[]{:S(2)}, u32[]{:S(2)}) %collective-permute-start.38) | collective-permute-done | bytes 163872 | tf_op jit(solution)/shard_map/ppermute | solution.py:764
  153.2 1.6 collective-permute-start.44
  154.8 1.5 collective-permute-start.45
  156.4 1.3 collective-permute-done.39.refs_2_
  158.4 1.7 collective-permute-start.41
  162.0 6.2 %collective-permute-done.46.refs_2_ = bf16[96,896]{1,0:T(8,128)(2,1)S(1)} collective-permute-done((bf16[96,896]{1,0:T(8,128)(2,1)S(1)}, bf16[96,896]{1,0:T(8,128)(2,1)S(1)}, u32[]{:S(2)}, u32[]{:S(2)}) %collective-permute-start.46) | collective-permute-done | bytes 172064 | tf_op jit(solution)/shard_map/ppermute | solution.py:764
  169.8 1.3 copy.16
  171.1 4.9 %collective-permute-done.47.refs_3_ = bf16[96,896]{1,0:T(8,128)(2,1)S(1)} collective-permute-done((bf16[96,896]{1,0:T(8,128)(2,1)S(1)}, bf16[96,896]{1,0:T(8,128)(2,1)S(1)}, u32[]{:S(2)}, u32[]{:S(2)}) %collective-permute-start.47) | collective-permute-done | bytes 172064 | tf_op jit(solution)/shard_map/ppermute | solution.py:764
  (98 shorter events, 30.7 us)
Async XLA Ops:
  0.7 19.5 %collective-permute-start.9 = (bf16[80,1920]{1,0:T(8,128)(2,1)}, bf16[80,1920]{1,0:T(8,128)(2,1)S(1)}, u32[]{:S(2)}, u32[]{:S(2)}) collective-permute-start(bf16[80,1920]{1,0:T(8,128)(2,1)} %bitcast.46), channel_id=1, source_target_pairs={{0,16},{8,24},{16,0},{24,8},{1,17},{9,25},{17,1},{25,9},{2,18},{10... | collective-permute-start | bytes 921608 | tf_op jit(solution)/shard_map/ppermute | solution.py:764
  4.8 14.4 %collective-permute-start.3 = (bf16[80,1920]{1,0:T(8,128)(2,1)}, bf16[80,1920]{1,0:T(8,128)(2,1)S(1)}, u32[]{:S(2)}, u32[]{:S(2)}) collective-permute-start(bf16[80,1920]{1,0:T(8,128)(2,1)} %bitcast.47), channel_id=1, source_target_pairs={{0,8},{8,0},{16,24},{24,16},{1,9},{9,1},{17,25},{25,17},{2,10},{10... | collective-permute-start | bytes 921608 | tf_op jit(solution)/shard_map/ppermute | solution.py:764
  6.3 1.8 %collective-permute-start = (bf16[80,1920]{1,0:T(8,128)(2,1)}, bf16[80,1920]{1,0:T(8,128)(2,1)S(1)}, u32[]{:S(2)}, u32[]{:S(2)}) collective-permute-start(bf16[80,1920]{1,0:T(8,128)(2,1)} %bitcast.48), channel_id=1, source_target_pairs={{0,1},{1,0},{2,3},{3,2},{4,5},{5,4},{6,7},{7,6},{8,9},{9,8},{10,11... | collective-permute-start | bytes 921608 | tf_op jit(solution)/shard_map/ppermute | solution.py:764
  8.7 13.0 %collective-permute-start.1 = (bf16[160,1920]{1,0:T(8,128)(2,1)S(1)}, bf16[160,1920]{1,0:T(8,128)(2,1)S(1)}, u32[]{:S(2)}, u32[]{:S(2)}) collective-permute-start(bf16[160,1920]{1,0:T(8,128)(2,1)S(1)} %join.4.refs_5_.refs_11_.refs_3_), channel_id=1, source_target_pairs={{0,3},{1,4},{2,1},{3,6},{4,7},{5,0},{6,5},{7,2},{8,11},{9,12},{10,... | collective-permute-start | bytes 1843208 | tf_op jit(solution)/shard_map/ppermute | solution.py:768
  19.1 2.6 %collective-permute-start.4 = (bf16[80,1920]{1,0:T(8,128)(2,1)S(1)}, bf16[80,1920]{1,0:T(8,128)(2,1)S(1)}, u32[]{:S(2)}, u32[]{:S(2)}) collective-permute-start(bf16[80,1920]{1,0:T(8,128)(2,1)S(1)} %collective-permute-done.3.own), channel_id=1, source_target_pairs={{0,1},{1,0},{2,3},{3,2},{4,5},{5,4},{6,7},{7,6},{8,9},{9,8},{10,11... | collective-permute-start | bytes 921608 | tf_op jit(solution)/shard_map/ppermute | solution.py:764
  20.2 9.7 %collective-permute-start.13 = (bf16[80,1920]{1,0:T(8,128)(2,1)S(1)}, bf16[80,1920]{1,0:T(8,128)(2,1)S(1)}, u32[]{:S(2)}, u32[]{:S(2)}) collective-permute-start(bf16[80,1920]{1,0:T(8,128)(2,1)S(1)} %collective-permute-done.9.own), channel_id=1, source_target_pairs={{0,8},{8,0},{16,24},{24,16},{1,9},{9,1},{17,25},{25,17},{2,10},{10... | collective-permute-start | bytes 921608 | tf_op jit(solution)/shard_map/ppermute | solution.py:764
  22.3 9.9 %collective-permute-start.5 = (bf16[160,1920]{1,0:T(8,128)(2,1)S(1)}, bf16[160,1920]{1,0:T(8,128)(2,1)S(1)}, u32[]{:S(2)}, u32[]{:S(2)}) collective-permute-start(bf16[160,1920]{1,0:T(8,128)(2,1)S(1)} %join.5.refs_8_.refs_14_.refs_6_), channel_id=1, source_target_pairs={{0,3},{1,4},{2,1},{3,6},{4,7},{5,0},{6,5},{7,2},{8,11},{9,12},{10,... | collective-permute-start | bytes 1843208 | tf_op jit(solution)/shard_map/ppermute | solution.py:768
  23.7 6.2 %collective-permute-start.10 = (bf16[80,1920]{1,0:T(8,128)(2,1)S(1)}, bf16[80,1920]{1,0:T(8,128)(2,1)S(1)}, u32[]{:S(2)}, u32[]{:S(2)}) collective-permute-start(bf16[80,1920]{1,0:T(8,128)(2,1)S(1)} %collective-permute-done.9.own), channel_id=1, source_target_pairs={{0,1},{1,0},{2,3},{3,2},{4,5},{5,4},{6,7},{7,6},{8,9},{9,8},{10,11... | collective-permute-start | bytes 921608 | tf_op jit(solution)/shard_map/ppermute | solution.py:764
  29.9 2.3 %collective-permute-start.14 = (bf16[80,1920]{1,0:T(8,128)(2,1)S(1)}, bf16[80,1920]{1,0:T(8,128)(2,1)S(1)}, u32[]{:S(2)}, u32[]{:S(2)}) collective-permute-start(bf16[80,1920]{1,0:T(8,128)(2,1)S(1)} %collective-permute-done.13.own), channel_id=1, source_target_pairs={{0,1},{1,0},{2,3},{3,2},{4,5},{5,4},{6,7},{7,6},{8,9},{9,8},{10,11... | collective-permute-start | bytes 921608 | tf_op jit(solution)/shard_map/ppermute | solution.py:764
  30.5 9.6 %collective-permute-start.11 = (bf16[160,1920]{1,0:T(8,128)(2,1)S(1)}, bf16[160,1920]{1,0:T(8,128)(2,1)S(1)}, u32[]{:S(2)}, u32[]{:S(2)}) collective-permute-start(bf16[160,1920]{1,0:T(8,128)(2,1)S(1)} %join.6.refs_13_.refs_19_.refs_11_), channel_id=1, source_target_pairs={{0,3},{1,4},{2,1},{3,6},{4,7},{5,0},{6,5},{7,2},{8,11},{9,12},{10,... | collective-permute-start | bytes 1843208 | tf_op jit(solution)/shard_map/ppermute | solution.py:768
  32.8 13.9 %collective-permute-start.15 = (bf16[160,1920]{1,0:T(8,128)(2,1)S(1)}, bf16[160,1920]{1,0:T(8,128)(2,1)S(1)}, u32[]{:S(2)}, u32[]{:S(2)}) collective-permute-start(bf16[160,1920]{1,0:T(8,128)(2,1)S(1)} %join.7.refs_16_.refs_22_.refs_14_), channel_id=1, source_target_pairs={{0,3},{1,4},{2,1},{3,6},{4,7},{5,0},{6,5},{7,2},{8,11},{9,12},{10,... | collective-permute-start | bytes 1843208 | tf_op jit(solution)/shard_map/ppermute | solution.py:768
  34.0 15.4 %collective-permute-start.2 = (bf16[160,1920]{1,0:T(8,128)(2,1)S(1)}, bf16[160,1920]{1,0:T(8,128)(2,1)S(1)}, u32[]{:S(2)}, u32[]{:S(2)}) collective-permute-start(bf16[160,1920]{1,0:T(8,128)(2,1)S(1)} %collective-permute-done.1.refs_0_.first.refs_6_.refs_12_.refs_4_), channel_id=1, source_target_pairs={{0,1},{1,0},{2,3},{3,2},{4,5},{5,4},{6,7},{7,6},{8,9},{9,8},{10,11... | collective-permute-start | bytes 1843208 | tf_op jit(solution)/shard_map/ppermute | solution.py:764
  35.1 18.9 %collective-permute-start.7 = (bf16[160,1920]{1,0:T(8,128)(2,1)S(1)}, bf16[160,1920]{1,0:T(8,128)(2,1)S(1)}, u32[]{:S(2)}, u32[]{:S(2)}) collective-permute-start(bf16[160,1920]{1,0:T(8,128)(2,1)S(1)} %pick.2), channel_id=1, source_target_pairs={{0,2},{1,5},{2,0},{3,7},{4,6},{5,1},{6,4},{7,3},{8,10},{9,13},{10,... | collective-permute-start | bytes 1843208 | tf_op jit(solution)/shard_map/ppermute | solution.py:768
  47.3 13.2 %collective-permute-start.17 = (bf16[160,1920]{1,0:T(8,128)(2,1)S(1)}, bf16[160,1920]{1,0:T(8,128)(2,1)S(1)}, u32[]{:S(2)}, u32[]{:S(2)}) collective-permute-start(bf16[160,1920]{1,0:T(8,128)(2,1)S(1)} %pick.3), channel_id=1, source_target_pairs={{0,2},{1,5},{2,0},{3,7},{4,6},{5,1},{6,4},{7,3},{8,10},{9,13},{10,... | collective-permute-start | bytes 1843208 | tf_op jit(solution)/shard_map/ppermute | solution.py:768
  48.9 11.7 %collective-permute-start.12 = (bf16[160,1920]{1,0:T(8,128)(2,1)S(1)}, bf16[160,1920]{1,0:T(8,128)(2,1)S(1)}, u32[]{:S(2)}, u32[]{:S(2)}) collective-permute-start(bf16[160,1920]{1,0:T(8,128)(2,1)S(1)} %collective-permute-done.11.first.refs_14_.refs_20_.refs_12_), channel_id=1, source_target_pairs={{0,1},{1,0},{2,3},{3,2},{4,5},{5,4},{6,7},{7,6},{8,9},{9,8},{10,11... | collective-permute-start | bytes 1843208 | tf_op jit(solution)/shard_map/ppermute | solution.py:764
  49.2 11.4 %collective-permute-start.6 = (bf16[160,1920]{1,0:T(8,128)(2,1)S(1)}, bf16[160,1920]{1,0:T(8,128)(2,1)S(1)}, u32[]{:S(2)}, u32[]{:S(2)}) collective-permute-start(bf16[160,1920]{1,0:T(8,128)(2,1)S(1)} %collective-permute-done.5.second.refs_0_.refs_9_.refs_15_.refs_7_), channel_id=1, source_target_pairs={{0,1},{1,0},{2,3},{3,2},{4,5},{5,4},{6,7},{7,6},{8,9},{9,8},{10,11... | collective-permute-start | bytes 1843208 | tf_op jit(solution)/shard_map/ppermute | solution.py:764
  49.5 11.2 %collective-permute-start.16 = (bf16[160,1920]{1,0:T(8,128)(2,1)S(1)}, bf16[160,1920]{1,0:T(8,128)(2,1)S(1)}, u32[]{:S(2)}, u32[]{:S(2)}) collective-permute-start(bf16[160,1920]{1,0:T(8,128)(2,1)S(1)} %collective-permute-done.15.second.refs_17_.refs_23_.refs_15_), channel_id=1, source_target_pairs={{0,1},{1,0},{2,3},{3,2},{4,5},{5,4},{6,7},{7,6},{8,9},{9,8},{10,11... | collective-permute-start | bytes 1843208 | tf_op jit(solution)/shard_map/ppermute | solution.py:764
  54.0 6.6 %collective-permute-start.8 = (bf16[160,1920]{1,0:T(8,128)(2,1)S(1)}, bf16[160,1920]{1,0:T(8,128)(2,1)S(1)}, u32[]{:S(2)}, u32[]{:S(2)}) collective-permute-start(bf16[160,1920]{1,0:T(8,128)(2,1)S(1)} %collective-permute-done.7.refs_11_.refs_17_.refs_9_), channel_id=1, source_target_pairs={{0,1},{1,0},{2,3},{3,2},{4,5},{5,4},{6,7},{7,6},{8,9},{9,8},{10,11... | collective-permute-start | bytes 1843208 | tf_op jit(solution)/shard_map/ppermute | solution.py:764
  60.6 2.0 %collective-permute-start.18 = (bf16[160,1920]{1,0:T(8,128)(2,1)S(1)}, bf16[160,1920]{1,0:T(8,128)(2,1)S(1)}, u32[]{:S(2)}, u32[]{:S(2)}) collective-permute-start(bf16[160,1920]{1,0:T(8,128)(2,1)S(1)} %collective-permute-done.17.refs_19_.refs_25_.refs_17_), channel_id=1, source_target_pairs={{0,1},{1,0},{2,3},{3,2},{4,5},{5,4},{6,7},{7,6},{8,9},{9,8},{10,11... | collective-permute-start | bytes 1843208 | tf_op jit(solution)/shard_map/ppermute | solution.py:764
  68.5 5.8 %collective-permute-start.21 = (f32[8,640]{1,0:T(8,128)S(1)}, f32[8,640]{1,0:T(8,128)S(1)}, u32[]{:S(2)}, u32[]{:S(2)}) collective-permute-start(f32[8,640]{1,0:T(8,128)S(1)} %get-tuple-element.60.refs_7_), channel_id=1, source_target_pairs={{0,24},{8,16},{16,8},{24,0},{1,25},{9,17},{17,9},{25,1},{2,26},{10... | collective-permute-start | bytes 61448 | tf_op jit(solution)/shard_map/ppermute | solution.py:764
  70.2 4.7 %collective-permute-start.20 = (f32[8,640]{1,0:T(8,128)S(1)}, f32[8,640]{1,0:T(8,128)S(1)}, u32[]{:S(2)}, u32[]{:S(2)}) collective-permute-start(f32[8,640]{1,0:T(8,128)S(1)} %get-tuple-element.60.refs_7_), channel_id=1, source_target_pairs={{0,16},{8,24},{16,0},{24,8},{1,17},{9,25},{17,1},{25,9},{2,18},{10... | collective-permute-start | bytes 61448 | tf_op jit(solution)/shard_map/ppermute | solution.py:764
  71.5 3.8 %collective-permute-start.19 = (f32[8,640]{1,0:T(8,128)S(1)}, f32[8,640]{1,0:T(8,128)S(1)}, u32[]{:S(2)}, u32[]{:S(2)}) collective-permute-start(f32[8,640]{1,0:T(8,128)S(1)} %get-tuple-element.60.refs_7_), channel_id=1, source_target_pairs={{0,8},{8,0},{16,24},{24,16},{1,9},{9,1},{17,25},{25,17},{2,10},{10... | collective-permute-start | bytes 61448 | tf_op jit(solution)/shard_map/ppermute | solution.py:764
  82.7 6.0 %collective-permute-start.24 = (f32[16,640]{1,0:T(8,128)S(1)}, f32[16,640]{1,0:T(8,128)S(1)}, u32[]{:S(2)}, u32[]{:S(2)}) collective-permute-start(f32[16,640]{1,0:T(8,128)S(1)} %get-tuple-element.66.refs_10_), channel_id=1, source_target_pairs={{0,24},{8,16},{16,8},{24,0},{1,25},{9,17},{17,9},{25,1},{2,26},{10... | collective-permute-start | bytes 122888 | tf_op jit(solution)/shard_map/ppermute | solution.py:764
  84.6 5.0 %collective-permute-start.23 = (f32[16,640]{1,0:T(8,128)S(1)}, f32[16,640]{1,0:T(8,128)S(1)}, u32[]{:S(2)}, u32[]{:S(2)}) collective-permute-start(f32[16,640]{1,0:T(8,128)S(1)} %get-tuple-element.66.refs_10_), channel_id=1, source_target_pairs={{0,16},{8,24},{16,0},{24,8},{1,17},{9,25},{17,1},{25,9},{2,18},{10... | collective-permute-start | bytes 122888 | tf_op jit(solution)/shard_map/ppermute | solution.py:764
  85.7 4.4 %collective-permute-start.22 = (f32[16,640]{1,0:T(8,128)S(1)}, f32[16,640]{1,0:T(8,128)S(1)}, u32[]{:S(2)}, u32[]{:S(2)}) collective-permute-start(f32[16,640]{1,0:T(8,128)S(1)} %get-tuple-element.66.refs_10_), channel_id=1, source_target_pairs={{0,8},{8,0},{16,24},{24,16},{1,9},{9,1},{17,25},{25,17},{2,10},{10... | collective-permute-start | bytes 122888 | tf_op jit(solution)/shard_map/ppermute | solution.py:764
  97.2 4.7 %collective-permute-start.28 = (bf16[640,1920]{1,0:T(8,128)(2,1)S(1)}, bf16[640,1920]{1,0:T(8,128)(2,1)S(1)}, u32[]{:S(2)}, u32[]{:S(2)}) collective-permute-start(bf16[640,1920]{1,0:T(8,128)(2,1)S(1)} %get-tuple-element.77), channel_id=1, source_target_pairs={{0,1},{1,0},{2,3},{3,2},{4,5},{5,4},{6,7},{7,6},{8,9},{9,8},{10,11... | collective-permute-start | bytes 7372808 | tf_op jit(solution)/shard_map/ppermute | solution.py:764
  102.1 9.7 %collective-permute-start.29 = (bf16[80,1920]{1,0:T(8,128)(2,1)S(1)}, bf16[80,1920]{1,0:T(8,128)(2,1)S(1)}, u32[]{:S(2)}, u32[]{:S(2)}) collective-permute-start(bf16[80,1920]{1,0:T(8,128)(2,1)S(1)} %get-tuple-element.78), channel_id=1, source_target_pairs={{0,2},{1,3},{2,0},{3,1},{4,6},{5,7},{6,4},{7,5},{8,10},{9,11},{10,... | collective-permute-start | bytes 921608 | tf_op jit(solution)/shard_map/ppermute | solution.py:764
  103.6 9.0 %collective-permute-start.30 = (bf16[80,1920]{1,0:T(8,128)(2,1)S(1)}, bf16[80,1920]{1,0:T(8,128)(2,1)S(1)}, u32[]{:S(2)}, u32[]{:S(2)}) collective-permute-start(bf16[80,1920]{1,0:T(8,128)(2,1)S(1)} %get-tuple-element.79), channel_id=1, source_target_pairs={{0,4},{1,5},{2,6},{3,7},{4,0},{5,1},{6,2},{7,3},{8,12},{9,13},{10,... | collective-permute-start | bytes 921608 | tf_op jit(solution)/shard_map/ppermute | solution.py:764
  105.1 5.6 %collective-permute-start.27 = (f32[8,640]{1,0:T(8,128)S(1)}, f32[8,640]{1,0:T(8,128)S(1)}, u32[]{:S(2)}, u32[]{:S(2)}) collective-permute-start(f32[8,640]{1,0:T(8,128)S(1)} %get-tuple-element.75.refs_12_), channel_id=1, source_target_pairs={{0,24},{8,16},{16,8},{24,0},{1,25},{9,17},{17,9},{25,1},{2,26},{10... | collective-permute-start | bytes 61448 | tf_op jit(solution)/shard_map/ppermute | solution.py:764
  107.0 4.7 %collective-permute-start.26 = (f32[8,640]{1,0:T(8,128)S(1)}, f32[8,640]{1,0:T(8,128)S(1)}, u32[]{:S(2)}, u32[]{:S(2)}) collective-permute-start(f32[8,640]{1,0:T(8,128)S(1)} %get-tuple-element.75.refs_12_), channel_id=1, source_target_pairs={{0,16},{8,24},{16,0},{24,8},{1,17},{9,25},{17,1},{25,9},{2,18},{10... | collective-permute-start | bytes 61448 | tf_op jit(solution)/shard_map/ppermute | solution.py:764
  107.7 4.0 %collective-permute-start.25 = (f32[8,640]{1,0:T(8,128)S(1)}, f32[8,640]{1,0:T(8,128)S(1)}, u32[]{:S(2)}, u32[]{:S(2)}) collective-permute-start(f32[8,640]{1,0:T(8,128)S(1)} %get-tuple-element.75.refs_12_), channel_id=1, source_target_pairs={{0,8},{8,0},{16,24},{24,16},{1,9},{9,1},{17,25},{25,17},{2,10},{10... | collective-permute-start | bytes 61448 | tf_op jit(solution)/shard_map/ppermute | solution.py:764
  113.0 15.2 %collective-permute-start.32 = (bf16[160,1920]{1,0:T(8,128)(2,1)S(1)}, bf16[160,1920]{1,0:T(8,128)(2,1)S(1)}, u32[]{:S(2)}, u32[]{:S(2)}) collective-permute-start(bf16[160,1920]{1,0:T(8,128)(2,1)S(1)} %get-tuple-element.80.refs_16_), channel_id=1, source_target_pairs={{0,2},{1,3},{2,0},{3,1},{4,6},{5,7},{6,4},{7,5},{8,10},{9,11},{10,... | collective-permute-start | bytes 1843208 | tf_op jit(solution)/shard_map/ppermute | solution.py:764
  113.6 14.6 %collective-permute-start.33 = (bf16[160,1920]{1,0:T(8,128)(2,1)S(1)}, bf16[160,1920]{1,0:T(8,128)(2,1)S(1)}, u32[]{:S(2)}, u32[]{:S(2)}) collective-permute-start(bf16[160,1920]{1,0:T(8,128)(2,1)S(1)} %get-tuple-element.81.refs_17_), channel_id=1, source_target_pairs={{0,4},{1,5},{2,6},{3,7},{4,0},{5,1},{6,2},{7,3},{8,12},{9,13},{10,... | collective-permute-start | bytes 1843208 | tf_op jit(solution)/shard_map/ppermute | solution.py:764
  122.3 10.1 %collective-permute-start.36 = (bf16[656,896]{1,0:T(8,128)(2,1)S(1)}, bf16[656,896]{1,0:T(8,128)(2,1)S(1)}, u32[]{:S(2)}, u32[]{:S(2)}) collective-permute-start(bf16[656,896]{1,0:T(8,128)(2,1)S(1)} %get-tuple-element.90), channel_id=1, source_target_pairs={{0,1},{1,0},{2,3},{3,2},{4,5},{5,4},{6,7},{7,6},{8,9},{9,8},{10,11... | collective-permute-start | bytes 3526664 | tf_op jit(solution)/shard_map/ppermute | solution.py:764
  122.3 6.9 %collective-permute-start.31 = (bf16[656,1024]{1,0:T(8,128)(2,1)S(1)}, bf16[656,1024]{1,0:T(8,128)(2,1)S(1)}, u32[]{:S(2)}, u32[]{:S(2)}) collective-permute-start(bf16[656,1024]{1,0:T(8,128)(2,1)S(1)} %get-tuple-element.85), channel_id=1, source_target_pairs={{0,1},{1,0},{2,3},{3,2},{4,5},{5,4},{6,7},{7,6},{8,9},{9,8},{10,11... | collective-permute-start | bytes 4030472 | tf_op jit(solution)/shard_map/ppermute | solution.py:764
  129.4 11.3 %collective-permute-start.35 = (bf16[176,1024]{1,0:T(8,128)(2,1)S(1)}, bf16[176,1024]{1,0:T(8,128)(2,1)S(1)}, u32[]{:S(2)}, u32[]{:S(2)}) collective-permute-start(bf16[176,1024]{1,0:T(8,128)(2,1)S(1)} %get-tuple-element.88), channel_id=1, source_target_pairs={{0,4},{1,5},{2,6},{3,7},{4,0},{5,1},{6,2},{7,3},{8,12},{9,13},{10,... | collective-permute-start | bytes 1081352 | tf_op jit(solution)/shard_map/ppermute | solution.py:764
  131.0 11.3 %collective-permute-start.34 = (bf16[176,1024]{1,0:T(8,128)(2,1)S(1)}, bf16[176,1024]{1,0:T(8,128)(2,1)S(1)}, u32[]{:S(2)}, u32[]{:S(2)}) collective-permute-start(bf16[176,1024]{1,0:T(8,128)(2,1)S(1)} %get-tuple-element.87.refs_2_), channel_id=1, source_target_pairs={{0,2},{1,3},{2,0},{3,1},{4,6},{5,7},{6,4},{7,5},{8,10},{9,11},{10,... | collective-permute-start | bytes 1081352 | tf_op jit(solution)/shard_map/ppermute | solution.py:764
  132.6 20.5 %collective-permute-start.43 = (bf16[176,896]{1,0:T(8,128)(2,1)S(1)}, bf16[176,896]{1,0:T(8,128)(2,1)S(1)}, u32[]{:S(2)}, u32[]{:S(2)}) collective-permute-start(bf16[176,896]{1,0:T(8,128)(2,1)S(1)} %get-tuple-element.99), channel_id=1, source_target_pairs={{0,4},{1,5},{2,6},{3,7},{4,0},{5,1},{6,2},{7,3},{8,12},{9,13},{10,... | collective-permute-start | bytes 946184 | tf_op jit(solution)/shard_map/ppermute | solution.py:764
  133.3 19.8 %collective-permute-start.42 = (bf16[176,896]{1,0:T(8,128)(2,1)S(1)}, bf16[176,896]{1,0:T(8,128)(2,1)S(1)}, u32[]{:S(2)}, u32[]{:S(2)}) collective-permute-start(bf16[176,896]{1,0:T(8,128)(2,1)S(1)} %get-tuple-element.91.refs_4_), channel_id=1, source_target_pairs={{0,2},{1,3},{2,0},{3,1},{4,6},{5,7},{6,4},{7,5},{8,10},{9,11},{10,... | collective-permute-start | bytes 946184 | tf_op jit(solution)/shard_map/ppermute | solution.py:764
  142.4 8.6 %collective-permute-start.37 = (bf16[96,1024]{1,0:T(8,128)(2,1)S(1)}, bf16[96,1024]{1,0:T(8,128)(2,1)S(1)}, u32[]{:S(2)}, u32[]{:S(2)}) collective-permute-start(bf16[96,1024]{1,0:T(8,128)(2,1)S(1)} %get-tuple-element.92), channel_id=1, source_target_pairs={{0,2},{1,3},{2,0},{3,1},{4,6},{5,7},{6,4},{7,5},{8,10},{9,11},{10,... | collective-permute-start | bytes 589832 | tf_op jit(solution)/shard_map/ppermute | solution.py:764
  143.9 6.2 %collective-permute-start.38 = (bf16[80,1024]{1,0:T(8,128)(2,1)S(1)}, bf16[80,1024]{1,0:T(8,128)(2,1)S(1)}, u32[]{:S(2)}, u32[]{:S(2)}) collective-permute-start(bf16[80,1024]{1,0:T(8,128)(2,1)S(1)} %get-tuple-element.93), channel_id=1, source_target_pairs={{0,4},{1,5},{2,6},{3,7},{4,0},{5,1},{6,2},{7,3},{8,12},{9,13},{10,... | collective-permute-start | bytes 491528 | tf_op jit(solution)/shard_map/ppermute | solution.py:764
  144.5 11.8 %collective-permute-start.40 = (bf16[80,1920]{1,0:T(8,128)(2,1)S(1)}, bf16[80,1920]{1,0:T(8,128)(2,1)S(1)}, u32[]{:S(2)}, u32[]{:S(2)}) collective-permute-start(bf16[80,1920]{1,0:T(8,128)(2,1)S(1)} %get-tuple-element.96), channel_id=1, source_target_pairs={{0,8},{8,0},{16,24},{24,16},{1,9},{9,1},{17,25},{25,17},{2,10},{10... | collective-permute-start | bytes 921608 | tf_op jit(solution)/shard_map/ppermute | solution.py:764
  152.0 5.7 %collective-permute-start.39 = (bf16[96,1024]{1,0:T(8,128)(2,1)S(1)}, bf16[96,1024]{1,0:T(8,128)(2,1)S(1)}, u32[]{:S(2)}, u32[]{:S(2)}) collective-permute-start(bf16[96,1024]{1,0:T(8,128)(2,1)S(1)} %get-tuple-element.95), channel_id=1, source_target_pairs={{0,8},{8,0},{16,24},{24,16},{1,9},{9,1},{17,25},{25,17},{2,10},{10... | collective-permute-start | bytes 589832 | tf_op jit(solution)/shard_map/ppermute | solution.py:764
  153.2 6.8 %collective-permute-start.44 = (bf16[96,896]{1,0:T(8,128)(2,1)S(1)}, bf16[96,896]{1,0:T(8,128)(2,1)S(1)}, u32[]{:S(2)}, u32[]{:S(2)}) collective-permute-start(bf16[96,896]{1,0:T(8,128)(2,1)S(1)} %get-tuple-element.100), channel_id=1, source_target_pairs={{0,2},{1,3},{2,0},{3,1},{4,6},{5,7},{6,4},{7,5},{8,10},{9,11},{10,... | collective-permute-start | bytes 516104 | tf_op jit(solution)/shard_map/ppermute | solution.py:764
  154.8 5.3 %collective-permute-start.45 = (bf16[80,896]{1,0:T(8,128)(2,1)S(1)}, bf16[80,896]{1,0:T(8,128)(2,1)S(1)}, u32[]{:S(2)}, u32[]{:S(2)}) collective-permute-start(bf16[80,896]{1,0:T(8,128)(2,1)S(1)} %get-tuple-element.101), channel_id=1, source_target_pairs={{0,4},{1,5},{2,6},{3,7},{4,0},{5,1},{6,2},{7,3},{8,12},{9,13},{10,... | collective-permute-start | bytes 430088 | tf_op jit(solution)/shard_map/ppermute | solution.py:764
  158.4 9.8 %collective-permute-start.41 = (bf16[96,1024]{1,0:T(8,128)(2,1)S(1)}, bf16[96,1024]{1,0:T(8,128)(2,1)S(1)}, u32[]{:S(2)}, u32[]{:S(2)}) collective-permute-start(bf16[96,1024]{1,0:T(8,128)(2,1)S(1)} %get-tuple-element.98), channel_id=1, source_target_pairs={{0,16},{8,24},{16,0},{24,8},{1,17},{9,25},{17,1},{25,9},{2,18},{10... | collective-permute-start | bytes 589832 | tf_op jit(solution)/shard_map/ppermute | solution.py:764
  161.0 7.2 %collective-permute-start.46 = (bf16[96,896]{1,0:T(8,128)(2,1)S(1)}, bf16[96,896]{1,0:T(8,128)(2,1)S(1)}, u32[]{:S(2)}, u32[]{:S(2)}) collective-permute-start(bf16[96,896]{1,0:T(8,128)(2,1)S(1)} %get-tuple-element.103), channel_id=1, source_target_pairs={{0,8},{8,0},{16,24},{24,16},{1,9},{9,1},{17,25},{25,17},{2,10},{10... | collective-permute-start | bytes 516104 | tf_op jit(solution)/shard_map/ppermute | solution.py:764
  168.8 7.2 %collective-permute-start.47 = (bf16[96,896]{1,0:T(8,128)(2,1)S(1)}, bf16[96,896]{1,0:T(8,128)(2,1)S(1)}, u32[]{:S(2)}, u32[]{:S(2)}) collective-permute-start(bf16[96,896]{1,0:T(8,128)(2,1)S(1)} %get-tuple-element.105), channel_id=1, source_target_pairs={{0,16},{8,24},{16,0},{24,8},{1,17},{9,25},{17,1},{25,9},{2,18},{10... | collective-permute-start | bytes 516104 | tf_op jit(solution)/shard_map/ppermute | solution.py:764
  (3 other events, 19.2 us)

commit v4 on v3

--- a/solution.py
+++ b/solution.py
@@ -13,7 +13,7 @@
 SUBS = 8
 BIAS_ROWS = 16
 COST = 100
-UNROLL = 32
+UNROLL = 64
 LIMITS = (14, 16, 16, 12, 16, 12)
 ANY = pl.BlockSpec(memory_space=pl.ANY)
 HBM = pl.BlockSpec(memory_space=pltpu.HBM)

time: 178 us -> 177 us (level)
  transfers between devices with their start and end apart: 48 -> 48, of which waited for: 25 -> 26; matrix products, arithmetic and copies ran while one was open for 3% -> 3% of each run, Pallas kernels for 14% -> 14%
where the time goes in v4:
time: 177 us; the launch traced here: 176 us
  waiting for transfers between devices  71.8 us (41%)
  starting transfers between devices  50.6 us (29%)
  Pallas kernels  47.1 us (27%)
  local copies, waits for them, and re-layouts  5.65 us (3%)
    ppermute x42, waiting for transfers between devices, swap(): return lax.ppermute(value, axis, pairs)  50.6 us
    ppermute x42, starting transfers between devices, swap(): return lax.ppermute(value, axis, pairs)  42.1 us
    ppermute x6, waiting for transfers between devices, moved(): lax.ppermute(value, axis, [(index, target(index)) for index in range(lax....  21.2 us
    pallas_call x20, Pallas kernels, small_call(): call(kernel, outs, specs + [ANY] * len(ties), [VMEM] * len(outs), list(sc...  10.6 us
    ppermute x6, starting transfers between devices, moved(): lax.ppermute(value, axis, [(index, target(index)) for index in range(lax....  8.53 us
    pallas_call x1, Pallas kernels, per_device(): call(functools.partial(second_backward_kernel, rows, quick), [half, wide,...  7.15 us
    pallas_call x1, Pallas kernels, per_device(): call(functools.partial(second_forward_kernel, plan, block), [shape(tiles,...  7.1 us
    pallas_call x1, Pallas kernels, per_device(): call(functools.partial(first_backward_kernel, rows, quick), [wide, wide,...  6.73 us
  transfers between devices with their start and end apart: 48, of which 26 were waited for; matrix products, arithmetic and copies ran while one was open for 3% of the time, Pallas kernels for 14%

profile of v4, /device:TPU:0, one launch (start us, length us, event | category | flops | bytes accessed | tf_op | source)
XLA Modules:
  0.0 176.4 jit_solution(15368423574485508008)
XLA Ops:
  0.7 4.1 %collective-permute-start.9 = (bf16[80,1920]{1,0:T(8,128)(2,1)}, bf16[80,1920]{1,0:T(8,128)(2,1)S(1)}, u32[]{:S(2)}, u32[]{:S(2)}) collective-permute-start(bf16[80,1920]{1,0:T(8,128)(2,1)} %bitcast.46), channel_id=1, source_target_pairs={{0,16},{8,24},{16,0},{24,8},{1,17},{9,25},{17,1},{25,9},{2,18},{10... | collective-permute-start | bytes 921608 | tf_op jit(solution)/shard_map/ppermute | solution.py:764
  4.8 1.6 collective-permute-start.3
  6.4 1.4 constant_dynamic-slice_fusion
  8.7 1.4 collective-permute-start.1
  12.0 7.1 %collective-permute-done.3.own = bf16[80,1920]{1,0:T(8,128)(2,1)S(1)} collective-permute-done((bf16[80,1920]{1,0:T(8,128)(2,1)}, bf16[80,1920]{1,0:T(8,128)(2,1)S(1)}, u32[]{:S(2)}, u32[]{:S(2)}) %collective-permute-start.3) | collective-permute-done | bytes 307232 | tf_op jit(solution)/shard_map/ppermute | solution.py:764
  20.2 1.6 collective-permute-start.13
  22.3 1.4 collective-permute-start.5
  24.0 5.9 %collective-permute-done.13.own = bf16[80,1920]{1,0:T(8,128)(2,1)S(1)} collective-permute-done((bf16[80,1920]{1,0:T(8,128)(2,1)S(1)}, bf16[80,1920]{1,0:T(8,128)(2,1)S(1)}, u32[]{:S(2)}, u32[]{:S(2)}) %collective-permute-start.13) | collective-permute-done | bytes 307232 | tf_op jit(solution)/shard_map/ppermute | solution.py:764
  30.5 1.7 collective-permute-start.11
  35.1 1.3 collective-permute-start.7
  36.4 3.7 %collective-permute-done.11.first.refs_14_.refs_20_.refs_12_ = bf16[160,1920]{1,0:T(8,128)(2,1)S(1)} collective-permute-done((bf16[160,1920]{1,0:T(8,128)(2,1)S(1)}, bf16[160,1920]{1,0:T(8,128)(2,1)S(1)}, u32[]{:S(2)}, u32[]{:S(2)}) %collective-permute-start.11) | collective-permute-done | bytes 614432 | tf_op jit(solution)/shard_map/ppermute | solution.py:768
  40.1 6.6 %collective-permute-done.15.second.refs_17_.refs_23_.refs_15_ = bf16[160,1920]{1,0:T(8,128)(2,1)S(1)} collective-permute-done((bf16[160,1920]{1,0:T(8,128)(2,1)S(1)}, bf16[160,1920]{1,0:T(8,128)(2,1)S(1)}, u32[]{:S(2)}, u32[]{:S(2)}) %collective-permute-start.15) | collective-permute-done | bytes 614432 | tf_op jit(solution)/shard_map/ppermute | solution.py:768
  47.3 1.6 collective-permute-start.17
  49.7 4.3 %collective-permute-done.7.refs_11_.refs_17_.refs_9_ = bf16[160,1920]{1,0:T(8,128)(2,1)S(1)} collective-permute-done((bf16[160,1920]{1,0:T(8,128)(2,1)S(1)}, bf16[160,1920]{1,0:T(8,128)(2,1)S(1)}, u32[]{:S(2)}, u32[]{:S(2)}) %collective-permute-start.7) | collective-permute-done | bytes 614432 | tf_op jit(solution)/shard_map/ppermute | solution.py:768
  54.0 6.6 %collective-permute-done.17.refs_19_.refs_25_.refs_17_ = bf16[160,1920]{1,0:T(8,128)(2,1)S(1)} collective-permute-done((bf16[160,1920]{1,0:T(8,128)(2,1)S(1)}, bf16[160,1920]{1,0:T(8,128)(2,1)S(1)}, u32[]{:S(2)}, u32[]{:S(2)}) %collective-permute-start.17) | collective-permute-done | bytes 614432 | tf_op jit(solution)/shard_map/ppermute | solution.py:768
  60.6 2.0 %collective-permute-done.18.refs_20_.refs_26_.refs_18_ = bf16[160,1920]{1,0:T(8,128)(2,1)S(1)} collective-permute-done((bf16[160,1920]{1,0:T(8,128)(2,1)S(1)}, bf16[160,1920]{1,0:T(8,128)(2,1)S(1)}, u32[]{:S(2)}, u32[]{:S(2)}) %collective-permute-start.18) | collective-permute-done | bytes 614432 | tf_op jit(solution)/shard_map/ppermute | solution.py:764
  62.6 5.7 %first_forward.1 = (f32[5,512,128]{2,1,0:T(8,128)S(1)}, f32[5,512,128]{2,1,0:T(8,128)S(1)}, f32[5,512,128]{2,1,0:T(8,128)S(1)}, f32[8,640]{1,0:T(8,128)S(1)}) custom-call(s32[2]{0:T(128)S(1)} %pad_add_fusion.refs_0_.place, bf16[512,640]{1,0:T(8,128)(2,1)S(1)} %bitcast.42, bf16[512,640]{1,0:T(8,128)(2,1)S(1)} %before.1.refs_1_.refs_2_.refs_7_, ...), custom_call_target="tpu_custom_call" | custom-call | flops 25165824 | bytes 147456 | tf_op jit(solution)/shard_map/first_forward/pallas_call | solution.py:947
  68.3 1.7 collective-permute-start.21
  70.0 1.3 collective-permute-start.20
  71.3 1.4 collective-permute-start.19
  72.7 1.3 collective-permute-done.21.refs_10_
  75.1 7.1 %second_forward.1 = (f32[5,520,128]{2,1,0:T(8,128)S(1)}, bf16[512,640]{1,0:T(8,128)(2,1)S(1)}, bf16[512,640]{1,0:T(8,128)(2,1)S(1)}, f32[8,640]{1,0:T(8,128)S(1)...) custom-call(s32[2]{0:T(128)S(1)} %pad_add_fusion.refs_0_.place, ...), custom_call_target="tpu_custom_call" | custom-call | flops 25165824 | bytes 114688 | tf_op jit(solution)/shard_map/second_forward/pallas_call | solution.py:959
  82.2 1.9 %collective-permute-start.24 = (f32[16,640]{1,0:T(8,128)S(1)}, f32[16,640]{1,0:T(8,128)S(1)}, u32[]{:S(2)}, u32[]{:S(2)}) collective-permute-start(f32[16,640]{1,0:T(8,128)S(1)} %get-tuple-element.66.refs_10_), channel_id=1, source_target_pairs={{0,24},{8,16},{16,8},{24,0},{1,25},{9,17},{17,9},{25,1},{2,26},{10... | collective-permute-start | bytes 122888 | tf_op jit(solution)/shard_map/ppermute | solution.py:764
  85.2 1.5 collective-permute-start.22
  86.6 1.5 collective-permute-done.24.refs_13_
  89.5 7.2 %second_backward.1 = (bf16[512,640]{1,0:T(8,128)(2,1)S(1)}, bf16[512,1920]{1,0:T(8,128)(2,1)S(1)}, bf16[512,1920]{1,0:T(8,128)(2,1)S(1)}, f32[8,1920]{1,0:T(8,12...) custom-call(s32[2]{0:T(128)S(1)} %pad_add_fusion.refs_0_.place, ...), custom_call_target="tpu_custom_call" | custom-call | flops 25165824 | bytes 147456 | tf_op jit(solution)/shard_map/second_backward/pallas_call | solution.py:988
  96.8 4.2 %middle.1 = (bf16[512,640]{1,0:T(8,128)(2,1)S(1)}, f32[8,640]{1,0:T(8,128)S(1)}) custom-call(s32[2]{0:T(128)S(1)} %pad_add_fusion.refs_0_.place, bf16[512,1920]{1,0:T(8,128)(2,1)S(1)} %get-tuple-element.70.refs_1_, bf16[512,1920]{1,0:T(8,128)(2,1)S(1)} %get-tuple-element.71.refs_2_, f32[5,512,128]{2,1,0:T(8,128)S(1)} %get-tuple-element.57.refs_1_.refs_3_, ...), custom_call_target="tpu_custom_call" | custom-call | flops 25165824 | bytes 114688 | tf_op jit(solution)/shard_map/middle/pallas_call | solution.py:1003
  101.6 1.6 collective-permute-start.29
  103.2 1.5 collective-permute-start.30
  104.7 1.9 %collective-permute-start.27 = (f32[8,640]{1,0:T(8,128)S(1)}, f32[8,640]{1,0:T(8,128)S(1)}, u32[]{:S(2)}, u32[]{:S(2)}) collective-permute-start(f32[8,640]{1,0:T(8,128)S(1)} %get-tuple-element.75.refs_12_), channel_id=1, source_target_pairs={{0,24},{8,16},{16,8},{24,0},{1,25},{9,17},{17,9},{25,1},{2,26},{10... | collective-permute-start | bytes 61448 | tf_op jit(solution)/shard_map/ppermute | solution.py:764
  107.2 1.8 %collective-permute-start.25 = (f32[8,640]{1,0:T(8,128)S(1)}, f32[8,640]{1,0:T(8,128)S(1)}, u32[]{:S(2)}, u32[]{:S(2)}) collective-permute-start(f32[8,640]{1,0:T(8,128)S(1)} %get-tuple-element.75.refs_12_), channel_id=1, source_target_pairs={{0,8},{8,0},{16,24},{24,16},{1,9},{9,1},{17,25},{25,17},{2,10},{10... | collective-permute-start | bytes 61448 | tf_op jit(solution)/shard_map/ppermute | solution.py:764
  109.1 1.2 collective-permute-done.27.refs_6_.refs_15_
  113.2 1.5 collective-permute-start.33
  114.7 6.7 %first_backward.1 = (bf16[512,1920]{1,0:T(8,128)(2,1)S(1)}, bf16[512,1920]{1,0:T(8,128)(2,1)S(1)}, f32[16,1920]{1,0:T(8,128)}, bf16[656,1024]{1,0:T(8,128)(2,1)S...) custom-call(s32[2]{0:T(128)S(1)} %pad_add_fusion.refs_0_.place, ...), custom_call_target="tpu_custom_call" | custom-call | flops 25165824 | bytes 147456 | tf_op jit(solution)/shard_map/first_backward/pallas_call | solution.py:1025
  121.9 5.7 %last.1.refs_7_ = f32[512,640]{1,0:T(8,128)S(1)} custom-call(s32[2]{0:T(128)S(1)} %pad_add_fusion.refs_0_.place, bf16[512,1920]{1,0:T(8,128)(2,1)S(1)} %get-tuple-element.82.refs_1_, bf16[512,1920]{1,0:T(8,128)(2,1)S(1)} %get-tuple-element.83.refs_2_, bf16[160,1920]{1,0:T(8,128)(2,1)S(1)} %join.4.refs_5_.refs_11_.refs_3_, ...), custom_call_target="tpu_custom_call" | custom-call | flops 2516582400 | bytes 4915200 | tf_op jit(solution)/shard_map/last/pallas_call | solution.py:1039
  128.9 1.6 collective-permute-start.35
  130.5 1.4 collective-permute-start.34
  133.3 6.9 %collective-permute-done.35.refs_3_.refs_6_ = bf16[176,1024]{1,0:T(8,128)(2,1)S(1)} collective-permute-done((bf16[176,1024]{1,0:T(8,128)(2,1)S(1)}, bf16[176,1024]{1,0:T(8,128)(2,1)S(1)}, u32[]{:S(2)}, u32[]{:S(2)}) %collective-permute-start.35) | collective-permute-done | bytes 360480 | tf_op jit(solution)/shard_map/ppermute | solution.py:764
  140.3 1.6 collective-permute-done.34.refs_2_.refs_5_
  142.0 1.5 collective-permute-start.37
  145.0 4.5 %collective-permute-done.38.refs_4_ = bf16[80,1024]{1,0:T(8,128)(2,1)S(1)} collective-permute-done((bf16[80,1024]{1,0:T(8,128)(2,1)S(1)}, bf16[80,1024]{1,0:T(8,128)(2,1)S(1)}, u32[]{:S(2)}, u32[]{:S(2)}) %collective-permute-start.38) | collective-permute-done | bytes 163872 | tf_op jit(solution)/shard_map/ppermute | solution.py:764
  152.6 1.6 collective-permute-start.44
  154.2 1.5 collective-permute-start.45
  155.8 1.3 collective-permute-done.39.refs_2_
  157.8 1.7 collective-permute-start.41
  161.4 6.2 %collective-permute-done.46.refs_2_ = bf16[96,896]{1,0:T(8,128)(2,1)S(1)} collective-permute-done((bf16[96,896]{1,0:T(8,128)(2,1)S(1)}, bf16[96,896]{1,0:T(8,128)(2,1)S(1)}, u32[]{:S(2)}, u32[]{:S(2)}) %collective-permute-start.46) | collective-permute-done | bytes 172064 | tf_op jit(solution)/shard_map/ppermute | solution.py:764
  169.2 1.3 copy.16
  170.5 4.9 %collective-permute-done.47.refs_3_ = bf16[96,896]{1,0:T(8,128)(2,1)S(1)} collective-permute-done((bf16[96,896]{1,0:T(8,128)(2,1)S(1)}, bf16[96,896]{1,0:T(8,128)(2,1)S(1)}, u32[]{:S(2)}, u32[]{:S(2)}) %collective-permute-start.47) | collective-permute-done | bytes 172064 | tf_op jit(solution)/shard_map/ppermute | solution.py:764
  (98 shorter events, 30.6 us)
Async XLA Ops:
  0.7 19.5 %collective-permute-start.9 = (bf16[80,1920]{1,0:T(8,128)(2,1)}, bf16[80,1920]{1,0:T(8,128)(2,1)S(1)}, u32[]{:S(2)}, u32[]{:S(2)}) collective-permute-start(bf16[80,1920]{1,0:T(8,128)(2,1)} %bitcast.46), channel_id=1, source_target_pairs={{0,16},{8,24},{16,0},{24,8},{1,17},{9,25},{17,1},{25,9},{2,18},{10... | collective-permute-start | bytes 921608 | tf_op jit(solution)/shard_map/ppermute | solution.py:764
  4.8 14.4 %collective-permute-start.3 = (bf16[80,1920]{1,0:T(8,128)(2,1)}, bf16[80,1920]{1,0:T(8,128)(2,1)S(1)}, u32[]{:S(2)}, u32[]{:S(2)}) collective-permute-start(bf16[80,1920]{1,0:T(8,128)(2,1)} %bitcast.47), channel_id=1, source_target_pairs={{0,8},{8,0},{16,24},{24,16},{1,9},{9,1},{17,25},{25,17},{2,10},{10... | collective-permute-start | bytes 921608 | tf_op jit(solution)/shard_map/ppermute | solution.py:764
  6.3 1.8 %collective-permute-start = (bf16[80,1920]{1,0:T(8,128)(2,1)}, bf16[80,1920]{1,0:T(8,128)(2,1)S(1)}, u32[]{:S(2)}, u32[]{:S(2)}) collective-permute-start(bf16[80,1920]{1,0:T(8,128)(2,1)} %bitcast.48), channel_id=1, source_target_pairs={{0,1},{1,0},{2,3},{3,2},{4,5},{5,4},{6,7},{7,6},{8,9},{9,8},{10,11... | collective-permute-start | bytes 921608 | tf_op jit(solution)/shard_map/ppermute | solution.py:764
  8.7 13.0 %collective-permute-start.1 = (bf16[160,1920]{1,0:T(8,128)(2,1)S(1)}, bf16[160,1920]{1,0:T(8,128)(2,1)S(1)}, u32[]{:S(2)}, u32[]{:S(2)}) collective-permute-start(bf16[160,1920]{1,0:T(8,128)(2,1)S(1)} %join.4.refs_5_.refs_11_.refs_3_), channel_id=1, source_target_pairs={{0,3},{1,4},{2,1},{3,6},{4,7},{5,0},{6,5},{7,2},{8,11},{9,12},{10,... | collective-permute-start | bytes 1843208 | tf_op jit(solution)/shard_map/ppermute | solution.py:768
  19.1 2.6 %collective-permute-start.4 = (bf16[80,1920]{1,0:T(8,128)(2,1)S(1)}, bf16[80,1920]{1,0:T(8,128)(2,1)S(1)}, u32[]{:S(2)}, u32[]{:S(2)}) collective-permute-start(bf16[80,1920]{1,0:T(8,128)(2,1)S(1)} %collective-permute-done.3.own), channel_id=1, source_target_pairs={{0,1},{1,0},{2,3},{3,2},{4,5},{5,4},{6,7},{7,6},{8,9},{9,8},{10,11... | collective-permute-start | bytes 921608 | tf_op jit(solution)/shard_map/ppermute | solution.py:764
  20.2 9.7 %collective-permute-start.13 = (bf16[80,1920]{1,0:T(8,128)(2,1)S(1)}, bf16[80,1920]{1,0:T(8,128)(2,1)S(1)}, u32[]{:S(2)}, u32[]{:S(2)}) collective-permute-start(bf16[80,1920]{1,0:T(8,128)(2,1)S(1)} %collective-permute-done.9.own), channel_id=1, source_target_pairs={{0,8},{8,0},{16,24},{24,16},{1,9},{9,1},{17,25},{25,17},{2,10},{10... | collective-permute-start | bytes 921608 | tf_op jit(solution)/shard_map/ppermute | solution.py:764
  22.3 9.9 %collective-permute-start.5 = (bf16[160,1920]{1,0:T(8,128)(2,1)S(1)}, bf16[160,1920]{1,0:T(8,128)(2,1)S(1)}, u32[]{:S(2)}, u32[]{:S(2)}) collective-permute-start(bf16[160,1920]{1,0:T(8,128)(2,1)S(1)} %join.5.refs_8_.refs_14_.refs_6_), channel_id=1, source_target_pairs={{0,3},{1,4},{2,1},{3,6},{4,7},{5,0},{6,5},{7,2},{8,11},{9,12},{10,... | collective-permute-start | bytes 1843208 | tf_op jit(solution)/shard_map/ppermute | solution.py:768
  23.7 6.2 %collective-permute-start.10 = (bf16[80,1920]{1,0:T(8,128)(2,1)S(1)}, bf16[80,1920]{1,0:T(8,128)(2,1)S(1)}, u32[]{:S(2)}, u32[]{:S(2)}) collective-permute-start(bf16[80,1920]{1,0:T(8,128)(2,1)S(1)} %collective-permute-done.9.own), channel_id=1, source_target_pairs={{0,1},{1,0},{2,3},{3,2},{4,5},{5,4},{6,7},{7,6},{8,9},{9,8},{10,11... | collective-permute-start | bytes 921608 | tf_op jit(solution)/shard_map/ppermute | solution.py:764
  29.9 2.3 %collective-permute-start.14 = (bf16[80,1920]{1,0:T(8,128)(2,1)S(1)}, bf16[80,1920]{1,0:T(8,128)(2,1)S(1)}, u32[]{:S(2)}, u32[]{:S(2)}) collective-permute-start(bf16[80,1920]{1,0:T(8,128)(2,1)S(1)} %collective-permute-done.13.own), channel_id=1, source_target_pairs={{0,1},{1,0},{2,3},{3,2},{4,5},{5,4},{6,7},{7,6},{8,9},{9,8},{10,11... | collective-permute-start | bytes 921608 | tf_op jit(solution)/shard_map/ppermute | solution.py:764
  30.5 9.6 %collective-permute-start.11 = (bf16[160,1920]{1,0:T(8,128)(2,1)S(1)}, bf16[160,1920]{1,0:T(8,128)(2,1)S(1)}, u32[]{:S(2)}, u32[]{:S(2)}) collective-permute-start(bf16[160,1920]{1,0:T(8,128)(2,1)S(1)} %join.6.refs_13_.refs_19_.refs_11_), channel_id=1, source_target_pairs={{0,3},{1,4},{2,1},{3,6},{4,7},{5,0},{6,5},{7,2},{8,11},{9,12},{10,... | collective-permute-start | bytes 1843208 | tf_op jit(solution)/shard_map/ppermute | solution.py:768
  32.8 13.9 %collective-permute-start.15 = (bf16[160,1920]{1,0:T(8,128)(2,1)S(1)}, bf16[160,1920]{1,0:T(8,128)(2,1)S(1)}, u32[]{:S(2)}, u32[]{:S(2)}) collective-permute-start(bf16[160,1920]{1,0:T(8,128)(2,1)S(1)} %join.7.refs_16_.refs_22_.refs_14_), channel_id=1, source_target_pairs={{0,3},{1,4},{2,1},{3,6},{4,7},{5,0},{6,5},{7,2},{8,11},{9,12},{10,... | collective-permute-start | bytes 1843208 | tf_op jit(solution)/shard_map/ppermute | solution.py:768
  34.0 15.4 %collective-permute-start.2 = (bf16[160,1920]{1,0:T(8,128)(2,1)S(1)}, bf16[160,1920]{1,0:T(8,128)(2,1)S(1)}, u32[]{:S(2)}, u32[]{:S(2)}) collective-permute-start(bf16[160,1920]{1,0:T(8,128)(2,1)S(1)} %collective-permute-done.1.refs_0_.first.refs_6_.refs_12_.refs_4_), channel_id=1, source_target_pairs={{0,1},{1,0},{2,3},{3,2},{4,5},{5,4},{6,7},{7,6},{8,9},{9,8},{10,11... | collective-permute-start | bytes 1843208 | tf_op jit(solution)/shard_map/ppermute | solution.py:764
  35.1 18.9 %collective-permute-start.7 = (bf16[160,1920]{1,0:T(8,128)(2,1)S(1)}, bf16[160,1920]{1,0:T(8,128)(2,1)S(1)}, u32[]{:S(2)}, u32[]{:S(2)}) collective-permute-start(bf16[160,1920]{1,0:T(8,128)(2,1)S(1)} %pick.2), channel_id=1, source_target_pairs={{0,2},{1,5},{2,0},{3,7},{4,6},{5,1},{6,4},{7,3},{8,10},{9,13},{10,... | collective-permute-start | bytes 1843208 | tf_op jit(solution)/shard_map/ppermute | solution.py:768
  47.3 13.2 %collective-permute-start.17 = (bf16[160,1920]{1,0:T(8,128)(2,1)S(1)}, bf16[160,1920]{1,0:T(8,128)(2,1)S(1)}, u32[]{:S(2)}, u32[]{:S(2)}) collective-permute-start(bf16[160,1920]{1,0:T(8,128)(2,1)S(1)} %pick.3), channel_id=1, source_target_pairs={{0,2},{1,5},{2,0},{3,7},{4,6},{5,1},{6,4},{7,3},{8,10},{9,13},{10,... | collective-permute-start | bytes 1843208 | tf_op jit(solution)/shard_map/ppermute | solution.py:768
  48.9 11.7 %collective-permute-start.12 = (bf16[160,1920]{1,0:T(8,128)(2,1)S(1)}, bf16[160,1920]{1,0:T(8,128)(2,1)S(1)}, u32[]{:S(2)}, u32[]{:S(2)}) collective-permute-start(bf16[160,1920]{1,0:T(8,128)(2,1)S(1)} %collective-permute-done.11.first.refs_14_.refs_20_.refs_12_), channel_id=1, source_target_pairs={{0,1},{1,0},{2,3},{3,2},{4,5},{5,4},{6,7},{7,6},{8,9},{9,8},{10,11... | collective-permute-start | bytes 1843208 | tf_op jit(solution)/shard_map/ppermute | solution.py:764
  49.2 11.4 %collective-permute-start.6 = (bf16[160,1920]{1,0:T(8,128)(2,1)S(1)}, bf16[160,1920]{1,0:T(8,128)(2,1)S(1)}, u32[]{:S(2)}, u32[]{:S(2)}) collective-permute-start(bf16[160,1920]{1,0:T(8,128)(2,1)S(1)} %collective-permute-done.5.second.refs_0_.refs_9_.refs_15_.refs_7_), channel_id=1, source_target_pairs={{0,1},{1,0},{2,3},{3,2},{4,5},{5,4},{6,7},{7,6},{8,9},{9,8},{10,11... | collective-permute-start | bytes 1843208 | tf_op jit(solution)/shard_map/ppermute | solution.py:764
  49.5 11.2 %collective-permute-start.16 = (bf16[160,1920]{1,0:T(8,128)(2,1)S(1)}, bf16[160,1920]{1,0:T(8,128)(2,1)S(1)}, u32[]{:S(2)}, u32[]{:S(2)}) collective-permute-start(bf16[160,1920]{1,0:T(8,128)(2,1)S(1)} %collective-permute-done.15.second.refs_17_.refs_23_.refs_15_), channel_id=1, source_target_pairs={{0,1},{1,0},{2,3},{3,2},{4,5},{5,4},{6,7},{7,6},{8,9},{9,8},{10,11... | collective-permute-start | bytes 1843208 | tf_op jit(solution)/shard_map/ppermute | solution.py:764
  54.0 6.6 %collective-permute-start.8 = (bf16[160,1920]{1,0:T(8,128)(2,1)S(1)}, bf16[160,1920]{1,0:T(8,128)(2,1)S(1)}, u32[]{:S(2)}, u32[]{:S(2)}) collective-permute-start(bf16[160,1920]{1,0:T(8,128)(2,1)S(1)} %collective-permute-done.7.refs_11_.refs_17_.refs_9_), channel_id=1, source_target_pairs={{0,1},{1,0},{2,3},{3,2},{4,5},{5,4},{6,7},{7,6},{8,9},{9,8},{10,11... | collective-permute-start | bytes 1843208 | tf_op jit(solution)/shard_map/ppermute | solution.py:764
  60.6 2.0 %collective-permute-start.18 = (bf16[160,1920]{1,0:T(8,128)(2,1)S(1)}, bf16[160,1920]{1,0:T(8,128)(2,1)S(1)}, u32[]{:S(2)}, u32[]{:S(2)}) collective-permute-start(bf16[160,1920]{1,0:T(8,128)(2,1)S(1)} %collective-permute-done.17.refs_19_.refs_25_.refs_17_), channel_id=1, source_target_pairs={{0,1},{1,0},{2,3},{3,2},{4,5},{5,4},{6,7},{7,6},{8,9},{9,8},{10,11... | collective-permute-start | bytes 1843208 | tf_op jit(solution)/shard_map/ppermute | solution.py:764
  68.3 5.8 %collective-permute-start.21 = (f32[8,640]{1,0:T(8,128)S(1)}, f32[8,640]{1,0:T(8,128)S(1)}, u32[]{:S(2)}, u32[]{:S(2)}) collective-permute-start(f32[8,640]{1,0:T(8,128)S(1)} %get-tuple-element.60.refs_7_), channel_id=1, source_target_pairs={{0,24},{8,16},{16,8},{24,0},{1,25},{9,17},{17,9},{25,1},{2,26},{10... | collective-permute-start | bytes 61448 | tf_op jit(solution)/shard_map/ppermute | solution.py:764
  70.0 4.7 %collective-permute-start.20 = (f32[8,640]{1,0:T(8,128)S(1)}, f32[8,640]{1,0:T(8,128)S(1)}, u32[]{:S(2)}, u32[]{:S(2)}) collective-permute-start(f32[8,640]{1,0:T(8,128)S(1)} %get-tuple-element.60.refs_7_), channel_id=1, source_target_pairs={{0,16},{8,24},{16,0},{24,8},{1,17},{9,25},{17,1},{25,9},{2,18},{10... | collective-permute-start | bytes 61448 | tf_op jit(solution)/shard_map/ppermute | solution.py:764
  71.3 3.8 %collective-permute-start.19 = (f32[8,640]{1,0:T(8,128)S(1)}, f32[8,640]{1,0:T(8,128)S(1)}, u32[]{:S(2)}, u32[]{:S(2)}) collective-permute-start(f32[8,640]{1,0:T(8,128)S(1)} %get-tuple-element.60.refs_7_), channel_id=1, source_target_pairs={{0,8},{8,0},{16,24},{24,16},{1,9},{9,1},{17,25},{25,17},{2,10},{10... | collective-permute-start | bytes 61448 | tf_op jit(solution)/shard_map/ppermute | solution.py:764
  82.2 6.0 %collective-permute-start.24 = (f32[16,640]{1,0:T(8,128)S(1)}, f32[16,640]{1,0:T(8,128)S(1)}, u32[]{:S(2)}, u32[]{:S(2)}) collective-permute-start(f32[16,640]{1,0:T(8,128)S(1)} %get-tuple-element.66.refs_10_), channel_id=1, source_target_pairs={{0,24},{8,16},{16,8},{24,0},{1,25},{9,17},{17,9},{25,1},{2,26},{10... | collective-permute-start | bytes 122888 | tf_op jit(solution)/shard_map/ppermute | solution.py:764
  84.1 5.0 %collective-permute-start.23 = (f32[16,640]{1,0:T(8,128)S(1)}, f32[16,640]{1,0:T(8,128)S(1)}, u32[]{:S(2)}, u32[]{:S(2)}) collective-permute-start(f32[16,640]{1,0:T(8,128)S(1)} %get-tuple-element.66.refs_10_), channel_id=1, source_target_pairs={{0,16},{8,24},{16,0},{24,8},{1,17},{9,25},{17,1},{25,9},{2,18},{10... | collective-permute-start | bytes 122888 | tf_op jit(solution)/shard_map/ppermute | solution.py:764
  85.2 4.4 %collective-permute-start.22 = (f32[16,640]{1,0:T(8,128)S(1)}, f32[16,640]{1,0:T(8,128)S(1)}, u32[]{:S(2)}, u32[]{:S(2)}) collective-permute-start(f32[16,640]{1,0:T(8,128)S(1)} %get-tuple-element.66.refs_10_), channel_id=1, source_target_pairs={{0,8},{8,0},{16,24},{24,16},{1,9},{9,1},{17,25},{25,17},{2,10},{10... | collective-permute-start | bytes 122888 | tf_op jit(solution)/shard_map/ppermute | solution.py:764
  96.7 4.7 %collective-permute-start.28 = (bf16[640,1920]{1,0:T(8,128)(2,1)S(1)}, bf16[640,1920]{1,0:T(8,128)(2,1)S(1)}, u32[]{:S(2)}, u32[]{:S(2)}) collective-permute-start(bf16[640,1920]{1,0:T(8,128)(2,1)S(1)} %get-tuple-element.77), channel_id=1, source_target_pairs={{0,1},{1,0},{2,3},{3,2},{4,5},{5,4},{6,7},{7,6},{8,9},{9,8},{10,11... | collective-permute-start | bytes 7372808 | tf_op jit(solution)/shard_map/ppermute | solution.py:764
  101.6 9.6 %collective-permute-start.29 = (bf16[80,1920]{1,0:T(8,128)(2,1)S(1)}, bf16[80,1920]{1,0:T(8,128)(2,1)S(1)}, u32[]{:S(2)}, u32[]{:S(2)}) collective-permute-start(bf16[80,1920]{1,0:T(8,128)(2,1)S(1)} %get-tuple-element.78), channel_id=1, source_target_pairs={{0,2},{1,3},{2,0},{3,1},{4,6},{5,7},{6,4},{7,5},{8,10},{9,11},{10,... | collective-permute-start | bytes 921608 | tf_op jit(solution)/shard_map/ppermute | solution.py:764
  103.2 9.0 %collective-permute-start.30 = (bf16[80,1920]{1,0:T(8,128)(2,1)S(1)}, bf16[80,1920]{1,0:T(8,128)(2,1)S(1)}, u32[]{:S(2)}, u32[]{:S(2)}) collective-permute-start(bf16[80,1920]{1,0:T(8,128)(2,1)S(1)} %get-tuple-element.79), channel_id=1, source_target_pairs={{0,4},{1,5},{2,6},{3,7},{4,0},{5,1},{6,2},{7,3},{8,12},{9,13},{10,... | collective-permute-start | bytes 921608 | tf_op jit(solution)/shard_map/ppermute | solution.py:764
  104.7 5.6 %collective-permute-start.27 = (f32[8,640]{1,0:T(8,128)S(1)}, f32[8,640]{1,0:T(8,128)S(1)}, u32[]{:S(2)}, u32[]{:S(2)}) collective-permute-start(f32[8,640]{1,0:T(8,128)S(1)} %get-tuple-element.75.refs_12_), channel_id=1, source_target_pairs={{0,24},{8,16},{16,8},{24,0},{1,25},{9,17},{17,9},{25,1},{2,26},{10... | collective-permute-start | bytes 61448 | tf_op jit(solution)/shard_map/ppermute | solution.py:764
  106.5 4.7 %collective-permute-start.26 = (f32[8,640]{1,0:T(8,128)S(1)}, f32[8,640]{1,0:T(8,128)S(1)}, u32[]{:S(2)}, u32[]{:S(2)}) collective-permute-start(f32[8,640]{1,0:T(8,128)S(1)} %get-tuple-element.75.refs_12_), channel_id=1, source_target_pairs={{0,16},{8,24},{16,0},{24,8},{1,17},{9,25},{17,1},{25,9},{2,18},{10... | collective-permute-start | bytes 61448 | tf_op jit(solution)/shard_map/ppermute | solution.py:764
  107.2 4.0 %collective-permute-start.25 = (f32[8,640]{1,0:T(8,128)S(1)}, f32[8,640]{1,0:T(8,128)S(1)}, u32[]{:S(2)}, u32[]{:S(2)}) collective-permute-start(f32[8,640]{1,0:T(8,128)S(1)} %get-tuple-element.75.refs_12_), channel_id=1, source_target_pairs={{0,8},{8,0},{16,24},{24,16},{1,9},{9,1},{17,25},{25,17},{2,10},{10... | collective-permute-start | bytes 61448 | tf_op jit(solution)/shard_map/ppermute | solution.py:764
  112.6 15.0 %collective-permute-start.32 = (bf16[160,1920]{1,0:T(8,128)(2,1)S(1)}, bf16[160,1920]{1,0:T(8,128)(2,1)S(1)}, u32[]{:S(2)}, u32[]{:S(2)}) collective-permute-start(bf16[160,1920]{1,0:T(8,128)(2,1)S(1)} %get-tuple-element.80.refs_16_), channel_id=1, source_target_pairs={{0,2},{1,3},{2,0},{3,1},{4,6},{5,7},{6,4},{7,5},{8,10},{9,11},{10,... | collective-permute-start | bytes 1843208 | tf_op jit(solution)/shard_map/ppermute | solution.py:764
  113.2 14.5 %collective-permute-start.33 = (bf16[160,1920]{1,0:T(8,128)(2,1)S(1)}, bf16[160,1920]{1,0:T(8,128)(2,1)S(1)}, u32[]{:S(2)}, u32[]{:S(2)}) collective-permute-start(bf16[160,1920]{1,0:T(8,128)(2,1)S(1)} %get-tuple-element.81.refs_17_), channel_id=1, source_target_pairs={{0,4},{1,5},{2,6},{3,7},{4,0},{5,1},{6,2},{7,3},{8,12},{9,13},{10,... | collective-permute-start | bytes 1843208 | tf_op jit(solution)/shard_map/ppermute | solution.py:764
  121.4 10.5 %collective-permute-start.36 = (bf16[656,896]{1,0:T(8,128)(2,1)S(1)}, bf16[656,896]{1,0:T(8,128)(2,1)S(1)}, u32[]{:S(2)}, u32[]{:S(2)}) collective-permute-start(bf16[656,896]{1,0:T(8,128)(2,1)S(1)} %get-tuple-element.90), channel_id=1, source_target_pairs={{0,1},{1,0},{2,3},{3,2},{4,5},{5,4},{6,7},{7,6},{8,9},{9,8},{10,11... | collective-permute-start | bytes 3526664 | tf_op jit(solution)/shard_map/ppermute | solution.py:764
  121.4 7.2 %collective-permute-start.31 = (bf16[656,1024]{1,0:T(8,128)(2,1)S(1)}, bf16[656,1024]{1,0:T(8,128)(2,1)S(1)}, u32[]{:S(2)}, u32[]{:S(2)}) collective-permute-start(bf16[656,1024]{1,0:T(8,128)(2,1)S(1)} %get-tuple-element.85), channel_id=1, source_target_pairs={{0,1},{1,0},{2,3},{3,2},{4,5},{5,4},{6,7},{7,6},{8,9},{9,8},{10,11... | collective-permute-start | bytes 4030472 | tf_op jit(solution)/shard_map/ppermute | solution.py:764
  128.9 11.4 %collective-permute-start.35 = (bf16[176,1024]{1,0:T(8,128)(2,1)S(1)}, bf16[176,1024]{1,0:T(8,128)(2,1)S(1)}, u32[]{:S(2)}, u32[]{:S(2)}) collective-permute-start(bf16[176,1024]{1,0:T(8,128)(2,1)S(1)} %get-tuple-element.88), channel_id=1, source_target_pairs={{0,4},{1,5},{2,6},{3,7},{4,0},{5,1},{6,2},{7,3},{8,12},{9,13},{10,... | collective-permute-start | bytes 1081352 | tf_op jit(solution)/shard_map/ppermute | solution.py:764
  130.5 11.4 %collective-permute-start.34 = (bf16[176,1024]{1,0:T(8,128)(2,1)S(1)}, bf16[176,1024]{1,0:T(8,128)(2,1)S(1)}, u32[]{:S(2)}, u32[]{:S(2)}) collective-permute-start(bf16[176,1024]{1,0:T(8,128)(2,1)S(1)} %get-tuple-element.87.refs_2_), channel_id=1, source_target_pairs={{0,2},{1,3},{2,0},{3,1},{4,6},{5,7},{6,4},{7,5},{8,10},{9,11},{10,... | collective-permute-start | bytes 1081352 | tf_op jit(solution)/shard_map/ppermute | solution.py:764
  132.1 20.4 %collective-permute-start.43 = (bf16[176,896]{1,0:T(8,128)(2,1)S(1)}, bf16[176,896]{1,0:T(8,128)(2,1)S(1)}, u32[]{:S(2)}, u32[]{:S(2)}) collective-permute-start(bf16[176,896]{1,0:T(8,128)(2,1)S(1)} %get-tuple-element.99), channel_id=1, source_target_pairs={{0,4},{1,5},{2,6},{3,7},{4,0},{5,1},{6,2},{7,3},{8,12},{9,13},{10,... | collective-permute-start | bytes 946184 | tf_op jit(solution)/shard_map/ppermute | solution.py:764
  132.7 19.8 %collective-permute-start.42 = (bf16[176,896]{1,0:T(8,128)(2,1)S(1)}, bf16[176,896]{1,0:T(8,128)(2,1)S(1)}, u32[]{:S(2)}, u32[]{:S(2)}) collective-permute-start(bf16[176,896]{1,0:T(8,128)(2,1)S(1)} %get-tuple-element.91.refs_4_), channel_id=1, source_target_pairs={{0,2},{1,3},{2,0},{3,1},{4,6},{5,7},{6,4},{7,5},{8,10},{9,11},{10,... | collective-permute-start | bytes 946184 | tf_op jit(solution)/shard_map/ppermute | solution.py:764
  142.0 8.5 %collective-permute-start.37 = (bf16[96,1024]{1,0:T(8,128)(2,1)S(1)}, bf16[96,1024]{1,0:T(8,128)(2,1)S(1)}, u32[]{:S(2)}, u32[]{:S(2)}) collective-permute-start(bf16[96,1024]{1,0:T(8,128)(2,1)S(1)} %get-tuple-element.92), channel_id=1, source_target_pairs={{0,2},{1,3},{2,0},{3,1},{4,6},{5,7},{6,4},{7,5},{8,10},{9,11},{10,... | collective-permute-start | bytes 589832 | tf_op jit(solution)/shard_map/ppermute | solution.py:764
  143.4 6.0 %collective-permute-start.38 = (bf16[80,1024]{1,0:T(8,128)(2,1)S(1)}, bf16[80,1024]{1,0:T(8,128)(2,1)S(1)}, u32[]{:S(2)}, u32[]{:S(2)}) collective-permute-start(bf16[80,1024]{1,0:T(8,128)(2,1)S(1)} %get-tuple-element.93), channel_id=1, source_target_pairs={{0,4},{1,5},{2,6},{3,7},{4,0},{5,1},{6,2},{7,3},{8,12},{9,13},{10,... | collective-permute-start | bytes 491528 | tf_op jit(solution)/shard_map/ppermute | solution.py:764
  143.9 11.8 %collective-permute-start.40 = (bf16[80,1920]{1,0:T(8,128)(2,1)S(1)}, bf16[80,1920]{1,0:T(8,128)(2,1)S(1)}, u32[]{:S(2)}, u32[]{:S(2)}) collective-permute-start(bf16[80,1920]{1,0:T(8,128)(2,1)S(1)} %get-tuple-element.96), channel_id=1, source_target_pairs={{0,8},{8,0},{16,24},{24,16},{1,9},{9,1},{17,25},{25,17},{2,10},{10... | collective-permute-start | bytes 921608 | tf_op jit(solution)/shard_map/ppermute | solution.py:764
  151.4 5.7 %collective-permute-start.39 = (bf16[96,1024]{1,0:T(8,128)(2,1)S(1)}, bf16[96,1024]{1,0:T(8,128)(2,1)S(1)}, u32[]{:S(2)}, u32[]{:S(2)}) collective-permute-start(bf16[96,1024]{1,0:T(8,128)(2,1)S(1)} %get-tuple-element.95), channel_id=1, source_target_pairs={{0,8},{8,0},{16,24},{24,16},{1,9},{9,1},{17,25},{25,17},{2,10},{10... | collective-permute-start | bytes 589832 | tf_op jit(solution)/shard_map/ppermute | solution.py:764
  152.6 6.8 %collective-permute-start.44 = (bf16[96,896]{1,0:T(8,128)(2,1)S(1)}, bf16[96,896]{1,0:T(8,128)(2,1)S(1)}, u32[]{:S(2)}, u32[]{:S(2)}) collective-permute-start(bf16[96,896]{1,0:T(8,128)(2,1)S(1)} %get-tuple-element.100), channel_id=1, source_target_pairs={{0,2},{1,3},{2,0},{3,1},{4,6},{5,7},{6,4},{7,5},{8,10},{9,11},{10,... | collective-permute-start | bytes 516104 | tf_op jit(solution)/shard_map/ppermute | solution.py:764
  154.2 5.3 %collective-permute-start.45 = (bf16[80,896]{1,0:T(8,128)(2,1)S(1)}, bf16[80,896]{1,0:T(8,128)(2,1)S(1)}, u32[]{:S(2)}, u32[]{:S(2)}) collective-permute-start(bf16[80,896]{1,0:T(8,128)(2,1)S(1)} %get-tuple-element.101), channel_id=1, source_target_pairs={{0,4},{1,5},{2,6},{3,7},{4,0},{5,1},{6,2},{7,3},{8,12},{9,13},{10,... | collective-permute-start | bytes 430088 | tf_op jit(solution)/shard_map/ppermute | solution.py:764
  157.8 9.8 %collective-permute-start.41 = (bf16[96,1024]{1,0:T(8,128)(2,1)S(1)}, bf16[96,1024]{1,0:T(8,128)(2,1)S(1)}, u32[]{:S(2)}, u32[]{:S(2)}) collective-permute-start(bf16[96,1024]{1,0:T(8,128)(2,1)S(1)} %get-tuple-element.98), channel_id=1, source_target_pairs={{0,16},{8,24},{16,0},{24,8},{1,17},{9,25},{17,1},{25,9},{2,18},{10... | collective-permute-start | bytes 589832 | tf_op jit(solution)/shard_map/ppermute | solution.py:764
  160.4 7.2 %collective-permute-start.46 = (bf16[96,896]{1,0:T(8,128)(2,1)S(1)}, bf16[96,896]{1,0:T(8,128)(2,1)S(1)}, u32[]{:S(2)}, u32[]{:S(2)}) collective-permute-start(bf16[96,896]{1,0:T(8,128)(2,1)S(1)} %get-tuple-element.103), channel_id=1, source_target_pairs={{0,8},{8,0},{16,24},{24,16},{1,9},{9,1},{17,25},{25,17},{2,10},{10... | collective-permute-start | bytes 516104 | tf_op jit(solution)/shard_map/ppermute | solution.py:764
  168.2 7.2 %collective-permute-start.47 = (bf16[96,896]{1,0:T(8,128)(2,1)S(1)}, bf16[96,896]{1,0:T(8,128)(2,1)S(1)}, u32[]{:S(2)}, u32[]{:S(2)}) collective-permute-start(bf16[96,896]{1,0:T(8,128)(2,1)S(1)} %get-tuple-element.105), channel_id=1, source_target_pairs={{0,16},{8,24},{16,0},{24,8},{1,17},{9,25},{17,1},{25,9},{2,18},{10... | collective-permute-start | bytes 516104 | tf_op jit(solution)/shard_map/ppermute | solution.py:764
  (3 other events, 19.2 us)
